TPU v7x, 512 devices: a whole 4x4x16 slice. The times are simulated.
512 devices in a mesh: dp: 64 (over z, y_hi, core), ctx: 8 (over x, y_lo).
Axes of the slice: x: 4, y: 4 (y_hi: 2, y_lo: 2; y = y_hi * 2 + y_lo), z: 16, core: 2. Of those that a mesh axis runs over, the one named last changes fastest.
Arguments:
- query_loader: bfloat16 [64, 2048, 1024], P('dp', 'ctx'), may hold values from -10 to 10, as said below
- key_loader: bfloat16 [64, 2048, 1024], P('dp', 'ctx'), may hold values from -10 to 10
- value_loader: bfloat16 [64, 2048, 1024], P('dp', 'ctx'), may hold values from -6 to 6
- conv_loader: bfloat16 [64, 2048, 1536], P('dp', 'ctx'), may hold values from -6 to 6
- slot_tile: int32 [8, 128], P('ctx'), may hold values from 0 to 127, each once within a row
- lengths: int32 [64, 4], P('dp'), may hold values from 1 to 32, 64 in all within a row
- conv_taps: float32 [31, 1536], replicated, may hold values from -1 to 1
- norm_scale: float32 [1536], replicated, may hold values from 0.5 to 2
- norm_shift: float32 [1536], replicated, may hold values from -2 to 2
Outputs:
- attention_out: bfloat16 [64, 2048, 1024], P('dp', 'ctx')
- conv_out: bfloat16 [64, 2048, 1536], P('dp', 'ctx')
Inputs may be any that keep to these rules, and one draw needn't show every extreme that they name: `query_loader`: in some draws, queries and keys share a direction per head.
All inputs are finite; a program needn't handle non-finite values.
Results may differ from a plain program's by a relative error of at most 0.006.
Values may be sent and summed in bfloat16 or wider, within the bound.
A program may use at most 128 MiB of HBM per device.

v0:
```python
import jax
import jax.numpy as jnp
from jax import lax
from jax.sharding import PartitionSpec as P

HEADS = 16
HEAD_DIM = 64
KERNEL = 31
TILE = 128
TILES_DEV = 2
SEG_UNIT = 32


def with_halo(cells, sides, width):
    for axis, dim in sides:
        count = lax.axis_size(axis)
        ends = count - 1
        head = lax.slice_in_dim(cells, 0, width, axis=dim)
        tail = lax.slice_in_dim(cells, cells.shape[dim] - width, cells.shape[dim], axis=dim)
        cells = jnp.concatenate(
            [
                lax.ppermute(tail, axis, [(i, (i + 1) % count) for i in range(ends)]),
                cells,
                lax.ppermute(head, axis, [((i + 1) % count, i) for i in range(ends)]),
            ],
            axis=dim,
        )
    return cells


def segment_of(positions, seg_ends):
    unit_index = positions // SEG_UNIT
    return jnp.sum((seg_ends[None, :] <= unit_index[:, None]).astype(jnp.int32), axis=1)


def split_shares(loader, dp_count):
    return loader[0].reshape(TILES_DEV, dp_count, TILE // dp_count, loader.shape[2])


def arrange_tiles(spread, tile_order, dp_count):
    shares = spread.reshape(dp_count * TILES_DEV, TILE // dp_count, spread.shape[3])
    return shares[tile_order]


def softmax_update(carry, queries, query_seg, keys_piece, values_piece, key_seg):
    running_max, norm_total, accumulated = carry
    scores = (
        jnp.einsum("qhd,khd->hqk", queries, keys_piece, preferred_element_type=jnp.float32) * 0.125
    )
    allowed = (query_seg[:, None] == key_seg[None, :])[None]
    masked = jnp.where(allowed, scores, -1e30)
    new_max = jnp.maximum(running_max, jnp.max(masked, axis=2))
    weights = jnp.where(allowed, jnp.exp(masked - new_max[:, :, None]), 0.0)
    norm_total = jnp.sum(weights, axis=2)
    update = jnp.einsum(
        "hqk,khd->qhd",
        weights.astype(jnp.bfloat16),
        values_piece,
        preferred_element_type=jnp.float32,
    )
    accumulated = update
    return (new_max, norm_total, accumulated)


def on_device(
    query_loader,
    key_loader,
    value_loader,
    conv_loader,
    slot_tile,
    lengths,
    conv_taps,
    norm_scale,
    norm_shift,
):
    dp_count = lax.axis_size("dp")
    row_count = query_loader.shape[1]
    feature_width = HEADS * HEAD_DIM
    spread_query, spread_key, spread_value, spread_conv = (
        lax.all_to_all(
            split_shares(query_loader, dp_count), "dp", split_axis=1, concat_axis=0, tiled=True
        ),
        lax.all_to_all(
            split_shares(key_loader, dp_count), "dp", split_axis=1, concat_axis=0, tiled=True
        ),
        lax.all_to_all(
            split_shares(value_loader, dp_count), "dp", split_axis=1, concat_axis=0, tiled=True
        ),
        lax.all_to_all(
            split_shares(conv_loader, dp_count), "dp", split_axis=1, concat_axis=0, tiled=True
        ),
    )
    tile_order = jnp.transpose(slot_tile[0].reshape(dp_count, TILES_DEV))
    send_query = arrange_tiles(spread_query, tile_order, dp_count)
    send_key = arrange_tiles(spread_key, tile_order, dp_count)
    send_value = arrange_tiles(spread_value, tile_order, dp_count)
    send_conv = arrange_tiles(spread_conv, tile_order, dp_count)
    got_query, got_key, got_value, got_conv = (
        lax.all_to_all(send_query, "dp", split_axis=1, concat_axis=1, tiled=True),
        lax.all_to_all(send_key, "dp", split_axis=1, concat_axis=1, tiled=True),
        lax.all_to_all(send_value, "dp", split_axis=1, concat_axis=1, tiled=True),
        lax.all_to_all(send_conv, "dp", split_axis=1, concat_axis=1, tiled=True),
    )
    queries = got_query.reshape(row_count, HEADS, HEAD_DIM)
    keys_local = got_key.reshape(row_count, HEADS, HEAD_DIM)
    values_local = got_value.reshape(row_count, HEADS, HEAD_DIM)
    seg_ends = jnp.cumsum(lengths[0])
    column = lax.axis_index("ctx")
    local_positions = column * row_count + jnp.arange(row_count, dtype=jnp.int32)
    query_seg = segment_of(local_positions, seg_ends)
    initial = (
        jnp.full((HEADS, row_count), -1e30, jnp.float32),
        jnp.zeros((HEADS, row_count), jnp.float32),
        jnp.zeros((row_count, HEADS, HEAD_DIM), jnp.float32),
    )
    keys_piece = lax.all_gather(keys_local, "ctx", axis=0, tiled=True)
    values_piece = lax.all_gather(values_local, "ctx", axis=0, tiled=True)
    piece_rows = keys_piece.shape[0]
    key_seg = segment_of(jnp.arange(piece_rows, dtype=jnp.int32), seg_ends)
    running_max, norm_total, accumulated = softmax_update(
        initial, queries, query_seg, keys_piece, values_piece, key_seg
    )
    mixture = (accumulated / jnp.transpose(norm_total)[:, :, None]).astype(jnp.bfloat16)
    attention_out = mixture.reshape(1, row_count, feature_width)
    signal = got_conv.reshape(row_count, got_conv.shape[3])
    half_width = (KERNEL - 1) // 2
    padded = with_halo(signal, (("ctx", 0),), half_width).astype(jnp.float32)
    padded_seg = segment_of(
        column * row_count - half_width + jnp.arange(row_count + 2 * half_width, dtype=jnp.int32),
        seg_ends,
    )
    conv_sum = jnp.zeros(signal.shape, jnp.float32)
    for offset_tap in range(KERNEL):
        same_seg = (padded_seg[offset_tap : offset_tap + row_count] == query_seg)[:, None]
        conv_sum = conv_sum + jnp.where(
            same_seg, conv_taps[offset_tap] * padded[offset_tap : offset_tap + row_count], 0.0
        )
    conv_out = jax.nn.silu(norm_scale * conv_sum + norm_shift).astype(jnp.bfloat16)
    return (attention_out, conv_out.reshape(1, row_count, signal.shape[1]))


def solution(mesh):
    return jax.shard_map(
        on_device,
        mesh=mesh,
        in_specs=(
            P("dp", "ctx", None),
            P("dp", "ctx", None),
            P("dp", "ctx", None),
            P("dp", "ctx", None),
            P("ctx", None),
            P("dp", None),
            P(),
            P(),
            P(),
        ),
        out_specs=(P("dp", "ctx", None), P("dp", "ctx", None)),
        check_vma=False,
    )
```

profile of v0, /device:TPU:26, one launch (start us, length us, event | category | flops | bytes accessed | tf_op | source)
XLA Modules:
  0.0 480.9 jit_solution(3792680349821187126)
XLA Ops:
  9.6 18.6 %all-to-all-start.4 = ((bf16[2,64,2,1024]{3,2,0,1:T(2,128)(2,1)}), bf16[2,64,2,1024]{3,2,0,1:T(2,128)(2,1)S(1)}, u32[]{:S(2)}, u32[]{:S(2)}) async-start(bf16[2,64,2,1024]{3,2,0,1:T(2,128)(2,1)} %copy.63), calls=%async_computation.4 | async-start | bytes 1048576 | tf_op jit(solution)/shard_map/all_to_all | solution.py:83
  29.6 32.2 %all-to-all-done.4 = bf16[2,64,2,1024]{3,2,0,1:T(2,128)(2,1)S(1)} async-done(((bf16[2,64,2,1024]{3,2,0,1:T(2,128)(2,1)}), bf16[2,64,2,1024]{3,2,0,1:T(2,128)(2,1)S(1)}, u32[]{:S(2)}, u32[]{:S(2)}) %all-to-all-start.4) | async-done | bytes 524320 | tf_op jit(solution)/shard_map/all_to_all | solution.py:83
  61.8 5.4 %all-to-all-start.2 = ((bf16[2,64,2,1024]{3,2,0,1:T(2,128)(2,1)}), bf16[2,64,2,1024]{3,2,0,1:T(2,128)(2,1)S(1)}, u32[]{:S(2)}, u32[]{:S(2)}) async-start(bf16[2,64,2,1024]{3,2,0,1:T(2,128)(2,1)} %copy.60), calls=%async_computation.2 | async-start | bytes 1048576 | tf_op jit(solution)/shard_map/all_to_all | solution.py:80
  68.6 32.2 %all-to-all-done.2 = bf16[2,64,2,1024]{3,2,0,1:T(2,128)(2,1)S(1)} async-done(((bf16[2,64,2,1024]{3,2,0,1:T(2,128)(2,1)}), bf16[2,64,2,1024]{3,2,0,1:T(2,128)(2,1)S(1)}, u32[]{:S(2)}, u32[]{:S(2)}) %all-to-all-start.2) | async-done | bytes 524320 | tf_op jit(solution)/shard_map/all_to_all | solution.py:80
  100.8 5.4 %all-to-all-start = ((bf16[2,64,2,1024]{3,2,0,1:T(2,128)(2,1)}), bf16[2,64,2,1024]{3,2,0,1:T(2,128)(2,1)S(1)}, u32[]{:S(2)}, u32[]{:S(2)}) async-start(bf16[2,64,2,1024]{3,2,0,1:T(2,128)(2,1)} %copy.55), calls=%async_computation | async-start | bytes 1048576 | tf_op jit(solution)/shard_map/all_to_all | solution.py:86
  110.5 29.3 %all-to-all-done = bf16[2,64,2,1024]{3,2,0,1:T(2,128)(2,1)S(1)} async-done(((bf16[2,64,2,1024]{3,2,0,1:T(2,128)(2,1)}), bf16[2,64,2,1024]{3,2,0,1:T(2,128)(2,1)S(1)}, u32[]{:S(2)}, u32[]{:S(2)}) %all-to-all-start) | async-done | bytes 524320 | tf_op jit(solution)/shard_map/all_to_all | solution.py:86
  139.8 5.4 %all-to-all-start.5 = ((bf16[2,64,2,1024]{3,2,0,1:T(2,128)(2,1)}), bf16[2,64,2,1024]{3,2,0,1:T(2,128)(2,1)S(1)}, u32[]{:S(2)}, u32[]{:S(2)}) async-start(bf16[2,64,2,1024]{3,2,0,1:T(2,128)(2,1)} %copy.64), calls=%async_computation.5 | async-start | bytes 1048576 | tf_op jit(solution)/shard_map/all_to_all | solution.py:100
  146.9 31.9 %all-to-all-done.5 = bf16[2,64,2,1024]{3,2,0,1:T(2,128)(2,1)S(1)} async-done(((bf16[2,64,2,1024]{3,2,0,1:T(2,128)(2,1)}), bf16[2,64,2,1024]{3,2,0,1:T(2,128)(2,1)S(1)}, u32[]{:S(2)}, u32[]{:S(2)}) %all-to-all-start.5) | async-done | bytes 524320 | tf_op jit(solution)/shard_map/all_to_all | solution.py:100
  178.7 5.4 %all-to-all-start.6 = ((bf16[2,64,2,1536]{3,2,0,1:T(2,128)(2,1)}), bf16[2,64,2,1536]{3,2,0,1:T(2,128)(2,1)S(1)}, u32[]{:S(2)}, u32[]{:S(2)}) async-start(bf16[2,64,2,1536]{3,2,0,1:T(2,128)(2,1)} %copy.68), calls=%async_computation.6 | async-start | bytes 1572864 | tf_op jit(solution)/shard_map/all_to_all | solution.py:89
  190.0 38.9 %all-to-all-done.6 = bf16[2,64,2,1536]{3,2,0,1:T(2,128)(2,1)S(1)} async-done(((bf16[2,64,2,1536]{3,2,0,1:T(2,128)(2,1)}), bf16[2,64,2,1536]{3,2,0,1:T(2,128)(2,1)S(1)}, u32[]{:S(2)}, u32[]{:S(2)}) %all-to-all-start.6) | async-done | bytes 786464 | tf_op jit(solution)/shard_map/all_to_all | solution.py:89
  228.9 5.4 %all-to-all-start.3 = ((bf16[2,64,2,1024]{3,2,0,1:T(2,128)(2,1)}), bf16[2,64,2,1024]{3,2,0,1:T(2,128)(2,1)S(1)}, u32[]{:S(2)}, u32[]{:S(2)}) async-start(bf16[2,64,2,1024]{3,2,0,1:T(2,128)(2,1)} %copy.61), calls=%async_computation.3 | async-start | bytes 1048576 | tf_op jit(solution)/shard_map/all_to_all | solution.py:99
  237.9 29.9 %all-to-all-done.3 = bf16[2,64,2,1024]{3,2,0,1:T(2,128)(2,1)S(1)} async-done(((bf16[2,64,2,1024]{3,2,0,1:T(2,128)(2,1)}), bf16[2,64,2,1024]{3,2,0,1:T(2,128)(2,1)S(1)}, u32[]{:S(2)}, u32[]{:S(2)}) %all-to-all-start.3) | async-done | bytes 524320 | tf_op jit(solution)/shard_map/all_to_all | solution.py:99
  267.9 5.4 %all-to-all-start.7 = ((bf16[2,64,2,1536]{3,2,0,1:T(2,128)(2,1)}), bf16[2,64,2,1536]{3,2,0,1:T(2,128)(2,1)S(1)}, u32[]{:S(2)}, u32[]{:S(2)}) async-start(bf16[2,64,2,1536]{3,2,0,1:T(2,128)(2,1)} %copy.69), calls=%async_computation.7 | async-start | bytes 1572864 | tf_op jit(solution)/shard_map/all_to_all | solution.py:102
  276.3 41.8 %all-to-all-done.7 = bf16[2,64,2,1536]{3,2,0,1:T(2,128)(2,1)S(1)} async-done(((bf16[2,64,2,1536]{3,2,0,1:T(2,128)(2,1)}), bf16[2,64,2,1536]{3,2,0,1:T(2,128)(2,1)S(1)}, u32[]{:S(2)}, u32[]{:S(2)}) %all-to-all-start.7) | async-done | bytes 786464 | tf_op jit(solution)/shard_map/all_to_all | solution.py:102
  318.1 5.6 %all-to-all-start.1 = ((bf16[2,64,2,1024]{3,2,0,1:T(2,128)(2,1)}), bf16[2,64,2,1024]{3,2,0,1:T(2,128)(2,1)}, u32[]{:S(2)}, u32[]{:S(2)}) async-start(bf16[2,64,2,1024]{3,2,0,1:T(2,128)(2,1)} %copy.57), calls=%async_computation.1 | async-start | bytes 1048576 | tf_op jit(solution)/shard_map/all_to_all | solution.py:101
  327.6 3.7 collective-permute-start
  331.3 2.3 collective-permute-start.1
  335.4 21.8 %all-to-all-done.1 = bf16[2,64,2,1024]{3,2,0,1:T(2,128)(2,1)} async-done(((bf16[2,64,2,1024]{3,2,0,1:T(2,128)(2,1)}), bf16[2,64,2,1024]{3,2,0,1:T(2,128)(2,1)}, u32[]{:S(2)}, u32[]{:S(2)}) %all-to-all-start.1) | async-done | bytes 524320 | tf_op jit(solution)/shard_map/all_to_all | solution.py:101
  359.4 2.3 reshape.178
  365.2 10.8 %fusion.76 = bf16[1,256,1536]{2,1,0:T(8,128)(2,1)} fusion(f32[1536]{0:T(1024)S(1)} %copy-done.37, f32[286,1536]{1,0:T(8,128)S(1)} %maximum_convert_fusion, f32[1536]{0:T(1024)S(1)} %copy-done.35, pred[256]{0:T(512)(128)(4,1)S(1)} %copy-done.40, f32[1536]{0:T(1024)S(1)} %copy-done.36, pred[256]{0:T(512)(128)(4,1)S(1)} %copy-done.41, f32[1536]{0:T(1024)S(1)} %copy-done.7, ...), kind=kLoop, calls=%fused_computation.112 | loop fusion | flops 38928384 | bytes 49755904 | tf_op jit(solution)/shard_map/reshape | solution.py:139
  376.0 16.4 %fusion = (f32[16,256]{1,0:T(8,128)S(1)}, f32[16,256,2048]{2,1,0:T(8,128)}) fusion(pred[256,2048]{1,0:T(8,128)(4,1)S(1)} %broadcast_compare_fusion, bf16[2048,16,64]{0,2,1:T(8,128)(2,1)} %all-gather.5.cloned.1.call-done, bf16[256,16,64]{2,1,0:T(8,128)(2,1)S(1)} %reshape.182), kind=kOutput, calls=%fused_computation.6 | convolution fusion | flops 1098903552 | bytes 38813696 | tf_op jit(solution)/shard_map/qhd,khd->hqk/dot_general | solution.py:48
  392.4 15.6 %fusion.1 = f32[16,256]{1,0:T(8,128)S(1)} fusion(f32[16,256,2048]{2,1,0:T(8,128)} %get-tuple-element.77, f32[16,256]{1,0:T(8,128)S(1)} %broadcast_maximum_fusion, pred[256,2048]{1,0:T(8,128)(4,1)S(1)} %broadcast_compare_fusion), kind=kLoop, calls=%fused_computation.7 | loop fusion | flops 41938944 | bytes 34111488 | tf_op jit(solution)/shard_map/reduce_sum | solution.py:54
  408.1 48.5 %all-gather.3.cloned.1.call-done = bf16[2048,16,64]{0,2,1:T(8,128)(2,1)} async-done(((bf16[256,16,64]{0,2,1:T(8,128)(2,1)}), bf16[2048,16,64]{0,2,1:T(8,128)(2,1)}) %all-gather.3.cloned.1.call-update) | async-done | bytes 4194320 | tf_op jit(solution)/shard_map/all_gather | solution.py:117
  456.5 16.3 %divide_convert_fusion = bf16[256,16,64]{0,2,1:T(8,128)(2,1)S(1)} fusion(bf16[2048,16,64]{0,2,1:T(8,128)(2,1)} %all-gather.3.cloned.1.call-done, f32[16,256,2048]{2,1,0:T(8,128)} %get-tuple-element.77, f32[16,256]{1,0:T(8,128)S(1)} %broadcast_maximum_fusion, pred[256,2048]{1,0:T(8,128)(4,1)S(1)} %broadcast_compare_fusion, f32[256,16]{0,1:T(8,128)S(1)} %bitcast.47), kind=kOutput, calls=%fused_computation.109 | convolution fusion | flops 1116209152 | bytes 38830080 | tf_op jit(solution)/shard_map/hqk,khd->qhd/dot_general | solution.py:55
  (151 shorter events, 35.4 us)
Async XLA Ops:
  7.2 21.1 %copy-start.3 = (bf16[1,256,1024]{2,1,0:T(8,128)(2,1)S(1)}, bf16[1,256,1024]{2,1,0:T(8,128)(2,1)}, u32[]{:S(2)}) copy-start(bf16[1,256,1024]{2,1,0:T(8,128)(2,1)} %param.9) | copy-start | bytes 1572868
  9.6 52.2 %all-to-all-start.4 = ((bf16[2,64,2,1024]{3,2,0,1:T(2,128)(2,1)}), bf16[2,64,2,1024]{3,2,0,1:T(2,128)(2,1)S(1)}, u32[]{:S(2)}, u32[]{:S(2)}) async-start(bf16[2,64,2,1024]{3,2,0,1:T(2,128)(2,1)} %copy.63), calls=%async_computation.4 | async-start | bytes 1048576 | tf_op jit(solution)/shard_map/all_to_all | solution.py:83
  28.3 39.0 %copy-start.4 = (bf16[1,256,1024]{2,1,0:T(8,128)(2,1)S(1)}, bf16[1,256,1024]{2,1,0:T(8,128)(2,1)}, u32[]{:S(2)}) copy-start(bf16[1,256,1024]{2,1,0:T(8,128)(2,1)} %param.11) | copy-start | bytes 1572868
  61.8 39.0 %all-to-all-start.2 = ((bf16[2,64,2,1024]{3,2,0,1:T(2,128)(2,1)}), bf16[2,64,2,1024]{3,2,0,1:T(2,128)(2,1)S(1)}, u32[]{:S(2)}, u32[]{:S(2)}) async-start(bf16[2,64,2,1024]{3,2,0,1:T(2,128)(2,1)} %copy.60), calls=%async_computation.2 | async-start | bytes 1048576 | tf_op jit(solution)/shard_map/all_to_all | solution.py:80
  67.2 39.5 %copy-start.46 = (s32[1,128]{1,0:T(1,128)S(1)}, s32[1,128]{1,0:T(1,128)}, u32[]{:S(2)}) copy-start(s32[1,128]{1,0:T(1,128)} %param.13) | copy-start | bytes 1540
  100.8 39.0 %all-to-all-start = ((bf16[2,64,2,1024]{3,2,0,1:T(2,128)(2,1)}), bf16[2,64,2,1024]{3,2,0,1:T(2,128)(2,1)S(1)}, u32[]{:S(2)}, u32[]{:S(2)}) async-start(bf16[2,64,2,1024]{3,2,0,1:T(2,128)(2,1)} %copy.55), calls=%async_computation | async-start | bytes 1048576 | tf_op jit(solution)/shard_map/all_to_all | solution.py:86
  107.7 37.5 %copy-start.2 = (bf16[1,256,1536]{2,1,0:T(8,128)(2,1)S(1)}, bf16[1,256,1536]{2,1,0:T(8,128)(2,1)}, u32[]{:S(2)}) copy-start(bf16[1,256,1536]{2,1,0:T(8,128)(2,1)} %param.12) | copy-start | bytes 2359300
  139.8 39.0 %all-to-all-start.5 = ((bf16[2,64,2,1024]{3,2,0,1:T(2,128)(2,1)}), bf16[2,64,2,1024]{3,2,0,1:T(2,128)(2,1)S(1)}, u32[]{:S(2)}, u32[]{:S(2)}) async-start(bf16[2,64,2,1024]{3,2,0,1:T(2,128)(2,1)} %copy.64), calls=%async_computation.5 | async-start | bytes 1048576 | tf_op jit(solution)/shard_map/all_to_all | solution.py:100
  178.7 50.2 %all-to-all-start.6 = ((bf16[2,64,2,1536]{3,2,0,1:T(2,128)(2,1)}), bf16[2,64,2,1536]{3,2,0,1:T(2,128)(2,1)S(1)}, u32[]{:S(2)}, u32[]{:S(2)}) async-start(bf16[2,64,2,1536]{3,2,0,1:T(2,128)(2,1)} %copy.68), calls=%async_computation.6 | async-start | bytes 1572864 | tf_op jit(solution)/shard_map/all_to_all | solution.py:89
  184.1 191.9 %all-gather.5.cloned.1.call-start = ((), (), s32[]{:S(2)}) async-start(), calls=%async_computation.9 | async-start | bytes 4718592 | tf_op jit(solution)/shard_map/all_gather | solution.py:116
  228.9 39.0 %all-to-all-start.3 = ((bf16[2,64,2,1024]{3,2,0,1:T(2,128)(2,1)}), bf16[2,64,2,1024]{3,2,0,1:T(2,128)(2,1)S(1)}, u32[]{:S(2)}, u32[]{:S(2)}) async-start(bf16[2,64,2,1024]{3,2,0,1:T(2,128)(2,1)} %copy.61), calls=%async_computation.3 | async-start | bytes 1048576 | tf_op jit(solution)/shard_map/all_to_all | solution.py:99
  236.5 36.8 %copy-start.47 = (s32[1,4]{1,0:T(1,128)S(1)}, s32[1,4]{1,0:T(1,128)}, u32[]{:S(2)}) copy-start(s32[1,4]{1,0:T(1,128)} %param.14) | copy-start | bytes 52
  267.9 8.4 %copy-start = (bf16[2,64,2,1024]{3,2,0,1:T(2,128)(2,1)}, bf16[2,64,2,1024]{3,2,0,1:T(2,128)(2,1)S(1)}, u32[]{:S(2)}) copy-start(bf16[2,64,2,1024]{3,2,0,1:T(2,128)(2,1)S(1)} %all-to-all-done.3) | copy-start | bytes 1572868
  267.9 50.2 %all-to-all-start.7 = ((bf16[2,64,2,1536]{3,2,0,1:T(2,128)(2,1)}), bf16[2,64,2,1536]{3,2,0,1:T(2,128)(2,1)S(1)}, u32[]{:S(2)}, u32[]{:S(2)}) async-start(bf16[2,64,2,1536]{3,2,0,1:T(2,128)(2,1)} %copy.69), calls=%async_computation.7 | async-start | bytes 1572864 | tf_op jit(solution)/shard_map/all_to_all | solution.py:102
  273.5 50.5 %copy-start.5 = (f32[31,1536]{1,0:T(8,128)S(1)}, f32[31,1536]{1,0:T(8,128)}, u32[]{:S(2)}) copy-start(f32[31,1536]{1,0:T(8,128)} %param.15) | copy-start | bytes 571396
  318.1 39.1 %all-to-all-start.1 = ((bf16[2,64,2,1024]{3,2,0,1:T(2,128)(2,1)}), bf16[2,64,2,1024]{3,2,0,1:T(2,128)(2,1)}, u32[]{:S(2)}, u32[]{:S(2)}) async-start(bf16[2,64,2,1024]{3,2,0,1:T(2,128)(2,1)} %copy.57), calls=%async_computation.1 | async-start | bytes 1048576 | tf_op jit(solution)/shard_map/all_to_all | solution.py:101
  323.7 132.9 %all-gather.3.cloned.1.call-start = ((), (), s32[]{:S(2)}) async-start(), calls=%async_computation.8 | async-start | bytes 4718592 | tf_op jit(solution)/shard_map/all_gather | solution.py:117
  327.3 7.2 %copy-start.1 = (bf16[2,64,2,1024]{3,2,0,1:T(2,128)(2,1)S(1)}, bf16[2,64,2,1024]{3,2,0,1:T(2,128)(2,1)}, u32[]{:S(2)}) copy-start(bf16[2,64,2,1024]{3,2,0,1:T(2,128)(2,1)} %copy-done) | copy-start | bytes 1572868
  327.6 36.1 %collective-permute-start = (bf16[15,1536]{1,0:T(8,128)(2,1)S(1)}, bf16[15,1536]{1,0:T(8,128)(2,1)S(1)}, u32[]{:S(2)}, u32[]{:S(2)}) collective-permute-start(bf16[15,1536]{1,0:T(8,128)(2,1)S(1)} %get-tuple-element.43), channel_id=1, source_target_pairs={{0,1},{1,2},{2,3},{3,4},{4,5},{5,6},{6,7},{8,9},{9,10},{10,11},{11... | collective-permute-start | bytes 138248 | tf_op jit(solution)/shard_map/ppermute | solution.py:22
  331.3 32.4 %collective-permute-start.1 = (bf16[15,1536]{1,0:T(8,128)(2,1)S(1)}, bf16[15,1536]{1,0:T(8,128)(2,1)}, u32[]{:S(2)}, u32[]{:S(2)}) collective-permute-start(bf16[15,1536]{1,0:T(8,128)(2,1)S(1)} %get-tuple-element.44), channel_id=1, source_target_pairs={{1,0},{2,1},{3,2},{4,3},{5,4},{6,5},{7,6},{9,8},{10,9},{11,10},{12... | collective-permute-start | bytes 138248 | tf_op jit(solution)/shard_map/ppermute | solution.py:24
  363.3 1.5 copy-start.10
  363.3 1.5 copy-start.11
  363.3 1.5 copy-start.12
  363.3 1.5 copy-start.13
  (36 other events, 53.7 us)
Sparse Core Ops, SparseCore 0:
  187.4 134.5 all-gather.4
  363.8 92.6 all-gather.2
where the time goes:
time: 489 us; the launch traced here: 481 us
  waiting for transfers between devices  307 us (63%)
  starting transfers between devices  62.9 us (13%)
  local copies, waits for them, and re-layouts  33.1 us (7%)
  matrix products  32.7 us (7%)
  other arithmetic  30.4 us (6%)
  between operations  15.3 us (3%)
    all_gather x1, waiting for transfers between devices, on_device(): values_piece = lax.all_gather(values_local, 'ctx', axis=0, tiled=True)  48.5 us
    all_to_all x1, waiting for transfers between devices, on_device(): lax.all_to_all(send_conv, 'dp', split_axis=1, concat_axis=1, tiled=True)  41.8 us
    all_to_all x1, waiting for transfers between devices, on_device(): lax.all_to_all(split_shares(conv_loader, dp_count), 'dp', split_axis=1, c...  38.9 us
    all_to_all x1, waiting for transfers between devices, on_device(): lax.all_to_all(split_shares(query_loader, dp_count), 'dp', split_axis=1,...  32.2 us
    all_to_all x1, waiting for transfers between devices, on_device(): lax.all_to_all(split_shares(key_loader, dp_count), 'dp', split_axis=1, co...  32.2 us
    all_to_all x1, waiting for transfers between devices, on_device(): lax.all_to_all(send_key, 'dp', split_axis=1, concat_axis=1, tiled=True)  31.9 us
    all_to_all x1, waiting for transfers between devices, on_device(): lax.all_to_all(send_query, 'dp', split_axis=1, concat_axis=1, tiled=True)  29.9 us
    all_to_all x1, waiting for transfers between devices, on_device(): lax.all_to_all(split_shares(value_loader, dp_count), 'dp', split_axis=1,...  29.3 us
  transfers between devices with their start and end apart: 12, of which 9 were waited for; matrix products, arithmetic and copies ran while one was open for 16% of the time, Pallas kernels for 0%

commit v1 on v0

v1 whole, which is shorter than its diff:
```python
import functools

import jax
import jax.numpy as jnp
from jax import lax
from jax.experimental import pallas as pl
from jax.experimental.pallas import tpu as pltpu
from jax.sharding import PartitionSpec as P

MESH = pl.DeviceIdType.MESH
HEADS = 16
HEAD_DIM = 64
KERNEL = 31
TILE = 128
TILES_DEV = 2
SEG_UNIT = 32
ROWS = 16
LANES = 128
N_DP = 64
N_CTX = 8
QKV = 3 * ROWS
CONV_ROWS = 24
QBLOCK = 256
KBLOCK = 256
FRAMES = 2048
UNITS = QBLOCK // SEG_UNIT


def share_of(dp, ctx):
    return (dp // 8) * 8 + lax.rem(dp + ctx, 8)


def entry(count, device):
    barrier = pltpu.get_barrier_semaphore()

    def one(k, carry):
        pl.semaphore_signal(barrier, inc=1, device_id=device(k), device_id_type=MESH)
        return carry

    lax.fori_loop(0, count, one, 0)
    pl.semaphore_wait(barrier, count)


def all_arrived(ref, sem):
    pltpu.make_async_copy(ref, ref, sem).wait()


def spread_kernel(x_ref, out_ref, send_sem, recv_sem):
    dp, ctx = lax.axis_index("dp"), lax.axis_index("ctx")
    entry(N_DP - 1, lambda k: (lax.rem(dp + 1 + k, N_DP), ctx))

    def copy(k):
        peer = lax.rem(dp + k, N_DP)
        return pltpu.make_async_remote_copy(
            src_ref=x_ref.at[share_of(peer, ctx)],
            dst_ref=out_ref.at[dp],
            send_sem=send_sem,
            recv_sem=recv_sem,
            device_id=(peer, ctx),
            device_id_type=MESH,
        )

    own = pltpu.make_async_copy(x_ref.at[share_of(dp, ctx)], out_ref.at[dp], recv_sem)

    def start(k, carry):
        copy(k).start()
        return carry

    def sent(k, carry):
        copy(k).wait_send()
        return carry

    lax.fori_loop(1, N_DP, start, 0)
    own.start()
    lax.fori_loop(1, N_DP, sent, 0)
    all_arrived(out_ref, recv_sem)


def spread(x):
    return pl.pallas_call(
        spread_kernel,
        out_shape=jax.ShapeDtypeStruct(x.shape, x.dtype),
        in_specs=[pl.BlockSpec(memory_space=pl.ANY)],
        out_specs=pl.BlockSpec(memory_space=pl.ANY),
        scratch_shapes=[pltpu.SemaphoreType.DMA, pltpu.SemaphoreType.DMA],
        compiler_params=pltpu.CompilerParams(collective_id=0, has_side_effects=True),
        name="spread",
    )(x)


def heads_kernel(x_ref, out_ref, send_sem, recv_sem):
    dp, ctx = lax.axis_index("dp"), lax.axis_index("ctx")
    share = share_of(dp, ctx)
    group, column = share // 8, lax.rem(share, 8)

    def sender(k):
        other = k // 8
        return (lax.rem(k, 8) * 8 + lax.rem(ctx - other + 8, 8), other)

    barrier = pltpu.get_barrier_semaphore()

    def greet(k, carry):
        peer = sender(k)

        @pl.when(jnp.logical_or(peer[0] != dp, peer[1] != ctx))
        def _():
            pl.semaphore_signal(barrier, inc=1, device_id=peer, device_id_type=MESH)

        return carry

    lax.fori_loop(0, N_DP, greet, 0)
    is_own = column == ctx

    @pl.when(is_own)
    def _():
        pl.semaphore_wait(barrier, N_DP - 1)

    @pl.when(jnp.logical_not(is_own))
    def _():
        pl.semaphore_wait(barrier, N_DP)

    def copy(k):
        peer = lax.rem(dp + k, N_DP)
        return pltpu.make_async_remote_copy(
            src_ref=x_ref.at[peer],
            dst_ref=out_ref.at[pl.ds(ctx * TILES_DEV, TILES_DEV), group],
            send_sem=send_sem,
            recv_sem=recv_sem,
            device_id=(peer, column),
            device_id_type=MESH,
        )

    def start(k, carry):
        copy(k).start()
        return carry

    def sent(k, carry):
        copy(k).wait_send()
        return carry

    lax.fori_loop(1, N_DP, start, 0)

    @pl.when(is_own)
    def _():
        pltpu.make_async_copy(
            x_ref.at[dp], out_ref.at[pl.ds(ctx * TILES_DEV, TILES_DEV), group], recv_sem
        ).start()

    @pl.when(jnp.logical_not(is_own))
    def _():
        copy(0).start()
        copy(0).wait_send()

    lax.fori_loop(1, N_DP, sent, 0)
    all_arrived(out_ref, recv_sem)


def to_heads(x):
    return pl.pallas_call(
        heads_kernel,
        out_shape=jax.ShapeDtypeStruct((N_CTX * TILES_DEV, TILE // ROWS, 3, ROWS, LANES), x.dtype),
        in_specs=[pl.BlockSpec(memory_space=pl.ANY)],
        out_specs=pl.BlockSpec(memory_space=pl.ANY),
        scratch_shapes=[pltpu.SemaphoreType.DMA, pltpu.SemaphoreType.DMA],
        compiler_params=pltpu.CompilerParams(collective_id=1, has_side_effects=True),
        name="to_heads",
    )(x)


def deliver_kernel(x_ref, mix_ref, out_ref, heads_ref, send_sem, recv_sem, mix_send, mix_recv):
    dp, ctx = lax.axis_index("dp"), lax.axis_index("ctx")
    share = share_of(dp, ctx)
    barrier = pltpu.get_barrier_semaphore()

    def greet_dp(k, carry):
        pl.semaphore_signal(
            barrier, inc=1, device_id=(lax.rem(dp + k, N_DP), ctx), device_id_type=MESH
        )
        return carry

    def greet_ctx(k, carry):
        pl.semaphore_signal(
            barrier, inc=1, device_id=(dp, lax.rem(ctx + k, N_CTX)), device_id_type=MESH
        )
        return carry

    lax.fori_loop(1, N_DP, greet_dp, 0)
    lax.fori_loop(1, N_CTX, greet_ctx, 0)
    pl.semaphore_wait(barrier, N_DP - 1 + N_CTX - 1)

    def mix_copy(k):
        peer = lax.rem(ctx + k, N_CTX)
        return pltpu.make_async_remote_copy(
            src_ref=mix_ref.at[peer],
            dst_ref=heads_ref.at[:, pl.ds(pl.multiple_of(ctx * LANES, LANES), LANES)],
            send_sem=mix_send,
            recv_sem=mix_recv,
            device_id=(dp, peer),
            device_id_type=MESH,
        )

    def copy(k):
        peer = lax.rem(dp + k, N_DP)
        return pltpu.make_async_remote_copy(
            src_ref=x_ref.at[peer],
            dst_ref=out_ref.at[share],
            send_sem=send_sem,
            recv_sem=recv_sem,
            device_id=(peer, ctx),
            device_id_type=MESH,
        )

    def start(k, carry):
        copy(k).start()
        return carry

    def sent(k, carry):
        copy(k).wait_send()
        return carry

    def mix_start(k, carry):
        mix_copy(k).start()
        return carry

    def mix_sent(k, carry):
        mix_copy(k).wait_send()
        return carry

    lax.fori_loop(1, N_DP, start, 0)
    lax.fori_loop(1, N_CTX, mix_start, 0)
    pltpu.make_async_copy(x_ref.at[dp], out_ref.at[share], recv_sem).start()
    pltpu.make_async_copy(
        mix_ref.at[ctx],
        heads_ref.at[:, pl.ds(pl.multiple_of(ctx * LANES, LANES), LANES)],
        mix_recv,
    ).start()
    lax.fori_loop(1, N_DP, sent, 0)
    lax.fori_loop(1, N_CTX, mix_sent, 0)
    all_arrived(out_ref, recv_sem)
    all_arrived(heads_ref, mix_recv)


def deliver(x, mix):
    rows = FRAMES // N_CTX
    return pl.pallas_call(
        deliver_kernel,
        out_shape=(
            jax.ShapeDtypeStruct(x.shape, x.dtype),
            jax.ShapeDtypeStruct((rows, N_CTX * LANES), x.dtype),
        ),
        in_specs=[pl.BlockSpec(memory_space=pl.ANY)] * 2,
        out_specs=[pl.BlockSpec(memory_space=pl.ANY)] * 2,
        scratch_shapes=[pltpu.SemaphoreType.DMA] * 4,
        compiler_params=pltpu.CompilerParams(collective_id=2, has_side_effects=True),
        name="deliver",
    )(x, mix)


def attend_kernel(len_ref, x_ref, out_ref):
    block = pl.program_id(0)
    ends = [len_ref[0, 0]]
    for i in range(1, 4):
        ends.append(ends[-1] + len_ref[0, i])
    first = block * UNITS
    last = first + UNITS - 1
    low = jnp.int32(0)
    high = jnp.int32(FRAMES // SEG_UNIT)
    for end in ends:
        low = jnp.where(end <= first, jnp.maximum(low, end), low)
        high = jnp.where(end > last, jnp.minimum(high, end), high)
    per_key = KBLOCK // SEG_UNIT
    low_block = low // per_key
    high_block = (high + per_key - 1) // per_key

    def segment(unit):
        seg = jnp.zeros(unit.shape, jnp.int32)
        for end in ends[:3]:
            seg = seg + (unit >= end).astype(jnp.int32)
        return seg

    per_tile = QBLOCK // TILE
    queries = x_ref[pl.ds(block * per_tile, per_tile), :, 0].reshape(QBLOCK, LANES) * 0.125
    lane = lax.broadcasted_iota(jnp.int32, (QBLOCK, LANES), 1)
    zero = jnp.zeros_like(queries)
    both = jnp.concatenate(
        [jnp.where(lane < HEAD_DIM, queries, zero), jnp.where(lane < HEAD_DIM, zero, queries)], axis=0
    )
    row = lax.broadcasted_iota(jnp.int32, (2 * QBLOCK, 1), 0)
    row_seg = segment(first + lax.rem(row, QBLOCK) // SEG_UNIT)
    key_tiles = KBLOCK // TILE

    def step(index, carry):
        top, total, mixed = carry
        keys = x_ref[pl.ds(index * key_tiles, key_tiles), :, 1].reshape(KBLOCK, LANES)
        values = x_ref[pl.ds(index * key_tiles, key_tiles), :, 2].reshape(KBLOCK, LANES)
        scores = lax.dot_general(
            both, keys, (((1,), (1,)), ((), ())), preferred_element_type=jnp.float32
        )
        col = lax.broadcasted_iota(jnp.int32, (1, KBLOCK), 1)
        col_seg = segment(index * per_key + col // SEG_UNIT)
        scores = jnp.where(row_seg == col_seg, scores, -2e30)
        new_top = jnp.maximum(top, jnp.max(scores, axis=1, keepdims=True))
        weights = jnp.exp(scores - new_top)
        scale = jnp.exp(top - new_top)
        total = total * scale + jnp.sum(weights, axis=1, keepdims=True)
        mixed = mixed * scale + jnp.dot(
            weights.astype(jnp.bfloat16), values, preferred_element_type=jnp.float32
        )
        return new_top, total, mixed

    top, total, mixed = lax.fori_loop(
        low_block,
        high_block,
        step,
        (
            jnp.full((2 * QBLOCK, 1), -1e30, jnp.float32),
            jnp.zeros((2 * QBLOCK, 1), jnp.float32),
            jnp.zeros((2 * QBLOCK, LANES), jnp.float32),
        ),
    )
    mixed = mixed / total
    out_ref[0] = jnp.where(lane < HEAD_DIM, mixed[:QBLOCK], mixed[QBLOCK:]).astype(jnp.bfloat16)


def attend(lengths, x):
    blocks = FRAMES // QBLOCK
    return pl.pallas_call(
        attend_kernel,
        grid_spec=pltpu.PrefetchScalarGridSpec(
            num_scalar_prefetch=1,
            grid=(blocks,),
            in_specs=[pl.BlockSpec(x.shape, lambda i, lens: (0, 0, 0, 0, 0))],
            out_specs=pl.BlockSpec((1, QBLOCK, LANES), lambda i, lens: (i, 0, 0)),
        ),
        out_shape=jax.ShapeDtypeStruct((blocks, QBLOCK, LANES), jnp.bfloat16),
        compiler_params=pltpu.CompilerParams(vmem_limit_bytes=48 * 2**20),
        cost_estimate=pl.CostEstimate(
            flops=8 * FRAMES * FRAMES * LANES, bytes_accessed=2**21, transcendentals=2 * FRAMES * FRAMES
        ),
        name="attend",
    )(lengths, x)


def with_halo(cells, width):
    ends = N_CTX - 1
    head = cells[:width]
    tail = cells[cells.shape[0] - width :]
    return jnp.concatenate(
        [
            lax.ppermute(tail, "ctx", [(i, (i + 1) % N_CTX) for i in range(ends)]),
            cells,
            lax.ppermute(head, "ctx", [((i + 1) % N_CTX, i) for i in range(ends)]),
        ],
        axis=0,
    )


def segment_of(positions, seg_ends):
    unit_index = positions // SEG_UNIT
    return jnp.sum((seg_ends[None, :] <= unit_index[:, None]).astype(jnp.int32), axis=1)


def convolve(signal, lengths, conv_taps, norm_scale, norm_shift):
    row_count = signal.shape[0]
    seg_ends = jnp.cumsum(lengths[0])
    column = lax.axis_index("ctx")
    half_width = (KERNEL - 1) // 2
    query_seg = segment_of(
        column * row_count + jnp.arange(row_count, dtype=jnp.int32), seg_ends
    )
    padded = with_halo(signal, half_width).astype(jnp.float32)
    padded_seg = segment_of(
        column * row_count - half_width + jnp.arange(row_count + 2 * half_width, dtype=jnp.int32),
        seg_ends,
    )
    conv_sum = jnp.zeros(signal.shape, jnp.float32)
    for tap in range(KERNEL):
        same_seg = (padded_seg[tap : tap + row_count] == query_seg)[:, None]
        conv_sum = conv_sum + jnp.where(
            same_seg, conv_taps[tap] * padded[tap : tap + row_count], 0.0
        )
    return jax.nn.silu(norm_scale * conv_sum + norm_shift).astype(jnp.bfloat16)


def on_device(
    query_loader,
    key_loader,
    value_loader,
    conv_loader,
    slot_tile,
    lengths,
    conv_taps,
    norm_scale,
    norm_shift,
):
    qkv = jnp.stack([query_loader[0], key_loader[0], value_loader[0]])
    qkv = qkv.reshape(3, TILES_DEV, TILE // ROWS, ROWS, N_CTX, LANES)
    qkv = jnp.transpose(qkv, (2, 4, 1, 0, 3, 5)).reshape(N_DP, TILES_DEV * QKV, LANES)
    conv = conv_loader[0].reshape(TILES_DEV, N_DP, CONV_ROWS, LANES)
    conv = jnp.transpose(conv, (1, 0, 2, 3)).reshape(N_DP, TILES_DEV * CONV_ROWS, LANES)
    got = spread(jnp.concatenate([qkv, conv], axis=1))
    order = slot_tile[0]
    got_qkv = got[:, : TILES_DEV * QKV].reshape(N_DP * TILES_DEV, 3, ROWS, LANES)
    send_qkv = got_qkv[order].reshape(N_DP, TILES_DEV, 3, ROWS, LANES)
    got_conv = got[:, TILES_DEV * QKV :].reshape(N_DP * TILES_DEV, CONV_ROWS, LANES)
    send_conv = got_conv[order].reshape(N_DP, TILES_DEV * CONV_ROWS, LANES)
    heads = to_heads(send_qkv)
    mix = attend(lengths, heads)
    signal, attention_out = deliver(send_conv, mix)
    signal = signal.reshape(N_DP, TILES_DEV, TILE // N_DP, CONV_ROWS // 2 * LANES)
    signal = jnp.transpose(signal, (1, 0, 2, 3)).reshape(TILES_DEV * TILE, CONV_ROWS // 2 * LANES)
    conv_out = convolve(signal, lengths, conv_taps, norm_scale, norm_shift)
    return (attention_out[None], conv_out[None])


def solution(mesh):
    return jax.shard_map(
        on_device,
        mesh=mesh,
        in_specs=(
            P("dp", "ctx", None),
            P("dp", "ctx", None),
            P("dp", "ctx", None),
            P("dp", "ctx", None),
            P("ctx", None),
            P("dp", None),
            P(),
            P(),
            P(),
        ),
        out_specs=(P("dp", "ctx", None), P("dp", "ctx", None)),
        check_vma=False,
    )
```

time: 489 us -> 312 us (0.64)
  the two profiles are of different devices: /device:TPU:26 before, /device:TPU:1 now
where the time goes in v1:
time: 312 us; the launch traced here: 308 us
  Pallas kernels  275 us (88%)
  local copies, waits for them, and re-layouts  14 us (4%)
  other arithmetic  12.7 us (4%)
  starting transfers between devices  5.28 us (2%)
    pallas_call x1, Pallas kernels, spread(): pl.pallas_call(spread_kernel, out_shape=jax.ShapeDtypeStruct(x.shape, x.d...  121 us
    pallas_call x1, Pallas kernels, to_heads(): pl.pallas_call(heads_kernel, out_shape=jax.ShapeDtypeStruct((N_CTX * TILE...  84.9 us
    pallas_call x1, Pallas kernels, deliver(): pl.pallas_call(deliver_kernel, out_shape=(jax.ShapeDtypeStruct(x.shape, x...  51.2 us
    pallas_call x1, Pallas kernels, attend(): pl.pallas_call(attend_kernel, grid_spec=pltpu.PrefetchScalarGridSpec(num_...  17.6 us
    broadcast_in_dim x1, other arithmetic, on_device(): return (attention_out[None], conv_out[None])  10.2 us
  transfers between devices with their start and end apart: 2, of which 1 were waited for; matrix products, arithmetic and copies ran while one was open for 0% of the time, Pallas kernels for 0%

profile of v1, /device:TPU:1, one launch (start us, length us, event | category | flops | bytes accessed | tf_op | source)
XLA Modules:
  0.0 308.1 jit_solution(9120400394453837946)
XLA Ops:
  0.7 2.1 reshape_squeeze.3
  3.1 0.4 copy.17
  3.6 0.3 copy.14
  3.9 1.6 pad_maximum_fusion.x_ref
  5.5 121.2 %spread.1 = bf16[64,144,128]{2,1,0:T(8,128)(2,1)} custom-call(bf16[64,144,128]{2,1,0:T(8,128)(2,1)} %pad_maximum_fusion.x_ref), custom_call_target="tpu_custom_call" | custom-call | tf_op jit(solution)/shard_map/spread/pallas_call | solution.py:80
  126.7 0.6 copy-done.10
  127.4 0.5 slice-done
  127.8 1.6 gather_fusion
  129.4 1.9 gather_fusion.1
  131.3 84.9 %to_heads.1.x_ref = bf16[16,8,3,16,128]{4,3,2,1,0:T(8,128)(2,1)} custom-call(bf16[64,2,3,16,128]{4,3,2,1,0:T(8,128)(2,1)} %bitcast.30), custom_call_target="tpu_custom_call" | custom-call | tf_op jit(solution)/shard_map/to_heads/pallas_call | solution.py:159
  216.3 1.4 copy-done
  217.7 17.6 %attend.1.mix_ref = bf16[8,256,128]{2,1,0:T(8,128)(2,1)S(1)} custom-call(s32[1,4]{1,0:T(1,128)S(1)} %copy-done.2, bf16[16,8,3,16,128]{4,3,2,1,0:T(8,128)(2,1)S(1)} %copy-done), custom_call_target="tpu_custom_call" | custom-call | flops 4294967296 | bytes 2097152 | tf_op jit(solution)/shard_map/attend/pallas_call | solution.py:327
  235.3 0.8 copy-done.1
  236.1 51.2 %deliver.1 = (bf16[64,48,128]{2,1,0:T(8,128)(2,1)}, bf16[256,1024]{1,0:T(8,128)(2,1)}) custom-call(bf16[64,48,128]{2,1,0:T(8,128)(2,1)} %bitcast.32, bf16[8,256,128]{2,1,0:T(8,128)(2,1)} %copy-done.1), custom_call_target="tpu_custom_call" | custom-call | tf_op jit(solution)/shard_map/deliver/pallas_call | solution.py:245
  287.3 2.0 reshape.163
  289.4 0.5 copy.16
  289.9 0.3 reshape.164
  290.3 1.3 collective-permute-start.1
  291.6 4.0 %collective-permute-start = (bf16[15,1536]{1,0:T(8,128)(2,1)S(1)}, bf16[15,1536]{1,0:T(8,128)(2,1)S(1)}, u32[]{:S(2)}, u32[]{:S(2)}) collective-permute-start(bf16[15,1536]{1,0:T(8,128)(2,1)S(1)} %get-tuple-element.37), channel_id=1, source_target_pairs={{0,1},{1,2},{2,3},{3,4},{4,5},{5,6},{6,7},{8,9},{9,10},{10,11},{11... | collective-permute-start | bytes 138248 | tf_op jit(solution)/shard_map/ppermute | solution.py:350
  296.2 0.3 slice_reduce_fusion.30
  296.5 0.2 slice_reduce_fusion.29
  296.9 0.2 maximum_convert_fusion
  297.1 10.2 %fusion.63 = bf16[1,256,1536]{2,1,0:T(8,128)(2,1)} fusion(f32[1536]{0:T(1024)S(1)} %copy-done.8, f32[286,1536]{1,0:T(8,128)S(1)} %maximum_convert_fusion, f32[1536]{0:T(1024)S(1)} %get-tuple-element.35, pred[256]{0:T(512)(128)(4,1)S(1)} %get-tuple-element.40, f32[1536]{0:T(1024)S(1)} %get-tuple-element.36, pred[256]{0:T(512)(128)(4,1)S(1)} %get-tuple-element.41, ...), kind=kLoop, calls=%fused_computation.100 | loop fusion | flops 38928384 | bytes 49755904 | tf_op jit(solution)/shard_map/broadcast_in_dim | solution.py:413
  307.3 0.8 copy.19
  (36 shorter events, 1.0 us)
Async XLA Ops:
  0.6 2.3 copy-start.4
  0.6 2.3 copy-start.5
  0.7 2.3 copy-start.6
  126.7 0.7 copy-start.10
  126.7 1.1 slice-start
  127.3 2.1 slice-start.1
  131.3 85.0 %copy-start.2 = (s32[1,4]{1,0:T(1,128)S(1)}, s32[1,4]{1,0:T(1,128)}, u32[]{:S(2)}) copy-start(s32[1,4]{1,0:T(1,128)} %len_ref.1) | copy-start | bytes 52
  216.3 1.4 copy-start
  235.3 0.8 copy-start.1
  289.4 6.8 %copy-start.7 = (f32[31,1536]{1,0:T(8,128)S(1)}, f32[31,1536]{1,0:T(8,128)}, u32[]{:S(2)}) copy-start(f32[31,1536]{1,0:T(8,128)} %param.15) | copy-start | bytes 571396
  290.3 6.4 %collective-permute-start.1 = (bf16[15,1536]{1,0:T(8,128)(2,1)S(1)}, bf16[15,1536]{1,0:T(8,128)(2,1)S(1)}, u32[]{:S(2)}, u32[]{:S(2)}) collective-permute-start(bf16[15,1536]{1,0:T(8,128)(2,1)S(1)} %get-tuple-element.38), channel_id=1, source_target_pairs={{1,0},{2,1},{3,2},{4,3},{5,4},{6,5},{7,6},{9,8},{10,9},{11,10},{12... | collective-permute-start | bytes 138248 | tf_op jit(solution)/shard_map/ppermute | solution.py:352
  291.6 5.3 %collective-permute-start = (bf16[15,1536]{1,0:T(8,128)(2,1)S(1)}, bf16[15,1536]{1,0:T(8,128)(2,1)S(1)}, u32[]{:S(2)}, u32[]{:S(2)}) collective-permute-start(bf16[15,1536]{1,0:T(8,128)(2,1)S(1)} %get-tuple-element.37), channel_id=1, source_target_pairs={{0,1},{1,2},{2,3},{3,4},{4,5},{5,6},{6,7},{8,9},{9,10},{10,11},{11... | collective-permute-start | bytes 138248 | tf_op jit(solution)/shard_map/ppermute | solution.py:350
  296.2 0.9 copy-start.8
  296.2 0.9 copy-start.9
  297.1 10.2 %copy-start.3 = (bf16[256,1024]{1,0:T(8,128)(2,1)S(1)}, bf16[256,1024]{1,0:T(8,128)(2,1)}, u32[]{:S(2)}) copy-start(bf16[256,1024]{1,0:T(8,128)(2,1)} %get-tuple-element.4) | copy-start | bytes 1572868

commit v2 on v0

--- a/solution.py
+++ b/solution.py
@@ -1,14 +1,789 @@
 import jax
 import jax.numpy as jnp
 from jax import lax
+from jax.experimental import pallas as pl
+from jax.experimental.pallas import tpu as pltpu
 from jax.sharding import PartitionSpec as P
 
+MESH = pl.DeviceIdType.MESH
 HEADS = 16
 HEAD_DIM = 64
+CHANNELS = 1536
 KERNEL = 31
 TILE = 128
 TILES_DEV = 2
 SEG_UNIT = 32
+FRAMES = 2048
+COLUMN = 256
+LANES = 128
+N_DP = 64
+N_CTX = 8
+QBLOCK = 256
+KBLOCK = 256
+UNITS = QBLOCK // SEG_UNIT
+
+N_Z = 16
+PLANE_DP = 4
+PLANE = PLANE_DP * N_CTX
+HELD = PLANE * TILES_DEV
+SHIFTS = N_Z - 1
+NEAR, NEAR_SLOTS, FAR_SLOTS = 6, 5, 4
+RELAYS, RELAY_SLOTS = 10, 2
+MAIN = NEAR * NEAR_SLOTS + (SHIFTS - NEAR) * FAR_SLOTS
+EXTRA = RELAYS * RELAY_SLOTS
+TABLE = 256
+AT_MAIN, AT_EXTRA, AT_FINAL, AT_BAD = 0, 72, 96, 160
+RANKS = 16
+PAIRS = N_Z * N_Z
+LIST = 2304
+FIELDS = 0x55555555
+
+
+def shift_of(j):
+    half = j // 2
+    return jnp.where(j % 2 == 0, half + 1, N_Z - 1 - half)
+
+
+def order_of(shift):
+    return jnp.where(shift <= N_Z // 2, 2 * (shift - 1), 2 * (N_Z - shift) - 1)
+
+
+def main_slots(shift):
+    return jnp.where(order_of(shift) < NEAR, NEAR_SLOTS, FAR_SLOTS)
+
+
+def main_offset(shift):
+    j = order_of(shift)
+    return jnp.where(j < NEAR, NEAR_SLOTS * j, NEAR * NEAR_SLOTS + FAR_SLOTS * (j - NEAR))
+
+
+def relay_offset(shift):
+    return RELAY_SLOTS * order_of(shift)
+
+
+def place():
+    dp, ctx = lax.axis_index("dp"), lax.axis_index("ctx")
+    return dp // PLANE_DP, dp % PLANE_DP, ctx
+
+
+def plane_peer(z, row, ctx, k):
+    index = (row * N_CTX + ctx + k) % PLANE
+    return index // N_CTX, index % N_CTX, (z * PLANE_DP + index // N_CTX, index % N_CTX)
+
+
+def z_peer(z, row, ctx, j):
+    return ((z + shift_of(j)) % N_Z * PLANE_DP + row, ctx)
+
+
+def repeat(first, last, body):
+    def one(k, carry):
+        body(k)
+        return carry
+
+    lax.fori_loop(first, last, one, 0)
+
+
+def remote(src, dst, send, recv, device):
+    return pltpu.make_async_remote_copy(
+        src_ref=src, dst_ref=dst, send_sem=send, recv_sem=recv, device_id=device, device_id_type=MESH
+    )
+
+
+def await_all(ref, sem):
+    pltpu.make_async_copy(ref, ref, sem).wait()
+
+
+def signal(device):
+    pl.semaphore_signal(pltpu.get_barrier_semaphore(), inc=1, device_id=device, device_id_type=MESH)
+
+
+class Spread:
+    def __init__(self, piece, held, send, recv):
+        z, row, ctx = place()
+        mine = pl.ds((ctx * PLANE_DP + row) * TILES_DEV, TILES_DEV)
+
+        def copy(k):
+            to_row, to_ctx, device = plane_peer(z, row, ctx, k)
+            return remote(piece(to_row, to_ctx), held.at[mine], send, recv, device)
+
+        self.copy, self.held, self.recv = copy, held, recv
+        self.own = pltpu.make_async_copy(piece(row, ctx), held.at[mine], recv)
+
+    def start(self):
+        repeat(1, PLANE, lambda k: self.copy(k).start())
+        self.own.start()
+
+    def arrived(self):
+        await_all(self.held, self.recv)
+
+    def sent(self):
+        repeat(1, PLANE, lambda k: self.copy(k).wait_send())
+
+
+class Along:
+    def __init__(self, groups, staged, got, send, recv):
+        z, row, ctx = place()
+        self.staged, self.got, self.send, self.recv = staged, got, send, recv
+
+        def copy(j, offset, slots):
+            part = pl.ds(offset, slots)
+            return remote(staged.at[part], got.at[part], send, recv, z_peer(z, row, ctx, j))
+
+        self.copy, self.groups = copy, groups
+
+    def start(self):
+        for first, last, base, slots in self.groups:
+            repeat(
+                first,
+                last,
+                lambda j: self.copy(j, base + (j - first) * slots, slots).start(),
+            )
+
+    def arrived(self):
+        await_all(self.got, self.recv)
+
+    def sent(self):
+        await_all(self.staged, self.send)
+
+
+MAIN_GROUPS = ((0, NEAR, 0, NEAR_SLOTS), (NEAR, SHIFTS, NEAR * NEAR_SLOTS, FAR_SLOTS))
+EXTRA_GROUPS = ((0, RELAYS, 0, RELAY_SLOTS),)
+
+
+def stage_main(table, held, staged):
+    def one(i):
+        staged[i] = held[table[AT_MAIN + i]]
+
+    repeat(0, MAIN, one)
+
+
+def stage_extra(table, held, got, staged):
+    def one(i):
+        code = table[AT_EXTRA + i]
+        staged[i] = jnp.where(
+            code < HELD, held[jnp.minimum(code, HELD - 1)], got[jnp.clip(code - HELD, 0, MAIN - 1)]
+        )
+
+    repeat(0, EXTRA, one)
+
+
+def stage_final(table, held, got, more, staged):
+    def one(i):
+        code = table[AT_FINAL + i]
+        first = held[jnp.minimum(code, HELD - 1)]
+        second = got[jnp.clip(code - HELD, 0, MAIN - 1)]
+        third = more[jnp.clip(code - HELD - MAIN, 0, EXTRA - 1)]
+        staged[i] = jnp.where(code < HELD, first, jnp.where(code < HELD + MAIN, second, third))
+
+    repeat(0, HELD, one)
+
+
+def head_piece(ref):
+    return lambda row, ctx: ref.at[:, row, :, pl.ds(pl.multiple_of(ctx * LANES, LANES), LANES)]
+
+
+WIDE = CHANNELS // PLANE_DP
+
+
+def conv_piece(ref):
+    return lambda row, ctx: ref.at[:, ctx, :, pl.ds(pl.multiple_of(row * WIDE, LANES), WIDE)]
+
+
+def first_kernel(q_ref, list_ref, held_ref, lists_ref, send, recv, list_send, list_recv):
+    z, row, ctx = place()
+    repeat(1, PLANE, lambda k: signal(plane_peer(z, row, ctx, k)[2]))
+    pl.semaphore_wait(pltpu.get_barrier_semaphore(), PLANE - 1)
+
+    def tell(k):
+        device = (z * PLANE_DP + row, (ctx + k) % N_CTX)
+        return remote(list_ref, lists_ref.at[ctx], list_send, list_recv, device)
+
+    repeat(1, N_CTX, lambda k: tell(k).start())
+    pltpu.make_async_copy(list_ref, lists_ref.at[ctx], list_recv).start()
+    spread = Spread(head_piece(q_ref), held_ref, send, recv)
+    spread.start()
+    repeat(1, N_CTX, lambda k: tell(k).wait_send())
+    await_all(lists_ref, list_recv)
+    spread.arrived()
+    spread.sent()
+
+
+def first(q, own_list):
+    return pl.pallas_call(
+        first_kernel,
+        out_shape=(
+            jax.ShapeDtypeStruct((HELD, SEG_UNIT, LANES), q.dtype),
+            jax.ShapeDtypeStruct((N_CTX,) + own_list.shape, own_list.dtype),
+        ),
+        in_specs=[pl.BlockSpec(memory_space=pl.ANY)] * 2,
+        out_specs=[pl.BlockSpec(memory_space=pl.ANY)] * 2,
+        scratch_shapes=[pltpu.SemaphoreType.DMA] * 4,
+        compiler_params=pltpu.CompilerParams(collective_id=0, has_side_effects=True),
+        name="spread_queries",
+    )(q, own_list)
+
+
+def filled(fields):
+    return (fields | (fields >> 1)) & FIELDS
+
+
+def field_index(bit):
+    def step(mask, worth):
+        return jnp.where((bit & mask) != 0, worth, 0)
+
+    high = jnp.where(bit >= (1 << 16), 8, 0)
+    return high + step(0x7F00FF00, 4) + step(0x70F0F0F0, 2) + step(0x4CCCCCCC & FIELDS, 1)
+
+
+def route_kernel(
+    lists_ref,
+    table,
+    count_v,
+    tile_v,
+    slot_v,
+    count,
+    tile,
+    slot,
+    direct,
+    relay_free,
+    next_rank,
+    next_main,
+    next_extra,
+    from_z,
+    to_z,
+    through,
+    sems,
+):
+    me = lax.axis_index("dp") // PLANE_DP
+    tiles = lists_ref[...]
+    source = tiles >> 3
+    rows = lax.broadcasted_iota(jnp.int32, (HELD, LANES), 0)
+    lanes = lax.broadcasted_iota(jnp.int32, (HELD, LANES), 1)
+    local = (rows & ~7) + (tiles & 7)
+    position = ((rows & 7) >> 1) * 16 + (rows >> 3) * 2 + (rows & 1)
+
+    def add_rank(i, rank):
+        other = lists_ref[pl.ds(i, 1), :] >> 3
+        return rank + jnp.where((other == source) & (rows > i), 1, 0)
+
+    rank = lax.fori_loop(0, HELD, add_rank, jnp.zeros((HELD, LANES), jnp.int32))
+    here = lanes == me
+    column_source = jnp.sum(jnp.where(here, source, 0), axis=1, keepdims=True)
+    column_rank = jnp.sum(jnp.where(here, rank, 0), axis=1, keepdims=True)
+    mine = source == me
+    for i in range(N_Z):
+        count_v[pl.ds(i, 1), :] = jnp.sum(
+            jnp.where(source == i, 1, 0), axis=0, keepdims=True, dtype=jnp.int32
+        )
+    for i in range(RANKS):
+        tile_v[pl.ds(i, 1), :] = jnp.sum(
+            jnp.where(mine & (rank == i), local, 0), axis=0, keepdims=True, dtype=jnp.int32
+        )
+        slot_v[pl.ds(i, 1), :] = jnp.sum(
+            jnp.where((column_source == lanes) & (column_rank == i), position, 0),
+            axis=0,
+            keepdims=True,
+            dtype=jnp.int32,
+        )
+    copies = [
+        pltpu.make_async_copy(a, b, sems.at[i])
+        for i, (a, b) in enumerate(((count_v, count), (tile_v, tile), (slot_v, slot)))
+    ]
+    for copy in copies:
+        copy.start()
+
+    def clear(i):
+        table[i] = 0
+
+    repeat(0, TABLE, clear)
+
+    def relay_fields(y):
+        def add(m, fields):
+            shift = (y - m) & 15
+            open_ = (shift != 0) & (order_of(shift) < RELAYS)
+            return fields | jnp.where(open_, jnp.int32(RELAY_SLOTS) << (2 * m), 0)
+
+        relay_free[y] = lax.fori_loop(0, N_Z, add, jnp.int32(0))
+
+    repeat(0, N_Z, relay_fields)
+    for copy in copies:
+        copy.wait()
+
+    def place_row(z, carry):
+        own = jnp.int32(1) << (2 * z)
+
+        def open_pair(y, carry):
+            free, bad = carry
+            held = count[z, y]
+            bad = bad | jnp.where(held > RANKS, 1, 0)
+            shift = (y - z) & 15
+            most = jnp.where(shift == 0, RANKS, main_slots(shift))
+            straight = jnp.minimum(held, most)
+            direct[z * N_Z + y] = straight
+            left = jnp.where(shift == 0, 3, jnp.minimum(most - straight, 3))
+            return free | (left << (2 * y)), bad
+
+        free, bad = lax.fori_loop(0, N_Z, open_pair, (jnp.int32(0), carry[1]))
+
+        def add(n, y, bit):
+            from_z[n] = z
+            to_z[n] = y
+            through[n] = bit
+
+        def take(free, bit):
+            return free - jnp.where(bit == own, 0, bit)
+
+        def place_pair(i, carry):
+            y = (i + z) & 15
+            shift = (y - z) & 15
+            most = jnp.where(shift == 0, RANKS, main_slots(shift))
+            excess = jnp.minimum(count[z, y], RANKS) - most
+
+            def place_one(_, carry):
+                free, n, bad = carry
+                open_ = filled(free) & filled(relay_free[y])
+
+                def simple():
+                    late = open_ & (jnp.int32(-1) << (2 * ((y + 8) & 15)))
+                    chosen = jnp.where(late != 0, late, open_)
+                    bit = chosen & -chosen
+                    relay_free[y] = relay_free[y] - bit
+                    add(n, y, bit)
+                    return take(free, bit), n + 1, bad
+
+                def swap():
+                    def look(m, carry):
+                        free, n, done = carry
+                        bit = jnp.int32(1) << (2 * m)
+                        other = filled(free) & filled(relay_free[m])
+                        fits = (
+                            (done == 0)
+                            & (m != z)
+                            & (m != y)
+                            & ((filled(relay_free[y]) & bit) != 0)
+                            & (direct[z * N_Z + m] > 0)
+                            & (other != 0)
+                        )
+
+                        def do():
+                            instead = other & -other
+                            direct[z * N_Z + m] = direct[z * N_Z + m] - 1
+                            relay_free[m] = relay_free[m] - instead
+                            relay_free[y] = relay_free[y] - bit
+                            add(n, m, instead)
+                            add(n + 1, y, bit)
+                            return take(free, instead), n + 2, jnp.int32(1)
+
+                        return lax.cond(fits, do, lambda: (free, n, done))
+
+                    free_, n_, done = lax.fori_loop(0, N_Z, look, (free, n, jnp.int32(0)))
+                    return free_, n_, bad | (1 - done)
+
+                return lax.cond(open_ != 0, simple, swap)
+
+            return lax.fori_loop(0, excess, place_one, carry)
+
+        free, n, bad = lax.fori_loop(0, N_Z, place_pair, (free, carry[0], bad))
+        return n, bad
+
+    n, bad = lax.fori_loop(0, N_Z, place_row, (jnp.int32(0), jnp.int32(0)))
+    table[AT_BAD] = bad
+
+    def begin(i):
+        next_rank[i] = direct[i]
+        next_main[i] = direct[i]
+        next_extra[i] = 0
+
+    repeat(0, PAIRS, begin)
+
+    def straight(other):
+        shift_out = (other - me) & 15
+        shift_in = (me - other) & 15
+
+        def out(r):
+            @pl.when(shift_out != 0)
+            def _():
+                table[AT_MAIN + main_offset(shift_out) + r] = tile[r, other]
+
+        def arrive(r):
+            table[AT_FINAL + slot[r, other]] = jnp.where(
+                shift_in == 0, tile[r, other], HELD + main_offset(shift_in) + r
+            )
+
+        repeat(0, direct[me * N_Z + other], out)
+        repeat(0, direct[other * N_Z + me], arrive)
+
+    repeat(0, N_Z, straight)
+
+    def finish(i):
+        z, y, bit = from_z[i], to_z[i], through[i]
+        m = field_index(bit)
+        rank = next_rank[z * N_Z + y]
+        next_rank[z * N_Z + y] = rank + 1
+        stays = m == z
+        main = next_main[z * N_Z + m]
+        next_main[z * N_Z + m] = main + 1
+        extra = next_extra[m * N_Z + y]
+        next_extra[m * N_Z + y] = extra + 1
+        main_at = main_offset((m - z) & 15) + main
+        extra_at = relay_offset((y - m) & 15) + extra
+
+        @pl.when((z == me) & jnp.logical_not(stays))
+        def _():
+            table[AT_MAIN + main_at] = tile[rank, y]
+
+        @pl.when(m == me)
+        def _():
+            table[AT_EXTRA + extra_at] = jnp.where(stays, tile[rank, y], HELD + main_at)
+
+        @pl.when(y == me)
+        def _():
+            table[AT_FINAL + slot[rank, z]] = HELD + MAIN + extra_at
+
+    repeat(0, n, finish)
+
+
+def route(lists):
+    smem = pltpu.SMEM
+    pair = smem((PAIRS,), jnp.int32)
+    square = smem((N_Z, LANES), jnp.int32)
+    square_v = pltpu.VMEM((N_Z, LANES), jnp.int32)
+    return pl.pallas_call(
+        route_kernel,
+        out_shape=jax.ShapeDtypeStruct((TABLE,), jnp.int32),
+        in_specs=[pl.BlockSpec(memory_space=pltpu.VMEM)],
+        out_specs=pl.BlockSpec(memory_space=smem),
+        scratch_shapes=[square_v] * 3
+        + [square] * 3
+        + [pair, smem((N_Z,), jnp.int32), pair, pair, pair]
+        + [smem((LIST,), jnp.int32)] * 3
+        + [pltpu.SemaphoreType.DMA((3,))],
+        name="route",
+    )(lists)
+
+
+def heads_kernel(
+    table, held_q, k_ref, v_ref, conv_ref, q_out, k_out, v_out, held_conv, *scratch
+):
+    z, row, ctx = place()
+    repeat(1, PLANE, lambda k: signal(plane_peer(z, row, ctx, k)[2]))
+    repeat(0, SHIFTS, lambda j: signal(z_peer(z, row, ctx, j)))
+    pl.semaphore_wait(pltpu.get_barrier_semaphore(), PLANE - 1 + SHIFTS)
+    held_k, held_v, *scratch = scratch
+    main_staged, main_got, extra_staged, extra_got, staged = (scratch[3 * i : 3 * i + 3] for i in range(5))
+    sems = scratch[15]
+    held = (held_q, held_k, held_v)
+    outs = (q_out, k_out, v_out)
+    spread = [
+        None,
+        Spread(head_piece(k_ref), held_k, sems.at[0], sems.at[1]),
+        Spread(head_piece(v_ref), held_v, sems.at[2], sems.at[3]),
+    ]
+    spread_conv = Spread(conv_piece(conv_ref), held_conv, sems.at[4], sems.at[5])
+    main = [
+        Along(MAIN_GROUPS, main_staged[i], main_got[i], sems.at[6 + 2 * i], sems.at[7 + 2 * i])
+        for i in range(3)
+    ]
+    extra = [
+        Along(EXTRA_GROUPS, extra_staged[i], extra_got[i], sems.at[12 + 2 * i], sems.at[13 + 2 * i])
+        for i in range(3)
+    ]
+
+    def final_copy(i, k):
+        to = (row + k) % PLANE_DP
+        return remote(
+            staged[i].at[pl.ds(to * 16, 16)],
+            outs[i].at[:, row],
+            sems.at[18 + 2 * i],
+            sems.at[19 + 2 * i],
+            (z * PLANE_DP + to, ctx),
+        )
+
+    def start_main(i):
+        if i:
+            spread[i].arrived()
+        stage_main(table, held[i], main_staged[i])
+        main[i].start()
+
+    def start_extra(i):
+        main[i].arrived()
+        stage_extra(table, held[i], main_got[i], extra_staged[i])
+        extra[i].start()
+
+    def start_final(i):
+        extra[i].arrived()
+        stage_final(table, held[i], main_got[i], extra_got[i], staged[i])
+        repeat(1, PLANE_DP, lambda k: final_copy(i, k).start())
+        pltpu.make_async_copy(
+            staged[i].at[pl.ds(row * 16, 16)], outs[i].at[:, row], sems.at[19 + 2 * i]
+        ).start()
+
+    spread[1].start()
+    start_main(0)
+    spread[2].start()
+    start_main(1)
+    spread_conv.start()
+    start_extra(0)
+    start_main(2)
+    start_extra(1)
+    start_final(0)
+    start_extra(2)
+    start_final(1)
+    start_final(2)
+    spread_conv.arrived()
+    spread_conv.sent()
+    for i in range(3):
+        if i:
+            spread[i].sent()
+        main[i].sent()
+        extra[i].sent()
+        repeat(1, PLANE_DP, lambda k: final_copy(i, k).wait_send())
+        await_all(outs[i], sems.at[19 + 2 * i])
+
+
+def to_heads(table, held_q, k, v, conv):
+    unit = (SEG_UNIT, LANES)
+    kind = held_q.dtype
+
+    def buffers(count):
+        return [pltpu.VMEM((count,) + unit, kind)] * 3
+
+    heads = jax.ShapeDtypeStruct((N_CTX * TILES_DEV, PLANE_DP) + unit, kind)
+    return pl.pallas_call(
+        heads_kernel,
+        out_shape=(heads, heads, heads, jax.ShapeDtypeStruct((HELD, 16, WIDE), kind)),
+        in_specs=[pl.BlockSpec(memory_space=pltpu.SMEM), pl.BlockSpec(memory_space=pltpu.VMEM)]
+        + [pl.BlockSpec(memory_space=pl.ANY)] * 3,
+        out_specs=[pl.BlockSpec(memory_space=pl.ANY)] * 4,
+        scratch_shapes=buffers(HELD)[:2]
+        + buffers(MAIN)
+        + buffers(MAIN)
+        + buffers(EXTRA)
+        + buffers(EXTRA)
+        + buffers(HELD)
+        + [pltpu.SemaphoreType.DMA((24,))],
+        compiler_params=pltpu.CompilerParams(
+            collective_id=1, has_side_effects=True, vmem_limit_bytes=32 * 2**20
+        ),
+        name="to_heads",
+    )(table, held_q, k, v, conv)
+
+
+def conv_kernel(
+    table,
+    held,
+    mix_ref,
+    rows_out,
+    halo_out,
+    heads_out,
+    main_staged,
+    main_got,
+    extra_staged,
+    extra_got,
+    staged,
+    sems,
+    halo_sems,
+):
+    z, row, ctx = place()
+    repeat(1, PLANE, lambda k: signal(plane_peer(z, row, ctx, k)[2]))
+    repeat(0, SHIFTS, lambda j: signal(z_peer(z, row, ctx, j)))
+    pl.semaphore_wait(pltpu.get_barrier_semaphore(), PLANE - 1 + SHIFTS)
+    main = Along(MAIN_GROUPS, main_staged, main_got, sems.at[0], sems.at[1])
+    extra = Along(EXTRA_GROUPS, extra_staged, extra_got, sems.at[2], sems.at[3])
+    stage_main(table, held, main_staged)
+    main.start()
+
+    mixed = heads_out.at[:, pl.ds(pl.multiple_of(ctx * LANES, LANES), LANES)]
+
+    def mix_copy(k):
+        to = (ctx + k) % N_CTX
+        return remote(mix_ref.at[to], mixed, sems.at[4], sems.at[5], (z * PLANE_DP + row, to))
+
+    repeat(1, N_CTX, lambda k: mix_copy(k).start())
+    pltpu.make_async_copy(mix_ref.at[ctx], mixed, sems.at[5]).start()
+
+    main.arrived()
+    stage_extra(table, held, main_got, extra_staged)
+    extra.start()
+    extra.arrived()
+    stage_final(table, held, main_got, extra_got, staged)
+    channels = pl.ds(pl.multiple_of(row * WIDE, LANES), WIDE)
+
+    def part(to_row, to_ctx):
+        return staged.at[pl.ds(to_row * 16 + to_ctx * TILES_DEV, TILES_DEV)]
+
+    def copy(k):
+        to_row, to_ctx, device = plane_peer(z, row, ctx, k)
+        return remote(
+            part(to_row, to_ctx), rows_out.at[:, ctx, :, channels], sems.at[6], sems.at[7], device
+        )
+
+    repeat(1, PLANE, lambda k: copy(k).start())
+    pltpu.make_async_copy(part(row, ctx), rows_out.at[:, ctx, :, channels], sems.at[7]).start()
+
+    def halo(side, act):
+        step, tile = (1, 1) if side == 0 else (-1, 0)
+
+        def one(k):
+            to_row = k // (N_CTX - 1)
+            column = k % (N_CTX - 1) + (0 if side == 0 else 1)
+            target = column + step
+            src = staged.at[to_row * 16 + column * TILES_DEV + tile]
+            dst = halo_out.at[side, :, channels]
+            is_own = (to_row == row) & (target == ctx)
+
+            @pl.when(is_own)
+            def _():
+                if act == "start":
+                    pltpu.make_async_copy(src, dst, halo_sems.at[side]).start()
+
+            @pl.when(jnp.logical_not(is_own))
+            def _():
+                far = remote(
+                    src, dst, sems.at[8], halo_sems.at[side], (z * PLANE_DP + to_row, target)
+                )
+                if act == "start":
+                    far.start()
+                else:
+                    far.wait_send()
+
+        @pl.when(ctx == (N_CTX - 1 if side == 0 else 0))
+        def _():
+            repeat(0, PLANE_DP * (N_CTX - 1), one)
+
+    for act in ("start", "sent"):
+        for side in (0, 1):
+            halo(side, act)
+    repeat(1, PLANE, lambda k: copy(k).wait_send())
+    main.sent()
+    extra.sent()
+    repeat(1, N_CTX, lambda k: mix_copy(k).wait_send())
+    await_all(heads_out, sems.at[5])
+    await_all(rows_out, sems.at[7])
+
+    @pl.when(ctx > 0)
+    def _():
+        await_all(halo_out.at[0], halo_sems.at[0])
+
+    @pl.when(ctx < N_CTX - 1)
+    def _():
+        await_all(halo_out.at[1], halo_sems.at[1])
+
+
+def to_conv(table, held, mix):
+    unit = (16, WIDE)
+    kind = held.dtype
+
+    def buffer(count):
+        return pltpu.VMEM((count,) + unit, kind)
+
+    return pl.pallas_call(
+        conv_kernel,
+        out_shape=(
+            jax.ShapeDtypeStruct((TILES_DEV, N_CTX, 16, CHANNELS), kind),
+            jax.ShapeDtypeStruct((2, 16, CHANNELS), kind),
+            jax.ShapeDtypeStruct((COLUMN, N_CTX * LANES), kind),
+        ),
+        in_specs=[
+            pl.BlockSpec(memory_space=pltpu.SMEM),
+            pl.BlockSpec(memory_space=pltpu.VMEM),
+            pl.BlockSpec(memory_space=pl.ANY),
+        ],
+        out_specs=[pl.BlockSpec(memory_space=pl.ANY)] * 3,
+        scratch_shapes=[buffer(MAIN), buffer(MAIN), buffer(EXTRA), buffer(EXTRA), buffer(HELD)]
+        + [pltpu.SemaphoreType.DMA((9,)), pltpu.SemaphoreType.DMA((2,))],
+        compiler_params=pltpu.CompilerParams(
+            collective_id=2, has_side_effects=True, vmem_limit_bytes=32 * 2**20
+        ),
+        name="to_conv",
+    )(table, held, mix)
+
+
+def attend_kernel(len_ref, q_ref, k_ref, v_ref, out_ref):
+    block = pl.program_id(0)
+    ends = [len_ref[0, 0]]
+    for i in range(1, 4):
+        ends.append(ends[-1] + len_ref[0, i])
+    first = block * UNITS
+    last = first + UNITS - 1
+    low = jnp.int32(0)
+    high = jnp.int32(FRAMES // SEG_UNIT)
+    for end in ends:
+        low = jnp.where(end <= first, jnp.maximum(low, end), low)
+        high = jnp.where(end > last, jnp.minimum(high, end), high)
+    per_key = KBLOCK // SEG_UNIT
+    low_block = low // per_key
+    high_block = (high + per_key - 1) // per_key
+
+    def segment(unit):
+        seg = jnp.zeros(unit.shape, jnp.int32)
+        for end in ends[:3]:
+            seg = seg + (unit >= end).astype(jnp.int32)
+        return seg
+
+    queries = q_ref[...] * 0.125
+    lane = lax.broadcasted_iota(jnp.int32, (QBLOCK, LANES), 1)
+    zero = jnp.zeros_like(queries)
+    both = jnp.concatenate(
+        [jnp.where(lane < HEAD_DIM, queries, zero), jnp.where(lane < HEAD_DIM, zero, queries)], axis=0
+    )
+    row = lax.broadcasted_iota(jnp.int32, (2 * QBLOCK, 1), 0)
+    row_seg = segment(first + lax.rem(row, QBLOCK) // SEG_UNIT)
+    def step(index, carry):
+        top, total, mixed = carry
+        part = pl.ds(pl.multiple_of(index * KBLOCK, KBLOCK), KBLOCK)
+        keys = k_ref[part, :]
+        values = v_ref[part, :]
+        scores = lax.dot_general(
+            both, keys, (((1,), (1,)), ((), ())), preferred_element_type=jnp.float32
+        )
+        col = lax.broadcasted_iota(jnp.int32, (1, KBLOCK), 1)
+        col_seg = segment(index * per_key + col // SEG_UNIT)
+        scores = jnp.where(row_seg == col_seg, scores, -2e30)
+        new_top = jnp.maximum(top, jnp.max(scores, axis=1, keepdims=True))
+        weights = jnp.exp(scores - new_top)
+        scale = jnp.exp(top - new_top)
+        total = total * scale + jnp.sum(weights, axis=1, keepdims=True)
+        mixed = mixed * scale + jnp.dot(
+            weights.astype(jnp.bfloat16), values, preferred_element_type=jnp.float32
+        )
+        return new_top, total, mixed
+
+    top, total, mixed = lax.fori_loop(
+        low_block,
+        high_block,
+        step,
+        (
+            jnp.full((2 * QBLOCK, 1), -1e30, jnp.float32),
+            jnp.zeros((2 * QBLOCK, 1), jnp.float32),
+            jnp.zeros((2 * QBLOCK, LANES), jnp.float32),
+        ),
+    )
+    mixed = mixed / total
+    out_ref[0] = jnp.where(lane < HEAD_DIM, mixed[:QBLOCK], mixed[QBLOCK:]).astype(jnp.bfloat16)
+
+
+def attend(lengths, q, k, v):
+    blocks = FRAMES // QBLOCK
+    return pl.pallas_call(
+        attend_kernel,
+        grid_spec=pltpu.PrefetchScalarGridSpec(
+            num_scalar_prefetch=1,
+            grid=(blocks,),
+            in_specs=[
+                pl.BlockSpec((QBLOCK, LANES), lambda i, lens: (i, 0)),
+                pl.BlockSpec((FRAMES, LANES), lambda i, lens: (0, 0)),
+                pl.BlockSpec((FRAMES, LANES), lambda i, lens: (0, 0)),
+            ],
+            out_specs=pl.BlockSpec((1, QBLOCK, LANES), lambda i, lens: (i, 0, 0)),
+        ),
+        out_shape=jax.ShapeDtypeStruct((blocks, QBLOCK, LANES), jnp.bfloat16),
+        compiler_params=pltpu.CompilerParams(vmem_limit_bytes=48 * 2**20),
+        cost_estimate=pl.CostEstimate(
+            flops=8 * FRAMES * FRAMES * LANES, bytes_accessed=2**21, transcendentals=2 * FRAMES * FRAMES
+        ),
+        name="attend",
+    )(lengths, q, k, v)
 
 
 def with_halo(cells, sides, width):
@@ -62,7 +837,7 @@
     return (new_max, norm_total, accumulated)
 
 
-def on_device(
+def general_path(
     query_loader,
     key_loader,
     value_loader,
@@ -139,6 +914,51 @@
     return (attention_out, conv_out.reshape(1, row_count, signal.shape[1]))
 
 
+def convolve(signal, halo, lengths, conv_taps, norm_scale, norm_shift):
+    seg_ends = jnp.cumsum(lengths[0])
+    column = lax.axis_index("ctx")
+    half_width = (KERNEL - 1) // 2
+    query_seg = segment_of(column * COLUMN + jnp.arange(COLUMN, dtype=jnp.int32), seg_ends)
+    before = jnp.where(column > 0, halo[0], 0)
+    after = jnp.where(column < N_CTX - 1, halo[1], 0)
+    padded = jnp.concatenate([before[1:], signal, after[:half_width]], axis=0).astype(jnp.float32)
+    padded_seg = segment_of(
+        column * COLUMN - half_width + jnp.arange(COLUMN + 2 * half_width, dtype=jnp.int32), seg_ends
+    )
+    conv_sum = jnp.zeros(signal.shape, jnp.float32)
+    for tap in range(KERNEL):
+        same_seg = (padded_seg[tap : tap + COLUMN] == query_seg)[:, None]
+        conv_sum = conv_sum + jnp.where(same_seg, conv_taps[tap] * padded[tap : tap + COLUMN], 0.0)
+    return jax.nn.silu(norm_scale * conv_sum + norm_shift).astype(jnp.bfloat16)
+
+
+def on_device(*inputs):
+    query, key, value, conv, slot_tile, lengths, conv_taps, norm_scale, norm_shift = inputs
+    places = jnp.transpose(slot_tile[0].reshape(N_Z, 8))
+    places = jnp.pad(places, ((0, 0), (0, LANES - N_Z)), constant_values=1 << 16)
+    shape = (TILES_DEV, PLANE_DP, SEG_UNIT, HEADS * HEAD_DIM)
+    held_q, lists = first(query.reshape(shape), places)
+    table = route(lists.reshape(HELD, LANES))
+    q, k, v, held_conv = to_heads(
+        table,
+        held_q,
+        key.reshape(shape),
+        value.reshape(shape),
+        conv.reshape(TILES_DEV, N_CTX, 16, CHANNELS),
+    )
+    heads = (FRAMES, LANES)
+    mix = attend(lengths, q.reshape(heads), k.reshape(heads), v.reshape(heads))
+    rows, halo, attention_out = to_conv(table, held_conv, mix)
+    conv_out = convolve(
+        rows.reshape(COLUMN, CHANNELS), halo, lengths, conv_taps, norm_scale, norm_shift
+    )
+    return lax.cond(
+        table[AT_BAD] == 0,
+        lambda: (attention_out[None], conv_out[None]),
+        lambda: general_path(*inputs),
+    )
+
+
 def solution(mesh):
     return jax.shard_map(
         on_device,

time: 489 us -> 291 us (0.60)
  the two profiles are of different devices: /device:TPU:26 before, /device:TPU:1 now
where the time goes in v2:
time: 291 us; the launch traced here: 288 us
  Pallas kernels  255 us (88%)
  between operations  14.9 us (5%)
  other arithmetic  12.2 us (4%)
  local copies, waits for them, and re-layouts  6.39 us (2%)
    pallas_call x1, Pallas kernels, to_heads(): pl.pallas_call(heads_kernel, out_shape=(heads, heads, heads, jax.ShapeDty...  112 us
    pallas_call x1, Pallas kernels, to_conv(): pl.pallas_call(conv_kernel, out_shape=(jax.ShapeDtypeStruct((TILES_DEV, N...  74.2 us
    pallas_call x1, Pallas kernels, route(): pl.pallas_call(route_kernel, out_shape=jax.ShapeDtypeStruct((TABLE,), jnp...  27.1 us
    pallas_call x1, Pallas kernels, attend(): pl.pallas_call(attend_kernel, grid_spec=pltpu.PrefetchScalarGridSpec(num_...  21.7 us
    pallas_call x1, Pallas kernels, first(): pl.pallas_call(first_kernel, out_shape=(jax.ShapeDtypeStruct((HELD, SEG_U...  19.7 us
    convert_element_type x1, other arithmetic, convolve(): return jax.nn.silu(norm_scale * conv_sum + norm_shift).astype(jnp.bfloat16)  10.1 us

profile of v2, /device:TPU:1, one launch (start us, length us, event | category | flops | bytes accessed | tf_op | source)
XLA Modules:
  0.0 288.4 jit_solution(14045968632357555510)
XLA Ops:
  7.2 0.5 broadcast.383
  7.7 1.3 reduce.131
  9.2 0.6 pad.4.list_ref
  9.8 19.7 %spread_queries.1 = (bf16[64,32,128]{2,1,0:T(8,128)(2,1)}, s32[8,8,128]{2,1,0:T(8,128)}) custom-call(bf16[2,4,32,1024]{3,2,1,0:T(8,128)(2,1)} %bitcast.70, s32[8,128]{1,0:T(8,128)} %pad.4.list_ref), custom_call_target="tpu_custom_call" | custom-call | tf_op jit(solution)/shard_map/spread_queries/pallas_call | solution.py:212
  29.5 27.1 %route.1.table = s32[256]{0:T(256)} custom-call(s32[64,128]{1,0:T(8,128)} %bitcast.76), custom_call_target="tpu_custom_call" | custom-call | tf_op jit(solution)/shard_map/route/pallas_call | solution.py:451
  56.6 1.0 copy-done
  57.6 0.7 copy-done.1
  58.3 111.9 %to_heads.1 = (bf16[16,4,32,128]{3,2,1,0:T(8,128)(2,1)S(1)}, bf16[16,4,32,128]{3,2,1,0:T(8,128)(2,1)S(1)}, bf16[16,4,32,128]{3,2,1,0:T(8,128)(2,1)S(1)}, bf16[64,16,384]{2,1,0:T(8,128)(2,1)S(1)}) custom-call(s32[256]{0:T(256)S(1)} %copy-done.1, bf16[64,32,128]{2,1,0:T(8,128)(2,1)S(1)} %copy-done, bf16[2,4,32,1024]{3,2,1,0:T(8,128)(2,1)} %bitcast.73, ...), custom_call_target="tpu_custom_call" | custom-call | tf_op jit(solution)/shard_map/to_heads/pallas_call | solution.py:552
  170.3 21.7 %attend.1.mix_ref = bf16[8,256,128]{2,1,0:T(8,128)(2,1)S(1)} custom-call(s32[1,4]{1,0:T(1,128)S(1)} %copy-done.59, bf16[2048,128]{1,0:T(8,128)(2,1)S(1)} %bitcast.58, bf16[2048,128]{1,0:T(8,128)(2,1)S(1)} %bitcast.59, bf16[2048,128]{1,0:T(8,128)(2,1)S(1)} %bitcast.60), custom_call_target="tpu_custom_call" | custom-call | flops 4294967296 | bytes 2097152 | tf_op jit(solution)/shard_map/attend/pallas_call | solution.py:768
  192.0 74.2 %to_conv.1 = (bf16[2,8,16,1536]{3,2,1,0:T(8,128)(2,1)S(1)}, bf16[2,16,1536]{2,1,0:T(8,128)(2,1)S(1)}, bf16[256,1024]{1,0:T(8,128)(2,1)}) custom-call(s32[256]{0:T(256)S(1)} %copy-done.2, bf16[64,16,384]{2,1,0:T(8,128)(2,1)S(1)} %get-tuple-element.46.held, bf16[8,256,128]{2,1,0:T(8,128)(2,1)S(1)} %attend.1.mix_ref), custom_call_target="tpu_custom_call" | custom-call | tf_op jit(solution)/shard_map/to_conv/pallas_call | solution.py:680
  266.3 0.2 maximum_convert_fusion.1
  266.6 0.2 reduce-window.16
  266.8 0.1 convert_reduce_fusion.3
  266.9 0.1 convert_reduce_fusion.4
  267.0 0.1 slice_compare_fusion.61
  267.1 0.1 slice_compare_fusion.60
  267.2 0.3 slice_reduce_fusion.61
  267.5 0.2 slice_reduce_fusion.60
  267.7 10.1 %multiply_convert_fusion.1 = bf16[256,1536]{1,0:T(8,128)(2,1)} fusion(f32[286,1536]{1,0:T(8,128)S(1)} %maximum_convert_fusion.1, f32[1536]{0:T(1024)S(1)} %copy-done.17, f32[1536]{0:T(1024)S(1)} %get-tuple-element.136, f32[1536]{0:T(1024)S(1)} %get-tuple-element.137, f32[1536]{0:T(1024)S(1)} %get-tuple-element.108, f32[1536]{0:T(1024)S(1)} %get-tuple-element.109, ...), kind=kLoop, calls=%fused_computation.298 | loop fusion | flops 38928384 | bytes 49755904 | tf_op jit(solution)/shard_map/convert_element_type | solution.py:932
  277.8 0.6 slice.585
  279.1 1.7 conditional.1
  279.3 1.2 copy.84
  280.6 0.2 copy.87
  280.8 0.8 copy-done.13
  (23 shorter events, 0.3 us)
Async XLA Ops:
  7.2 163.1 %copy-start.59 = (s32[1,4]{1,0:T(1,128)S(1)}, s32[1,4]{1,0:T(1,128)}, u32[]{:S(2)}) copy-start(s32[1,4]{1,0:T(1,128)} %len_ref.1) | copy-start | bytes 52
  56.6 1.0 copy-start
  57.6 0.7 copy-start.1
  170.3 21.8 %copy-start.2 = (s32[256]{0:T(256)S(1)}, s32[256]{0:T(256)}, u32[]{:S(2)}) copy-start(s32[256]{0:T(256)} %route.1.table) | copy-start | bytes 3076
  266.2 0.9 copy-start.12
  266.3 1.4 copy-start.14
  266.3 1.4 copy-start.17
  267.7 11.3 %copy-start.3 = (bf16[1,256,1536]{2,1,0:T(8,128)(2,1)S(1)}, bf16[1,256,1536]{2,1,0:T(8,128)(2,1)}, u32[]{:S(2)}) copy-start(bf16[1,256,1536]{2,1,0:T(8,128)(2,1)} %param.14) | copy-start | bytes 2359300
  267.7 11.3 %copy-start.58 = (s32[1,128]{1,0:T(1,128)S(1)}, s32[1,128]{1,0:T(1,128)}, u32[]{:S(2)}) copy-start(s32[1,128]{1,0:T(1,128)} %param.15) | copy-start | bytes 1540
  280.8 0.8 copy-start.13

commit v3 on v1

v3 whole, which is shorter than its diff:
```python
import jax
import jax.numpy as jnp
from jax import lax
from jax.experimental import pallas as pl
from jax.experimental.pallas import tpu as pltpu
from jax.sharding import PartitionSpec as P

MESH = pl.DeviceIdType.MESH
HEADS = 16
HEAD_DIM = 64
CHANNELS = 1536
KERNEL = 31
TILE = 128
TILES_DEV = 2
SEG_UNIT = 32
FRAMES = 2048
COLUMN = 256
LANES = 128
N_DP = 64
N_CTX = 8
ROWS = 16
QKV = 3 * ROWS
CONV_ROWS = 24
QBLOCK = 256
KBLOCK = 256
UNITS = QBLOCK // SEG_UNIT

N_Z = 16
PLANE_DP = 4
PLANE = PLANE_DP * N_CTX
HELD = PLANE * TILES_DEV
SHIFTS = N_Z - 1
NEAR, NEAR_SLOTS, FAR_SLOTS = 6, 5, 4
RELAYS, RELAY_SLOTS = 10, 2
MAIN = NEAR * NEAR_SLOTS + (SHIFTS - NEAR) * FAR_SLOTS
EXTRA = RELAYS * RELAY_SLOTS
TABLE = 256
AT_MAIN, AT_EXTRA, AT_FINAL, AT_BAD = 0, 72, 96, 160
RANKS = 16
PAIRS = N_Z * N_Z
LIST = 2304
FIELDS = 0x55555555


def shift_of(j):
    half = j // 2
    return jnp.where(j % 2 == 0, half + 1, N_Z - 1 - half)


def order_of(shift):
    return jnp.where(shift <= N_Z // 2, 2 * (shift - 1), 2 * (N_Z - shift) - 1)


def main_slots(shift):
    return jnp.where(order_of(shift) < NEAR, NEAR_SLOTS, FAR_SLOTS)


def main_offset(shift):
    j = order_of(shift)
    return jnp.where(j < NEAR, NEAR_SLOTS * j, NEAR * NEAR_SLOTS + FAR_SLOTS * (j - NEAR))


def relay_offset(shift):
    return RELAY_SLOTS * order_of(shift)


def place():
    dp, ctx = lax.axis_index("dp"), lax.axis_index("ctx")
    return dp // PLANE_DP, dp % PLANE_DP, ctx


def plane_peer(z, row, ctx, k):
    index = (row * N_CTX + ctx + k) % PLANE
    return index // N_CTX, index % N_CTX, (z * PLANE_DP + index // N_CTX, index % N_CTX)


def z_peer(z, row, ctx, j):
    return ((z + shift_of(j)) % N_Z * PLANE_DP + row, ctx)


def repeat(first, last, body):
    def one(k, carry):
        body(k)
        return carry

    lax.fori_loop(first, last, one, 0)


def remote(src, dst, send, recv, device):
    return pltpu.make_async_remote_copy(
        src_ref=src, dst_ref=dst, send_sem=send, recv_sem=recv, device_id=device, device_id_type=MESH
    )


def await_all(ref, sem):
    pltpu.make_async_copy(ref, ref, sem).wait()


def signal(device):
    pl.semaphore_signal(pltpu.get_barrier_semaphore(), inc=1, device_id=device, device_id_type=MESH)


class Spread:
    def __init__(self, piece, held, send, recv):
        z, row, ctx = place()
        mine = pl.ds((ctx * PLANE_DP + row) * TILES_DEV, TILES_DEV)

        def copy(k):
            to_row, to_ctx, device = plane_peer(z, row, ctx, k)
            return remote(piece(to_row, to_ctx), held.at[mine], send, recv, device)

        self.copy, self.held, self.recv = copy, held, recv
        self.own = pltpu.make_async_copy(piece(row, ctx), held.at[mine], recv)

    def start(self):
        repeat(1, PLANE, lambda k: self.copy(k).start())
        self.own.start()

    def arrived(self):
        await_all(self.held, self.recv)

    def sent(self):
        repeat(1, PLANE, lambda k: self.copy(k).wait_send())


class Along:
    def __init__(self, groups, staged, got, send, recv):
        z, row, ctx = place()
        self.staged, self.got, self.send, self.recv = staged, got, send, recv

        def copy(j, offset, slots):
            part = pl.ds(offset, slots)
            return remote(staged.at[part], got.at[part], send, recv, z_peer(z, row, ctx, j))

        self.copy, self.groups = copy, groups

    def start(self):
        for first, last, base, slots in self.groups:
            repeat(
                first,
                last,
                lambda j: self.copy(j, base + (j - first) * slots, slots).start(),
            )

    def arrived(self):
        await_all(self.got, self.recv)

    def sent(self):
        await_all(self.staged, self.send)


MAIN_GROUPS = ((0, NEAR, 0, NEAR_SLOTS), (NEAR, SHIFTS, NEAR * NEAR_SLOTS, FAR_SLOTS))
EXTRA_GROUPS = ((0, RELAYS, 0, RELAY_SLOTS),)


def stage_main(table, held, staged):
    def one(i):
        staged[i] = held[table[AT_MAIN + i]]

    repeat(0, MAIN, one)


def stage_extra(table, held, got, staged):
    def one(i):
        code = table[AT_EXTRA + i]
        staged[i] = jnp.where(
            code < HELD, held[jnp.minimum(code, HELD - 1)], got[jnp.clip(code - HELD, 0, MAIN - 1)]
        )

    repeat(0, EXTRA, one)


def stage_final(table, held, got, more, staged):
    def one(i):
        code = table[AT_FINAL + i]
        first = held[jnp.minimum(code, HELD - 1)]
        second = got[jnp.clip(code - HELD, 0, MAIN - 1)]
        third = more[jnp.clip(code - HELD - MAIN, 0, EXTRA - 1)]
        staged[i] = jnp.where(code < HELD, first, jnp.where(code < HELD + MAIN, second, third))

    repeat(0, HELD, one)


def head_piece(ref):
    return lambda row, ctx: ref.at[:, row, :, pl.ds(pl.multiple_of(ctx * LANES, LANES), LANES)]


WIDE = CHANNELS // PLANE_DP


def conv_piece(ref):
    return lambda row, ctx: ref.at[:, ctx, :, pl.ds(pl.multiple_of(row * WIDE, LANES), WIDE)]


def first_kernel(q_ref, list_ref, held_ref, lists_ref, send, recv, list_send, list_recv):
    z, row, ctx = place()
    repeat(1, PLANE, lambda k: signal(plane_peer(z, row, ctx, k)[2]))
    pl.semaphore_wait(pltpu.get_barrier_semaphore(), PLANE - 1)

    def tell(k):
        device = (z * PLANE_DP + row, (ctx + k) % N_CTX)
        return remote(list_ref, lists_ref.at[ctx], list_send, list_recv, device)

    repeat(1, N_CTX, lambda k: tell(k).start())
    pltpu.make_async_copy(list_ref, lists_ref.at[ctx], list_recv).start()
    spread = Spread(head_piece(q_ref), held_ref, send, recv)
    spread.start()
    repeat(1, N_CTX, lambda k: tell(k).wait_send())
    await_all(lists_ref, list_recv)
    spread.arrived()
    spread.sent()


def first(q, own_list):
    return pl.pallas_call(
        first_kernel,
        out_shape=(
            jax.ShapeDtypeStruct((HELD, SEG_UNIT, LANES), q.dtype),
            jax.ShapeDtypeStruct((N_CTX,) + own_list.shape, own_list.dtype),
        ),
        in_specs=[pl.BlockSpec(memory_space=pl.ANY)] * 2,
        out_specs=[pl.BlockSpec(memory_space=pl.ANY)] * 2,
        scratch_shapes=[pltpu.SemaphoreType.DMA] * 4,
        compiler_params=pltpu.CompilerParams(collective_id=0, has_side_effects=True),
        name="spread_queries",
    )(q, own_list)


def filled(fields):
    return (fields | (fields >> 1)) & FIELDS


def field_index(bit):
    def step(mask, worth):
        return jnp.where((bit & mask) != 0, worth, 0)

    high = jnp.where(bit >= (1 << 16), 8, 0)
    return high + step(0x7F00FF00, 4) + step(0x70F0F0F0, 2) + step(0x4CCCCCCC & FIELDS, 1)


def field_value(fields, bit):
    return jnp.where((fields & bit) != 0, 1, 0) + jnp.where((fields & (bit << 1)) != 0, 2, 0)


def relay_fields(y):
    fields = 0
    for m in range(N_Z):
        shift = (y - m) % N_Z
        order = 2 * (shift - 1) if shift <= N_Z // 2 else 2 * (N_Z - shift) - 1
        if shift and order < RELAYS:
            fields |= RELAY_SLOTS << (2 * m)
    return fields - (1 << 32) if fields >= 1 << 31 else fields


LOW, HIGH, OVER = N_Z, N_Z + 1, N_Z + 2


def route_kernel(
    lists_ref,
    table,
    count_v,
    excess_v,
    tile_v,
    slot_v,
    count,
    excess,
    tile,
    slot,
    direct,
    relay_free,
    sems,
):
    me = lax.axis_index("dp") // PLANE_DP
    tiles = lists_ref[...]
    source = tiles >> 3
    rows = lax.broadcasted_iota(jnp.int32, (HELD, LANES), 0)
    lanes = lax.broadcasted_iota(jnp.int32, (HELD, LANES), 1)
    local = (rows & ~7) + (tiles & 7)
    position = ((rows & 7) >> 1) * 16 + (rows >> 3) * 2 + (rows & 1)

    def total(values):
        return jnp.sum(values, axis=0, keepdims=True, dtype=jnp.int32)

    for i in range(N_Z):
        count_v[pl.ds(i, 1), :] = total(jnp.where(source == i, 1, 0))
    held = count_v[...]
    z = lax.broadcasted_iota(jnp.int32, held.shape, 0)
    y = lax.broadcasted_iota(jnp.int32, held.shape, 1)
    shift = (y - z) & 15
    stays = shift == 0
    most = jnp.where(stays, RANKS, main_slots(shift))
    real = y < N_Z
    left = jnp.where(stays, 3, jnp.clip(most - held, 0, 3)) << (2 * (y & 7))
    low = jnp.sum(jnp.where(y < 8, left, 0), axis=1, keepdims=True)
    high = jnp.sum(jnp.where((y >= 8) & real, left, 0), axis=1, keepdims=True)
    over = jnp.max(jnp.where(real & (held > RANKS), 1, 0), axis=1, keepdims=True)
    extra = jnp.where(real, jnp.maximum(jnp.minimum(held, RANKS) - most, 0), 0)
    extra = jnp.where(y == LOW, low, jnp.where(y == HIGH, high, jnp.where(y == OVER, over, extra)))
    excess_v[...] = extra
    copies = [
        pltpu.make_async_copy(a, b, sems.at[i])
        for i, (a, b) in enumerate(
            ((count_v, count), (excess_v, excess), (tile_v, tile), (slot_v, slot))
        )
    ]
    copies[0].start()
    copies[1].start()

    def add_rank(i, rank):
        other = lists_ref[pl.ds(i, 1), :] >> 3
        return rank + jnp.where((other == source) & (rows > i), 1, 0)

    rank = lax.fori_loop(0, HELD, add_rank, jnp.zeros((HELD, LANES), jnp.int32), unroll=8)
    here = lanes == me
    column_source = jnp.sum(jnp.where(here, source, 0), axis=1, keepdims=True)
    column_rank = jnp.sum(jnp.where(here, rank, 0), axis=1, keepdims=True)
    mine = jnp.where(source == me, rank, -1)
    taken = jnp.where(column_source == lanes, column_rank, -1)
    for i in range(RANKS):
        tile_v[pl.ds(i, 1), :] = total(jnp.where(mine == i, local, 0))
        slot_v[pl.ds(i, 1), :] = total(jnp.where(taken == i, position, 0))
    copies[2].start()
    copies[3].start()
    for i in range(AT_BAD):
        table[i] = 0
    for i in range(N_Z):
        relay_free[i] = jnp.int32(relay_fields(i))
    for copy in copies:
        copy.wait()

    def open_row(z):
        def open_pair(y):
            shift = (y - z) & 15
            most = jnp.where(shift == 0, RANKS, main_slots(shift))
            direct[z * N_Z + y] = jnp.minimum(count[z, y], most)

        for y in range(N_Z):
            open_pair(y)

    repeat(0, N_Z, open_row)
    my_bit = jnp.int32(1) << (2 * me)

    def record(z, y, bit, rank, free, relay, main):
        @pl.when((z == me) | (bit == my_bit) | (y == me))
        def _():
            m = field_index(bit)
            own = jnp.where(main >= 0, main, count[z, m] + field_value(free, bit) - 1)
            main_at = main_offset((m - z) & 15) + own
            extra_at = relay_offset((y - m) & 15) + field_value(relay, bit) - 1

            @pl.when((z == me) & (m != z))
            def _():
                table[AT_MAIN + main_at] = tile[rank, y]

            @pl.when(m == me)
            def _():
                table[AT_EXTRA + extra_at] = jnp.where(m == z, tile[rank, y], HELD + main_at)

            @pl.when(y == me)
            def _():
                table[AT_FINAL + slot[rank, z]] = HELD + MAIN + extra_at

    def place_row(z, bad):
        own = jnp.int32(1) << (2 * z)

        def take(free, bit):
            return free - jnp.where(bit == own, 0, bit)

        def place_pair(i, carry):
            y = (i + z) & 15
            most = main_slots(i)

            def place_one(e, carry):
                free, bad = carry
                relay = relay_free[y]
                open_ = filled(free) & filled(relay)

                def simple():
                    late = open_ & (jnp.int32(-1) << (2 * ((y + 8) & 15)))
                    chosen = jnp.where(late != 0, late, open_)
                    bit = chosen & -chosen
                    record(z, y, bit, most + e, free, relay, jnp.int32(-1))
                    relay_free[y] = relay - bit
                    return take(free, bit), bad

                def swap():
                    def look(m, carry):
                        free, done = carry
                        bit = jnp.int32(1) << (2 * m)
                        relay_m = relay_free[m]
                        other = filled(free) & filled(relay_m)
                        straight = direct[z * N_Z + m]
                        fits = (
                            (done == 0)
                            & (m != z)
                            & (m != y)
                            & ((filled(relay) & bit) != 0)
                            & (straight > 0)
                            & (other != 0)
                        )

                        def do():
                            instead = other & -other
                            direct[z * N_Z + m] = straight - 1
                            record(z, m, instead, straight - 1, free, relay_m, jnp.int32(-1))
                            record(z, y, bit, most + e, free, relay, straight - 1)
                            relay_free[m] = relay_m - instead
                            relay_free[y] = relay - bit
                            return take(free, instead), jnp.int32(1)

                        return lax.cond(fits, do, lambda: (free, done))

                    free_, done = lax.fori_loop(0, N_Z, look, (free, jnp.int32(0)))
                    return free_, bad | (1 - done)

                return lax.cond(open_ != 0, simple, swap)

            return lax.fori_loop(0, excess[z, y], place_one, carry)

        free = excess[z, LOW] | (excess[z, HIGH] << 16)
        free, bad = lax.fori_loop(1, N_Z, place_pair, (free, bad | excess[z, OVER]))
        return bad

    table[AT_BAD] = lax.fori_loop(0, N_Z, place_row, jnp.int32(0))

    def straight(other):
        shift_out = (other - me) & 15
        shift_in = (me - other) & 15

        @pl.when(shift_out != 0)
        def _():
            first_out = AT_MAIN + main_offset(shift_out)
            first_in = HELD + main_offset(shift_in)

            def out(r):
                table[first_out + r] = tile[r, other]

            def arrive(r):
                table[AT_FINAL + slot[r, other]] = first_in + r

            repeat(0, direct[me * N_Z + other], out)
            repeat(0, direct[other * N_Z + me], arrive)

        @pl.when(shift_out == 0)
        def _():
            def keep(r):
                table[AT_FINAL + slot[r, me]] = tile[r, me]

            repeat(0, direct[me * N_Z + me], keep)

    repeat(0, N_Z, straight)


def route(lists):
    smem = pltpu.SMEM
    square = smem((N_Z, LANES), jnp.int32)
    square_v = pltpu.VMEM((N_Z, LANES), jnp.int32)
    return pl.pallas_call(
        route_kernel,
        out_shape=jax.ShapeDtypeStruct((TABLE,), jnp.int32),
        in_specs=[pl.BlockSpec(memory_space=pltpu.VMEM)],
        out_specs=pl.BlockSpec(memory_space=smem),
        scratch_shapes=[square_v] * 4
        + [square] * 4
        + [smem((PAIRS,), jnp.int32), smem((N_Z,), jnp.int32), pltpu.SemaphoreType.DMA((4,))],
        name="route",
    )(lists)


def exchange_kernel(
    table, held_q, conv_ref, k_ref, v_ref, q_out, k_out, v_out, rows_out, halo_out, *scratch
):
    z, row, ctx = place()
    repeat(1, PLANE, lambda k: signal(plane_peer(z, row, ctx, k)[2]))
    repeat(0, SHIFTS, lambda j: signal(z_peer(z, row, ctx, j)))
    pl.semaphore_wait(pltpu.get_barrier_semaphore(), PLANE - 1 + SHIFTS)
    held = (held_q,) + scratch[:3]
    main_staged, main_got, extra_staged, extra_got, staged = (
        scratch[3 + 4 * i : 7 + 4 * i] for i in range(5)
    )
    sems, halo_sems = scratch[23:]
    outs = (q_out, rows_out, k_out, v_out)
    pieces = (None, conv_piece(conv_ref), head_piece(k_ref), head_piece(v_ref))
    spread = [None] + [
        Spread(pieces[i], held[i], sems.at[0, i], sems.at[1, i]) for i in range(1, 4)
    ]
    main = [
        Along(MAIN_GROUPS, main_staged[i], main_got[i], sems.at[2, i], sems.at[3, i])
        for i in range(4)
    ]
    extra = [
        Along(EXTRA_GROUPS, extra_staged[i], extra_got[i], sems.at[4, i], sems.at[5, i])
        for i in range(4)
    ]

    def start_main(i):
        if i:
            spread[i].arrived()
        stage_main(table, held[i], main_staged[i])
        main[i].start()

    def start_extra(i):
        main[i].arrived()
        stage_extra(table, held[i], main_got[i], extra_staged[i])
        extra[i].start()

    def head_copy(i, k):
        to = (row + k) % PLANE_DP
        return remote(
            staged[i].at[pl.ds(to * 16, 16)],
            outs[i].at[:, row],
            sems.at[6, i],
            sems.at[7, i],
            (z * PLANE_DP + to, ctx),
        )

    channels = pl.ds(pl.multiple_of(row * WIDE, LANES), WIDE)

    def part(to_row, to_ctx):
        return staged[1].at[pl.ds(to_row * 16 + to_ctx * TILES_DEV, TILES_DEV)]

    def conv_copy(k):
        to_row, to_ctx, device = plane_peer(z, row, ctx, k)
        return remote(
            part(to_row, to_ctx), rows_out.at[:, ctx, :, channels], sems.at[6, 1], sems.at[7, 1], device
        )

    def halo(side, act):
        step, tile = (1, 1) if side == 0 else (-1, 0)

        def one(k):
            to_row = k // (N_CTX - 1)
            column = k % (N_CTX - 1) + (0 if side == 0 else 1)
            target = column + step
            src = staged[1].at[to_row * 16 + column * TILES_DEV + tile]
            dst = halo_out.at[side, :, channels]
            is_own = (to_row == row) & (target == ctx)

            @pl.when(is_own)
            def _():
                if act == "start":
                    pltpu.make_async_copy(src, dst, halo_sems.at[side]).start()

            @pl.when(jnp.logical_not(is_own))
            def _():
                far = remote(
                    src, dst, halo_sems.at[2], halo_sems.at[side], (z * PLANE_DP + to_row, target)
                )
                if act == "start":
                    far.start()
                else:
                    far.wait_send()

        @pl.when(ctx == (N_CTX - 1 if side == 0 else 0))
        def _():
            repeat(0, PLANE_DP * (N_CTX - 1), one)

    def start_final(i):
        extra[i].arrived()
        stage_final(table, held[i], main_got[i], extra_got[i], staged[i])
        if i == 1:
            repeat(1, PLANE, lambda k: conv_copy(k).start())
            pltpu.make_async_copy(
                part(row, ctx), rows_out.at[:, ctx, :, channels], sems.at[7, 1]
            ).start()
            halo(0, "start")
            halo(1, "start")
        else:
            repeat(1, PLANE_DP, lambda k: head_copy(i, k).start())
            pltpu.make_async_copy(
                staged[i].at[pl.ds(row * 16, 16)], outs[i].at[:, row], sems.at[7, i]
            ).start()

    spread[1].start()
    start_main(0)
    spread[2].start()
    start_main(1)
    spread[3].start()
    start_extra(0)
    start_main(2)
    start_extra(1)
    start_final(0)
    start_main(3)
    start_extra(2)
    start_final(1)
    start_extra(3)
    start_final(2)
    start_final(3)
    halo(0, "sent")
    halo(1, "sent")
    repeat(1, PLANE, lambda k: conv_copy(k).wait_send())
    for i in range(4):
        if i:
            spread[i].sent()
        main[i].sent()
        extra[i].sent()
        if i != 1:
            repeat(1, PLANE_DP, lambda k: head_copy(i, k).wait_send())
        await_all(outs[i], sems.at[7, i])

    @pl.when(ctx > 0)
    def _():
        await_all(halo_out.at[0], halo_sems.at[0])

    @pl.when(ctx < N_CTX - 1)
    def _():
        await_all(halo_out.at[1], halo_sems.at[1])


def exchange(table, held_q, conv, k, v):
    unit = (SEG_UNIT, LANES)
    conv_unit = (16, WIDE)
    kind = held_q.dtype

    def buffers(count):
        return [pltpu.VMEM((count,) + (conv_unit if i == 1 else unit), kind) for i in range(4)]

    heads = jax.ShapeDtypeStruct((N_CTX * TILES_DEV, PLANE_DP) + unit, kind)
    return pl.pallas_call(
        exchange_kernel,
        out_shape=(
            heads,
            heads,
            heads,
            jax.ShapeDtypeStruct((TILES_DEV, N_CTX, 16, CHANNELS), kind),
            jax.ShapeDtypeStruct((2, 16, CHANNELS), kind),
        ),
        in_specs=[pl.BlockSpec(memory_space=pltpu.SMEM), pl.BlockSpec(memory_space=pltpu.VMEM)]
        + [pl.BlockSpec(memory_space=pl.ANY)] * 3,
        out_specs=[pl.BlockSpec(memory_space=pl.ANY)] * 5,
        scratch_shapes=buffers(HELD)[1:]
        + buffers(MAIN)
        + buffers(MAIN)
        + buffers(EXTRA)
        + buffers(EXTRA)
        + buffers(HELD)
        + [pltpu.SemaphoreType.DMA((8, 4)), pltpu.SemaphoreType.DMA((3,))],
        compiler_params=pltpu.CompilerParams(
            collective_id=1, has_side_effects=True, vmem_limit_bytes=40 * 2**20
        ),
        name="exchange",
    )(table, held_q, conv, k, v)


def mix_kernel(mix_ref, heads_out, send, recv):
    z, row, ctx = place()
    dp = z * PLANE_DP + row
    repeat(1, N_CTX, lambda k: signal((dp, (ctx + k) % N_CTX)))
    pl.semaphore_wait(pltpu.get_barrier_semaphore(), N_CTX - 1)
    mixed = heads_out.at[:, pl.ds(pl.multiple_of(ctx * LANES, LANES), LANES)]

    def copy(k):
        to = (ctx + k) % N_CTX
        return remote(mix_ref.at[to], mixed, send, recv, (dp, to))

    repeat(1, N_CTX, lambda k: copy(k).start())
    pltpu.make_async_copy(mix_ref.at[ctx], mixed, recv).start()
    repeat(1, N_CTX, lambda k: copy(k).wait_send())
    await_all(heads_out, recv)


def to_frames(mix):
    return pl.pallas_call(
        mix_kernel,
        out_shape=jax.ShapeDtypeStruct((COLUMN, N_CTX * LANES), mix.dtype),
        in_specs=[pl.BlockSpec(memory_space=pl.ANY)],
        out_specs=pl.BlockSpec(memory_space=pl.ANY),
        scratch_shapes=[pltpu.SemaphoreType.DMA, pltpu.SemaphoreType.DMA],
        compiler_params=pltpu.CompilerParams(collective_id=2, has_side_effects=True),
        name="to_frames",
    )(mix)


def attend_kernel(len_ref, q_ref, k_ref, v_ref, out_ref):
    block = pl.program_id(0)
    ends = [len_ref[0, 0]]
    for i in range(1, 4):
        ends.append(ends[-1] + len_ref[0, i])
    first = block * UNITS
    last = first + UNITS - 1
    low = jnp.int32(0)
    high = jnp.int32(FRAMES // SEG_UNIT)
    for end in ends:
        low = jnp.where(end <= first, jnp.maximum(low, end), low)
        high = jnp.where(end > last, jnp.minimum(high, end), high)
    per_key = KBLOCK // SEG_UNIT
    low_block = low // per_key
    high_block = (high + per_key - 1) // per_key

    def segment(unit):
        seg = jnp.zeros(unit.shape, jnp.int32)
        for end in ends[:3]:
            seg = seg + (unit >= end).astype(jnp.int32)
        return seg

    queries = q_ref[...] * 0.125
    lane = lax.broadcasted_iota(jnp.int32, (QBLOCK, LANES), 1)
    zero = jnp.zeros_like(queries)
    both = jnp.concatenate(
        [jnp.where(lane < HEAD_DIM, queries, zero), jnp.where(lane < HEAD_DIM, zero, queries)], axis=0
    )
    row = lax.broadcasted_iota(jnp.int32, (2 * QBLOCK, 1), 0)
    row_seg = segment(first + lax.rem(row, QBLOCK) // SEG_UNIT)
    def step(index, carry):
        top, total, mixed = carry
        part = pl.ds(pl.multiple_of(index * KBLOCK, KBLOCK), KBLOCK)
        keys = k_ref[part, :]
        values = v_ref[part, :]
        scores = lax.dot_general(
            both, keys, (((1,), (1,)), ((), ())), preferred_element_type=jnp.float32
        )
        col = lax.broadcasted_iota(jnp.int32, (1, KBLOCK), 1)
        col_seg = segment(index * per_key + col // SEG_UNIT)
        scores = jnp.where(row_seg == col_seg, scores, -2e30)
        new_top = jnp.maximum(top, jnp.max(scores, axis=1, keepdims=True))
        weights = jnp.exp(scores - new_top)
        scale = jnp.exp(top - new_top)
        total = total * scale + jnp.sum(weights, axis=1, keepdims=True)
        mixed = mixed * scale + jnp.dot(
            weights.astype(jnp.bfloat16), values, preferred_element_type=jnp.float32
        )
        return new_top, total, mixed

    top, total, mixed = lax.fori_loop(
        low_block,
        high_block,
        step,
        (
            jnp.full((2 * QBLOCK, 1), -1e30, jnp.float32),
            jnp.zeros((2 * QBLOCK, 1), jnp.float32),
            jnp.zeros((2 * QBLOCK, LANES), jnp.float32),
        ),
    )
    mixed = mixed / total
    out_ref[0] = jnp.where(lane < HEAD_DIM, mixed[:QBLOCK], mixed[QBLOCK:]).astype(jnp.bfloat16)


def attend(lengths, q, k, v):
    blocks = FRAMES // QBLOCK
    return pl.pallas_call(
        attend_kernel,
        grid_spec=pltpu.PrefetchScalarGridSpec(
            num_scalar_prefetch=1,
            grid=(blocks,),
            in_specs=[
                pl.BlockSpec((QBLOCK, LANES), lambda i, lens: (i, 0)),
                pl.BlockSpec((FRAMES, LANES), lambda i, lens: (0, 0)),
                pl.BlockSpec((FRAMES, LANES), lambda i, lens: (0, 0)),
            ],
            out_specs=pl.BlockSpec((1, QBLOCK, LANES), lambda i, lens: (i, 0, 0)),
        ),
        out_shape=jax.ShapeDtypeStruct((blocks, QBLOCK, LANES), jnp.bfloat16),
        compiler_params=pltpu.CompilerParams(vmem_limit_bytes=48 * 2**20),
        cost_estimate=pl.CostEstimate(
            flops=8 * FRAMES * FRAMES * LANES, bytes_accessed=2**21, transcendentals=2 * FRAMES * FRAMES
        ),
        name="attend",
    )(lengths, q, k, v)


def segment_of(positions, seg_ends):
    unit_index = positions // SEG_UNIT
    return jnp.sum((seg_ends[None, :] <= unit_index[:, None]).astype(jnp.int32), axis=1)


def convolve(signal, halo, lengths, conv_taps, norm_scale, norm_shift):
    seg_ends = jnp.cumsum(lengths[0])
    column = lax.axis_index("ctx")
    half_width = (KERNEL - 1) // 2
    query_seg = segment_of(column * COLUMN + jnp.arange(COLUMN, dtype=jnp.int32), seg_ends)
    before = jnp.where(column > 0, halo[0], 0)
    after = jnp.where(column < N_CTX - 1, halo[1], 0)
    padded = jnp.concatenate([before[1:], signal, after[:half_width]], axis=0).astype(jnp.float32)
    padded_seg = segment_of(
        column * COLUMN - half_width + jnp.arange(COLUMN + 2 * half_width, dtype=jnp.int32), seg_ends
    )
    conv_sum = jnp.zeros(signal.shape, jnp.float32)
    for tap in range(KERNEL):
        same_seg = (padded_seg[tap : tap + COLUMN] == query_seg)[:, None]
        conv_sum = conv_sum + jnp.where(same_seg, conv_taps[tap] * padded[tap : tap + COLUMN], 0.0)
    return jax.nn.silu(norm_scale * conv_sum + norm_shift).astype(jnp.bfloat16)


def share_of(dp, ctx):
    return (dp // 8) * 8 + lax.rem(dp + ctx, 8)


def entry(count, device):
    barrier = pltpu.get_barrier_semaphore()

    def one(k, carry):
        pl.semaphore_signal(barrier, inc=1, device_id=device(k), device_id_type=MESH)
        return carry

    lax.fori_loop(0, count, one, 0)
    pl.semaphore_wait(barrier, count)


def all_arrived(ref, sem):
    pltpu.make_async_copy(ref, ref, sem).wait()


def general_spread_kernel(x_ref, out_ref, send_sem, recv_sem):
    dp, ctx = lax.axis_index("dp"), lax.axis_index("ctx")
    entry(N_DP - 1, lambda k: (lax.rem(dp + 1 + k, N_DP), ctx))

    def copy(k):
        peer = lax.rem(dp + k, N_DP)
        return pltpu.make_async_remote_copy(
            src_ref=x_ref.at[share_of(peer, ctx)],
            dst_ref=out_ref.at[dp],
            send_sem=send_sem,
            recv_sem=recv_sem,
            device_id=(peer, ctx),
            device_id_type=MESH,
        )

    own = pltpu.make_async_copy(x_ref.at[share_of(dp, ctx)], out_ref.at[dp], recv_sem)

    def start(k, carry):
        copy(k).start()
        return carry

    def sent(k, carry):
        copy(k).wait_send()
        return carry

    lax.fori_loop(1, N_DP, start, 0)
    own.start()
    lax.fori_loop(1, N_DP, sent, 0)
    all_arrived(out_ref, recv_sem)


def general_spread(x):
    return pl.pallas_call(
        general_spread_kernel,
        out_shape=jax.ShapeDtypeStruct(x.shape, x.dtype),
        in_specs=[pl.BlockSpec(memory_space=pl.ANY)],
        out_specs=pl.BlockSpec(memory_space=pl.ANY),
        scratch_shapes=[pltpu.SemaphoreType.DMA, pltpu.SemaphoreType.DMA],
        compiler_params=pltpu.CompilerParams(collective_id=3, has_side_effects=True),
        name="general_spread",
    )(x)


def general_heads_kernel(x_ref, out_ref, send_sem, recv_sem):
    dp, ctx = lax.axis_index("dp"), lax.axis_index("ctx")
    share = share_of(dp, ctx)
    group, column = share // 8, lax.rem(share, 8)

    def sender(k):
        other = k // 8
        return (lax.rem(k, 8) * 8 + lax.rem(ctx - other + 8, 8), other)

    barrier = pltpu.get_barrier_semaphore()

    def greet(k, carry):
        peer = sender(k)

        @pl.when(jnp.logical_or(peer[0] != dp, peer[1] != ctx))
        def _():
            pl.semaphore_signal(barrier, inc=1, device_id=peer, device_id_type=MESH)

        return carry

    lax.fori_loop(0, N_DP, greet, 0)
    is_own = column == ctx

    @pl.when(is_own)
    def _():
        pl.semaphore_wait(barrier, N_DP - 1)

    @pl.when(jnp.logical_not(is_own))
    def _():
        pl.semaphore_wait(barrier, N_DP)

    def copy(k):
        peer = lax.rem(dp + k, N_DP)
        return pltpu.make_async_remote_copy(
            src_ref=x_ref.at[peer],
            dst_ref=out_ref.at[pl.ds(ctx * TILES_DEV, TILES_DEV), group],
            send_sem=send_sem,
            recv_sem=recv_sem,
            device_id=(peer, column),
            device_id_type=MESH,
        )

    def start(k, carry):
        copy(k).start()
        return carry

    def sent(k, carry):
        copy(k).wait_send()
        return carry

    lax.fori_loop(1, N_DP, start, 0)

    @pl.when(is_own)
    def _():
        pltpu.make_async_copy(
            x_ref.at[dp], out_ref.at[pl.ds(ctx * TILES_DEV, TILES_DEV), group], recv_sem
        ).start()

    @pl.when(jnp.logical_not(is_own))
    def _():
        copy(0).start()
        copy(0).wait_send()

    lax.fori_loop(1, N_DP, sent, 0)
    all_arrived(out_ref, recv_sem)


def general_heads(x):
    return pl.pallas_call(
        general_heads_kernel,
        out_shape=jax.ShapeDtypeStruct((N_CTX * TILES_DEV, TILE // ROWS, 3, ROWS, LANES), x.dtype),
        in_specs=[pl.BlockSpec(memory_space=pl.ANY)],
        out_specs=pl.BlockSpec(memory_space=pl.ANY),
        scratch_shapes=[pltpu.SemaphoreType.DMA, pltpu.SemaphoreType.DMA],
        compiler_params=pltpu.CompilerParams(collective_id=4, has_side_effects=True),
        name="general_heads",
    )(x)


def general_deliver_kernel(x_ref, mix_ref, out_ref, heads_ref, send_sem, recv_sem, mix_send, mix_recv):
    dp, ctx = lax.axis_index("dp"), lax.axis_index("ctx")
    share = share_of(dp, ctx)
    barrier = pltpu.get_barrier_semaphore()

    def greet_dp(k, carry):
        pl.semaphore_signal(
            barrier, inc=1, device_id=(lax.rem(dp + k, N_DP), ctx), device_id_type=MESH
        )
        return carry

    def greet_ctx(k, carry):
        pl.semaphore_signal(
            barrier, inc=1, device_id=(dp, lax.rem(ctx + k, N_CTX)), device_id_type=MESH
        )
        return carry

    lax.fori_loop(1, N_DP, greet_dp, 0)
    lax.fori_loop(1, N_CTX, greet_ctx, 0)
    pl.semaphore_wait(barrier, N_DP - 1 + N_CTX - 1)

    def mix_copy(k):
        peer = lax.rem(ctx + k, N_CTX)
        return pltpu.make_async_remote_copy(
            src_ref=mix_ref.at[peer],
            dst_ref=heads_ref.at[:, pl.ds(pl.multiple_of(ctx * LANES, LANES), LANES)],
            send_sem=mix_send,
            recv_sem=mix_recv,
            device_id=(dp, peer),
            device_id_type=MESH,
        )

    def copy(k):
        peer = lax.rem(dp + k, N_DP)
        return pltpu.make_async_remote_copy(
            src_ref=x_ref.at[peer],
            dst_ref=out_ref.at[share],
            send_sem=send_sem,
            recv_sem=recv_sem,
            device_id=(peer, ctx),
            device_id_type=MESH,
        )

    def start(k, carry):
        copy(k).start()
        return carry

    def sent(k, carry):
        copy(k).wait_send()
        return carry

    def mix_start(k, carry):
        mix_copy(k).start()
        return carry

    def mix_sent(k, carry):
        mix_copy(k).wait_send()
        return carry

    lax.fori_loop(1, N_DP, start, 0)
    lax.fori_loop(1, N_CTX, mix_start, 0)
    pltpu.make_async_copy(x_ref.at[dp], out_ref.at[share], recv_sem).start()
    pltpu.make_async_copy(
        mix_ref.at[ctx],
        heads_ref.at[:, pl.ds(pl.multiple_of(ctx * LANES, LANES), LANES)],
        mix_recv,
    ).start()
    lax.fori_loop(1, N_DP, sent, 0)
    lax.fori_loop(1, N_CTX, mix_sent, 0)
    all_arrived(out_ref, recv_sem)
    all_arrived(heads_ref, mix_recv)


def general_deliver(x, mix):
    rows = FRAMES // N_CTX
    return pl.pallas_call(
        general_deliver_kernel,
        out_shape=(
            jax.ShapeDtypeStruct(x.shape, x.dtype),
            jax.ShapeDtypeStruct((rows, N_CTX * LANES), x.dtype),
        ),
        in_specs=[pl.BlockSpec(memory_space=pl.ANY)] * 2,
        out_specs=[pl.BlockSpec(memory_space=pl.ANY)] * 2,
        scratch_shapes=[pltpu.SemaphoreType.DMA] * 4,
        compiler_params=pltpu.CompilerParams(collective_id=5, has_side_effects=True),
        name="general_deliver",
    )(x, mix)


def general_path(
    query_loader,
    key_loader,
    value_loader,
    conv_loader,
    slot_tile,
    lengths,
    conv_taps,
    norm_scale,
    norm_shift,
):
    qkv = jnp.stack([query_loader[0], key_loader[0], value_loader[0]])
    qkv = qkv.reshape(3, TILES_DEV, TILE // ROWS, ROWS, N_CTX, LANES)
    qkv = jnp.transpose(qkv, (2, 4, 1, 0, 3, 5)).reshape(N_DP, TILES_DEV * QKV, LANES)
    conv = conv_loader[0].reshape(TILES_DEV, N_DP, CONV_ROWS, LANES)
    conv = jnp.transpose(conv, (1, 0, 2, 3)).reshape(N_DP, TILES_DEV * CONV_ROWS, LANES)
    got = general_spread(jnp.concatenate([qkv, conv], axis=1))
    order = slot_tile[0]
    got_qkv = got[:, : TILES_DEV * QKV].reshape(N_DP * TILES_DEV, 3, ROWS, LANES)
    send_qkv = got_qkv[order].reshape(N_DP, TILES_DEV, 3, ROWS, LANES)
    got_conv = got[:, TILES_DEV * QKV :].reshape(N_DP * TILES_DEV, CONV_ROWS, LANES)
    send_conv = got_conv[order].reshape(N_DP, TILES_DEV * CONV_ROWS, LANES)
    heads = general_heads(send_qkv)
    flat = (FRAMES, LANES)
    mix = attend(lengths, *(heads[:, :, i].reshape(flat) for i in range(3)))
    signal, attention_out = general_deliver(send_conv, mix)
    signal = signal.reshape(N_DP, TILES_DEV, TILE // N_DP, CONV_ROWS // 2 * LANES)
    signal = jnp.transpose(signal, (1, 0, 2, 3)).reshape(TILES_DEV * TILE, CONV_ROWS // 2 * LANES)
    ends = N_CTX - 1
    halo = jnp.stack(
        [
            lax.ppermute(signal[COLUMN - 16 :], "ctx", [(i, i + 1) for i in range(ends)]),
            lax.ppermute(signal[:16], "ctx", [(i + 1, i) for i in range(ends)]),
        ]
    )
    conv_out = convolve(signal, halo, lengths, conv_taps, norm_scale, norm_shift)
    return attention_out[None], conv_out[None]


def on_device(*inputs):
    query, key, value, conv, slot_tile, lengths, conv_taps, norm_scale, norm_shift = inputs
    places = jnp.transpose(slot_tile[0].reshape(N_Z, 8))
    places = jnp.pad(places, ((0, 0), (0, LANES - N_Z)), constant_values=1 << 16)
    shape = (TILES_DEV, PLANE_DP, SEG_UNIT, HEADS * HEAD_DIM)
    held_q, lists = first(query.reshape(shape), places)
    table = route(lists.reshape(HELD, LANES))
    q, k, v, rows, halo = exchange(
        table,
        held_q,
        conv.reshape(TILES_DEV, N_CTX, 16, CHANNELS),
        key.reshape(shape),
        value.reshape(shape),
    )
    heads = (FRAMES, LANES)
    mix = attend(lengths, q.reshape(heads), k.reshape(heads), v.reshape(heads))
    attention_out = to_frames(mix)
    conv_out = convolve(
        rows.reshape(COLUMN, CHANNELS), halo, lengths, conv_taps, norm_scale, norm_shift
    )
    return lax.cond(
        table[AT_BAD] == 0,
        lambda: (attention_out[None], conv_out[None]),
        lambda: general_path(*inputs),
    )


def solution(mesh):
    return jax.shard_map(
        on_device,
        mesh=mesh,
        in_specs=(
            P("dp", "ctx", None),
            P("dp", "ctx", None),
            P("dp", "ctx", None),
            P("dp", "ctx", None),
            P("ctx", None),
            P("dp", None),
            P(),
            P(),
            P(),
        ),
        out_specs=(P("dp", "ctx", None), P("dp", "ctx", None)),
        check_vma=False,
    )
```

time: 312 us -> 249 us (0.80)
  Pallas kernels: 275 us -> 225 us
  local copies, waits for them, and re-layouts: 14 us -> 8.05 us
  starting transfers between devices: 5.28 us -> 0 us
    pallas_call x3 -> x4, Pallas kernels: 257 us -> 203 us  [the longest x1 155 us: exchange(): pl.pallas_call(exchange_kernel, out_shape=(heads, heads, heads, jax.Shape...]
    broadcast_in_dim x1 -> x0, other arithmetic: 10.2 us -> none  [on_device(): return (attention_out[None], conv_out[None])]
    convert_element_type x1 -> x2, other arithmetic: 0.23 us -> 10.2 us  [the longest x1 9.94 us: convolve(): return jax.nn.silu(norm_scale * conv_sum + norm_shift).astype(jnp.bfloat16)]
    ppermute x2 -> x0, starting transfers between devices: 5.28 us -> none  [the longest x1 3.99 us: with_halo(): lax.ppermute(tail, 'ctx', [(i, (i + 1) % N_CTX) for i in range(ends)])]
    pallas_call x1, Pallas kernels: 17.6 us -> 21.7 us  [attend(): pl.pallas_call(attend_kernel, grid_spec=pltpu.PrefetchScalarGridSpec(num_...]
    gather x2 -> x0, local copies, waits for them, and re-layouts: 3.49 us -> none  [the longest x1 1.91 us: on_device(): send_qkv = got_qkv[order].reshape(N_DP, TILES_DEV, 3, ROWS, LANES)]
  transfers between devices with their start and end apart: 2 -> 0, of which waited for: 1 -> 0; matrix products, arithmetic and copies ran while one was open for 0% -> 0% of each run, Pallas kernels for 0% -> 0%
where the time goes in v3:
time: 249 us; the launch traced here: 246 us
  Pallas kernels  225 us (90%)
  other arithmetic  12.1 us (5%)
  local copies, waits for them, and re-layouts  8.05 us (3%)
    pallas_call x1, Pallas kernels, exchange(): pl.pallas_call(exchange_kernel, out_shape=(heads, heads, heads, jax.Shape...  155 us
    pallas_call x1, Pallas kernels, attend(): pl.pallas_call(attend_kernel, grid_spec=pltpu.PrefetchScalarGridSpec(num_...  21.7 us
    pallas_call x1, Pallas kernels, first(): pl.pallas_call(first_kernel, out_shape=(jax.ShapeDtypeStruct((HELD, SEG_U...  19.7 us
    pallas_call x1, Pallas kernels, route(): pl.pallas_call(route_kernel, out_shape=jax.ShapeDtypeStruct((TABLE,), jnp...  18.7 us
    convert_element_type x1, other arithmetic, convolve(): return jax.nn.silu(norm_scale * conv_sum + norm_shift).astype(jnp.bfloat16)  9.94 us
    pallas_call x1, Pallas kernels, to_frames(): pl.pallas_call(mix_kernel, out_shape=jax.ShapeDtypeStruct((COLUMN, N_CTX...  9.23 us
    unnamed x18, local copies, waits for them, and re-layouts  5.51 us

profile of v3, /device:TPU:1, one launch (start us, length us, event | category | flops | bytes accessed | tf_op | source)
XLA Modules:
  0.0 246.2 jit_solution(16471298183528378899)
XLA Ops:
  0.6 0.5 broadcast.321
  1.2 1.3 reduce.127
  2.5 0.1 reshape_squeeze.3
  2.6 0.6 pad.4.list_ref
  3.2 19.7 %spread_queries.1 = (bf16[64,32,128]{2,1,0:T(8,128)(2,1)}, s32[8,8,128]{2,1,0:T(8,128)}) custom-call(bf16[2,4,32,1024]{3,2,1,0:T(8,128)(2,1)} %bitcast.63, s32[8,128]{1,0:T(8,128)} %pad.4.list_ref), custom_call_target="tpu_custom_call" | custom-call | tf_op jit(solution)/shard_map/spread_queries/pallas_call | solution.py:215
  23.0 18.7 %route.1.table = s32[256]{0:T(256)} custom-call(s32[64,128]{1,0:T(8,128)} %bitcast.67), custom_call_target="tpu_custom_call" | custom-call | tf_op jit(solution)/shard_map/route/pallas_call | solution.py:458
  41.7 1.3 slice.606
  43.6 1.0 copy-done.2
  44.6 0.7 copy-done.3
  45.3 155.2 %exchange.1 = (bf16[16,4,32,128]{3,2,1,0:T(8,128)(2,1)S(1)}, bf16[16,4,32,128]{3,2,1,0:T(8,128)(2,1)S(1)}, bf16[16,4,32,128]{3,2,1,0:T(8,128)(2,1)S(1)}, bf16[2,...) custom-call(s32[256]{0:T(256)S(1)} %copy-done.3, bf16[64,32,128]{2,1,0:T(8,128)(2,1)S(1)} %copy-done.2, ...), custom_call_target="tpu_custom_call" | custom-call | tf_op jit(solution)/shard_map/exchange/pallas_call | solution.py:619
  200.5 21.7 %attend.3.mix_ref = bf16[8,256,128]{2,1,0:T(8,128)(2,1)S(1)} custom-call(s32[1,4]{1,0:T(1,128)S(1)} %copy-done.12, bf16[2048,128]{1,0:T(8,128)(2,1)S(1)} %bitcast.49, bf16[2048,128]{1,0:T(8,128)(2,1)S(1)} %bitcast.50, bf16[2048,128]{1,0:T(8,128)(2,1)S(1)} %bitcast.51), custom_call_target="tpu_custom_call" | custom-call | flops 4294967296 | bytes 2097152 | tf_op jit(solution)/shard_map/attend/pallas_call | solution.py:740
  222.3 0.8 copy-done.1
  223.1 9.2 %to_frames.1 = bf16[256,1024]{1,0:T(8,128)(2,1)} custom-call(bf16[8,256,128]{2,1,0:T(8,128)(2,1)} %copy-done.1), custom_call_target="tpu_custom_call" | custom-call | tf_op jit(solution)/shard_map/to_frames/pallas_call | solution.py:663
  232.4 0.2 maximum_convert_fusion.1
  232.6 0.6 copy-done.8
  233.2 0.2 slice_reduce_fusion.60
  233.4 0.3 slice_reduce_fusion.61
  233.8 0.2 reduce-window.16
  233.9 0.1 convert_reduce_fusion.3
  234.0 0.1 convert_reduce_fusion.2
  234.1 0.1 slice_compare_fusion.61
  234.2 0.1 slice_compare_fusion.60
  234.3 9.9 %multiply_convert_fusion.1 = bf16[256,1536]{1,0:T(8,128)(2,1)} fusion(f32[286,1536]{1,0:T(8,128)S(1)} %maximum_convert_fusion.1, f32[1536]{0:T(1024)S(1)} %copy-done.10, f32[1536]{0:T(1024)S(1)} %get-tuple-element.116, f32[1536]{0:T(1024)S(1)} %get-tuple-element.117, f32[1536]{0:T(1024)S(1)} %get-tuple-element.88, f32[1536]{0:T(1024)S(1)} %get-tuple-element.89, ...), kind=kLoop, calls=%fused_computation.277 | loop fusion | flops 38928384 | bytes 49755904 | tf_op jit(solution)/shard_map/convert_element_type | solution.py:781
  244.3 1.9 copy.30
  (18 shorter events, 0.2 us)
Async XLA Ops:
  0.6 199.9 %copy-start.12 = (s32[1,4]{1,0:T(1,128)S(1)}, s32[1,4]{1,0:T(1,128)}, u32[]{:S(2)}) copy-start(s32[1,4]{1,0:T(1,128)} %len_ref.1) | copy-start | bytes 52
  43.6 1.0 copy-start.2
  44.6 0.7 copy-start.3
  222.3 0.8 copy-start.1
  232.3 0.9 copy-start.8
  232.4 2.0 copy-start.9
  232.4 2.0 copy-start.10
  234.3 10.0 %copy-start.4 = (bf16[1,256,1536]{2,1,0:T(8,128)(2,1)S(1)}, bf16[1,256,1536]{2,1,0:T(8,128)(2,1)}, u32[]{:S(2)}) copy-start(bf16[1,256,1536]{2,1,0:T(8,128)(2,1)} %param.14) | copy-start | bytes 2359300

commit v4 on v3

--- a/solution.py
+++ b/solution.py
@@ -642,7 +642,23 @@
     )(table, held_q, conv, k, v)
 
 
-def mix_kernel(mix_ref, heads_out, send, recv):
+EDGE = 16
+
+
+def last_kernel(
+    len_ref,
+    mix_ref,
+    rows_ref,
+    halo_ref,
+    taps_ref,
+    scale_ref,
+    shift_ref,
+    heads_out,
+    conv_out,
+    padded,
+    send,
+    recv,
+):
     z, row, ctx = place()
     dp = z * PLANE_DP + row
     repeat(1, N_CTX, lambda k: signal((dp, (ctx + k) % N_CTX)))
@@ -654,21 +670,83 @@
         return remote(mix_ref.at[to], mixed, send, recv, (dp, to))
 
     repeat(1, N_CTX, lambda k: copy(k).start())
-    pltpu.make_async_copy(mix_ref.at[ctx], mixed, recv).start()
+    own = pltpu.make_async_copy(mix_ref.at[ctx], mixed, recv)
+    own.start()
+
+    padded[pl.ds(0, EDGE), :] = halo_ref[0]
+    padded[pl.ds(EDGE, COLUMN), :] = rows_ref[...]
+    padded[pl.ds(EDGE + COLUMN, EDGE), :] = halo_ref[1]
+    ends = [jnp.int32(0), len_ref[0, 0]]
+    for i in range(1, 4):
+        ends.append(ends[-1] + len_ref[0, i])
+    window = SEG_UNIT + 2 * EDGE
+
+    def channels(group):
+        lanes = pl.ds(pl.multiple_of(group * LANES, LANES), LANES)
+        scale = scale_ref[:, lanes]
+        shift = shift_ref[:, lanes]
+
+        def unit(u):
+            place_ = ctx * UNITS + u
+            cut_before = jnp.bool_(False)
+            cut_after = jnp.bool_(False)
+            for end in ends:
+                cut_before = cut_before | (place_ == end)
+                cut_after = cut_after | (place_ + 1 == end)
+            frames = padded[pl.ds(pl.multiple_of(u * SEG_UNIT, SEG_UNIT), window), lanes]
+            frames = frames.astype(jnp.float32)
+            side = jnp.zeros((EDGE, LANES), jnp.float32)
+            frames = jnp.concatenate(
+                [
+                    jnp.where(cut_before, side, frames[:EDGE]),
+                    frames[EDGE : EDGE + SEG_UNIT],
+                    jnp.where(cut_after, side, frames[EDGE + SEG_UNIT :]),
+                ],
+                axis=0,
+            )
+            total = jnp.zeros((SEG_UNIT, LANES), jnp.float32)
+            for turn in range(8):
+                turned = pltpu.roll(frames, window - turn, 0) if turn else frames
+                for tap in range((turn - 1) % 8, KERNEL, 8):
+                    at = tap + 1 - turn
+                    total = total + taps_ref[pl.ds(tap, 1), lanes] * turned[at : at + SEG_UNIT]
+            value = scale * total + shift
+            value = value / (1.0 + jnp.exp(-value))
+            conv_out[pl.ds(pl.multiple_of(u * SEG_UNIT, SEG_UNIT), SEG_UNIT), lanes] = value.astype(
+                jnp.bfloat16
+            )
+
+        repeat(0, UNITS, unit)
+
+    repeat(0, CHANNELS // LANES, channels)
     repeat(1, N_CTX, lambda k: copy(k).wait_send())
     await_all(heads_out, recv)
 
 
-def to_frames(mix):
+def last(lengths, mix, rows, halo, taps, scale, shift):
+    vmem = pl.BlockSpec(memory_space=pltpu.VMEM)
+    anywhere = pl.BlockSpec(memory_space=pl.ANY)
     return pl.pallas_call(
-        mix_kernel,
-        out_shape=jax.ShapeDtypeStruct((COLUMN, N_CTX * LANES), mix.dtype),
-        in_specs=[pl.BlockSpec(memory_space=pl.ANY)],
-        out_specs=pl.BlockSpec(memory_space=pl.ANY),
-        scratch_shapes=[pltpu.SemaphoreType.DMA, pltpu.SemaphoreType.DMA],
-        compiler_params=pltpu.CompilerParams(collective_id=2, has_side_effects=True),
-        name="to_frames",
-    )(mix)
+        last_kernel,
+        out_shape=(
+            jax.ShapeDtypeStruct((COLUMN, N_CTX * LANES), mix.dtype),
+            jax.ShapeDtypeStruct((COLUMN, CHANNELS), mix.dtype),
+        ),
+        in_specs=[pl.BlockSpec(memory_space=pltpu.SMEM), anywhere] + [vmem] * 5,
+        out_specs=[anywhere, vmem],
+        scratch_shapes=[
+            pltpu.VMEM((COLUMN + 2 * EDGE, CHANNELS), mix.dtype),
+            pltpu.SemaphoreType.DMA,
+            pltpu.SemaphoreType.DMA,
+        ],
+        compiler_params=pltpu.CompilerParams(
+            collective_id=2, has_side_effects=True, vmem_limit_bytes=32 * 2**20
+        ),
+        name="convolve_and_return",
+    )(lengths, mix, rows, halo, taps, scale, shift)
+
+
+STEP = 2
 
 
 def attend_kernel(len_ref, q_ref, k_ref, v_ref, out_ref):
@@ -685,7 +763,8 @@
         high = jnp.where(end > last, jnp.minimum(high, end), high)
     per_key = KBLOCK // SEG_UNIT
     low_block = low // per_key
-    high_block = (high + per_key - 1) // per_key
+    steps = ((high + per_key - 1) // per_key - low_block + STEP - 1) // STEP
+    low_block = jnp.minimum(low_block, FRAMES // KBLOCK - STEP * steps)
 
     def segment(unit):
         seg = jnp.zeros(unit.shape, jnp.int32)
@@ -703,14 +782,15 @@
     row_seg = segment(first + lax.rem(row, QBLOCK) // SEG_UNIT)
     def step(index, carry):
         top, total, mixed = carry
-        part = pl.ds(pl.multiple_of(index * KBLOCK, KBLOCK), KBLOCK)
+        at = low_block + index * STEP
+        part = pl.ds(pl.multiple_of(at * KBLOCK, KBLOCK), STEP * KBLOCK)
         keys = k_ref[part, :]
         values = v_ref[part, :]
         scores = lax.dot_general(
             both, keys, (((1,), (1,)), ((), ())), preferred_element_type=jnp.float32
         )
-        col = lax.broadcasted_iota(jnp.int32, (1, KBLOCK), 1)
-        col_seg = segment(index * per_key + col // SEG_UNIT)
+        col = lax.broadcasted_iota(jnp.int32, (1, STEP * KBLOCK), 1)
+        col_seg = segment(at * per_key + col // SEG_UNIT)
         scores = jnp.where(row_seg == col_seg, scores, -2e30)
         new_top = jnp.maximum(top, jnp.max(scores, axis=1, keepdims=True))
         weights = jnp.exp(scores - new_top)
@@ -722,8 +802,8 @@
         return new_top, total, mixed
 
     top, total, mixed = lax.fori_loop(
-        low_block,
-        high_block,
+        0,
+        steps,
         step,
         (
             jnp.full((2 * QBLOCK, 1), -1e30, jnp.float32),
@@ -1066,9 +1146,14 @@
     )
     heads = (FRAMES, LANES)
     mix = attend(lengths, q.reshape(heads), k.reshape(heads), v.reshape(heads))
-    attention_out = to_frames(mix)
-    conv_out = convolve(
-        rows.reshape(COLUMN, CHANNELS), halo, lengths, conv_taps, norm_scale, norm_shift
+    attention_out, conv_out = last(
+        lengths,
+        mix,
+        rows.reshape(COLUMN, CHANNELS),
+        halo,
+        conv_taps,
+        norm_scale.reshape(1, CHANNELS),
+        norm_shift.reshape(1, CHANNELS),
     )
     return lax.cond(
         table[AT_BAD] == 0,

time: 249 us -> 236 us (0.948)
  other arithmetic: 12.1 us -> 1.32 us
  Pallas kernels: 225 us -> 221 us
    convert_element_type x2 -> x0, other arithmetic: 10.2 us -> none  [the longest x1 9.94 us: convolve(): return jax.nn.silu(norm_scale * conv_sum + norm_shift).astype(jnp.bfloat16)]
    pallas_call x1, Pallas kernels: 21.7 us -> 12.5 us  [attend(): pl.pallas_call(attend_kernel, grid_spec=pltpu.PrefetchScalarGridSpec(num_...]
    pallas_call x1, Pallas kernels: 9.23 us -> 13.5 us  [last(): pl.pallas_call(last_kernel, out_shape=(jax.ShapeDtypeStruct((COLUMN, N_CT...]
    unnamed x18 -> x27, local copies, waits for them, and re-layouts: 5.51 us -> 5.11 us
where the time goes in v4:
time: 236 us; the launch traced here: 231 us
  Pallas kernels  221 us (94%)
  local copies, waits for them, and re-layouts  7.14 us (3%)
    pallas_call x1, Pallas kernels, exchange(): pl.pallas_call(exchange_kernel, out_shape=(heads, heads, heads, jax.Shape...  155 us
    pallas_call x1, Pallas kernels, route(): pl.pallas_call(route_kernel, out_shape=jax.ShapeDtypeStruct((TABLE,), jnp...  20.2 us
    pallas_call x1, Pallas kernels, first(): pl.pallas_call(first_kernel, out_shape=(jax.ShapeDtypeStruct((HELD, SEG_U...  19.7 us
    pallas_call x1, Pallas kernels, last(): pl.pallas_call(last_kernel, out_shape=(jax.ShapeDtypeStruct((COLUMN, N_CT...  13.5 us
    pallas_call x1, Pallas kernels, attend(): pl.pallas_call(attend_kernel, grid_spec=pltpu.PrefetchScalarGridSpec(num_...  12.5 us
    unnamed x27, local copies, waits for them, and re-layouts  5.11 us

profile of v4, /device:TPU:1, one launch (start us, length us, event | category | flops | bytes accessed | tf_op | source)
XLA Modules:
  0.0 231.4 jit_solution(10649855831953309566)
XLA Ops:
  0.6 0.5 broadcast.173
  1.2 1.3 reduce.65
  2.5 0.1 reshape_squeeze.3
  2.6 0.1 copy.22
  2.6 0.6 pad.4.list_ref
  3.2 19.7 %spread_queries.1 = (bf16[64,32,128]{2,1,0:T(8,128)(2,1)}, s32[8,8,128]{2,1,0:T(8,128)}) custom-call(bf16[2,4,32,1024]{3,2,1,0:T(8,128)(2,1)} %bitcast.56, s32[8,128]{1,0:T(8,128)} %pad.4.list_ref), custom_call_target="tpu_custom_call" | custom-call | tf_op jit(solution)/shard_map/spread_queries/pallas_call | solution.py:215
  23.0 20.2 %route.1.table = s32[256]{0:T(256)} custom-call(s32[64,128]{1,0:T(8,128)} %bitcast.61), custom_call_target="tpu_custom_call" | custom-call | tf_op jit(solution)/shard_map/route/pallas_call | solution.py:458
  43.2 1.3 slice.309
  45.1 1.0 copy-done.1
  46.2 0.7 copy-done.2
  46.9 155.2 %exchange.1 = (bf16[16,4,32,128]{3,2,1,0:T(8,128)(2,1)S(1)}, bf16[16,4,32,128]{3,2,1,0:T(8,128)(2,1)S(1)}, bf16[16,4,32,128]{3,2,1,0:T(8,128)(2,1)S(1)}, bf16[2,...) custom-call(s32[256]{0:T(256)S(1)} %copy-done.2, bf16[64,32,128]{2,1,0:T(8,128)(2,1)S(1)} %copy-done.1, ...), custom_call_target="tpu_custom_call" | custom-call | tf_op jit(solution)/shard_map/exchange/pallas_call | solution.py:619
  202.1 0.0 copy-start.9
  202.1 0.0 copy-start.10
  202.1 0.0 copy-start.3
  202.1 0.0 copy-start.4
  202.1 0.0 copy-start.5
  202.2 0.0 copy-start.6
  202.2 0.0 copy-start.8
  202.2 0.0 copy-start.12
  202.2 12.5 %attend.3.mix_ref = bf16[8,256,128]{2,1,0:T(8,128)(2,1)S(1)} custom-call(s32[1,4]{1,0:T(1,128)S(1)} %copy-done.11, bf16[2048,128]{1,0:T(8,128)(2,1)S(1)} %bitcast.43, bf16[2048,128]{1,0:T(8,128)(2,1)S(1)} %bitcast.44, bf16[2048,128]{1,0:T(8,128)(2,1)S(1)} %bitcast.45), custom_call_target="tpu_custom_call" | custom-call | flops 4294967296 | bytes 2097152 | tf_op jit(solution)/shard_map/attend/pallas_call | solution.py:820
  214.8 13.5 %convolve_and_return.1 = (bf16[256,1024]{1,0:T(8,128)(2,1)}, bf16[256,1536]{1,0:T(8,128)(2,1)}) custom-call(s32[1,4]{1,0:T(1,128)S(1)} %copy-done.11, bf16[8,256,128]{2,1,0:T(8,128)(2,1)S(1)} %attend.3.mix_ref, bf16[256,1536]{1,0:T(8,128)(2,1)S(1)} %bitcast.39, bf16[2,16,1536]{2,1,0:T(8,128)(2,1)S(1)} %get-tuple-element.50.halo_ref, ...), custom_call_target="tpu_custom_call" | custom-call | tf_op jit(solution)/shard_map/convolve_and_return/pallas_call | solution.py:729
  228.3 0.2 conditional.1
  228.6 1.9 copy.30
  230.5 0.9 copy.31
  (16 shorter events, 0.0 us)
Async XLA Ops:
  0.6 201.5 %copy-start.11 = (s32[1,4]{1,0:T(1,128)S(1)}, s32[1,4]{1,0:T(1,128)}, u32[]{:S(2)}) copy-start(s32[1,4]{1,0:T(1,128)} %len_ref.3) | copy-start | bytes 52
  45.1 1.0 copy-start.1
  46.2 0.7 copy-start.2
  202.1 12.6 %copy-start.9 = (f32[1536]{0:T(1024)S(1)}, f32[1536]{0:T(1024)}, u32[]{:S(2)}) copy-start(f32[1536]{0:T(1024)} %param.18) | copy-start | bytes 18436
  202.1 12.6 %copy-start.10 = (f32[1536]{0:T(1024)S(1)}, f32[1536]{0:T(1024)}, u32[]{:S(2)}) copy-start(f32[1536]{0:T(1024)} %param.19) | copy-start | bytes 18436
  202.1 12.6 %copy-start.3 = (bf16[1,256,1536]{2,1,0:T(8,128)(2,1)S(1)}, bf16[1,256,1536]{2,1,0:T(8,128)(2,1)}, u32[]{:S(2)}) copy-start(bf16[1,256,1536]{2,1,0:T(8,128)(2,1)} %param.14) | copy-start | bytes 2359300
  202.1 12.6 %copy-start.4 = (bf16[1,256,1024]{2,1,0:T(8,128)(2,1)S(1)}, bf16[1,256,1024]{2,1,0:T(8,128)(2,1)}, u32[]{:S(2)}) copy-start(bf16[1,256,1024]{2,1,0:T(8,128)(2,1)} %param.11) | copy-start | bytes 1572868
  202.1 12.6 %copy-start.5 = (bf16[1,256,1024]{2,1,0:T(8,128)(2,1)S(1)}, bf16[1,256,1024]{2,1,0:T(8,128)(2,1)}, u32[]{:S(2)}) copy-start(bf16[1,256,1024]{2,1,0:T(8,128)(2,1)} %param.12) | copy-start | bytes 1572868
  202.2 12.6 %copy-start.6 = (bf16[1,256,1024]{2,1,0:T(8,128)(2,1)S(1)}, bf16[1,256,1024]{2,1,0:T(8,128)(2,1)}, u32[]{:S(2)}) copy-start(bf16[1,256,1024]{2,1,0:T(8,128)(2,1)} %param.13) | copy-start | bytes 1572868
  202.2 12.6 %copy-start.8 = (f32[31,1536]{1,0:T(8,128)S(1)}, f32[31,1536]{1,0:T(8,128)}, u32[]{:S(2)}) copy-start(f32[31,1536]{1,0:T(8,128)} %taps_ref.1) | copy-start | bytes 571396
  202.2 12.6 %copy-start.12 = (s32[1,128]{1,0:T(1,128)S(1)}, s32[1,128]{1,0:T(1,128)}, u32[]{:S(2)}) copy-start(s32[1,128]{1,0:T(1,128)} %param.15) | copy-start | bytes 1540
  228.6 2.0 copy-start.7

commit v5 on v4

--- a/solution.py
+++ b/solution.py
@@ -21,6 +21,7 @@
 ROWS = 16
 QKV = 3 * ROWS
 CONV_ROWS = 24
+KEYS = 512
 QBLOCK = 256
 KBLOCK = 256
 UNITS = QBLOCK // SEG_UNIT
@@ -186,10 +187,6 @@
 
 
 WIDE = CHANNELS // PLANE_DP
-
-
-def conv_piece(ref):
-    return lambda row, ctx: ref.at[:, ctx, :, pl.ds(pl.multiple_of(row * WIDE, LANES), WIDE)]
 
 
 def first_kernel(q_ref, list_ref, held_ref, lists_ref, send, recv, list_send, list_recv):
@@ -467,30 +464,44 @@
     )(lists)
 
 
+PARTS = ((0, 128), (128, 128), (256, 128))
+ARRAYS = 3 + len(PARTS)
+
+
+def conv_lanes(row, part):
+    first, width = PARTS[part]
+    return pl.ds(pl.multiple_of(row * WIDE + first, LANES), width)
+
+
+def conv_piece(ref, part):
+    return lambda row, ctx: ref.at[:, ctx, :, conv_lanes(row, part)]
+
+
 def exchange_kernel(
-    table, held_q, conv_ref, k_ref, v_ref, q_out, k_out, v_out, rows_out, halo_out, *scratch
+    table, lengths, held_q, k_ref, v_ref, conv_ref, heads_out, rows_out, halo_out, *scratch
 ):
     z, row, ctx = place()
+    dp = z * PLANE_DP + row
     repeat(1, PLANE, lambda k: signal(plane_peer(z, row, ctx, k)[2]))
     repeat(0, SHIFTS, lambda j: signal(z_peer(z, row, ctx, j)))
     pl.semaphore_wait(pltpu.get_barrier_semaphore(), PLANE - 1 + SHIFTS)
-    held = (held_q,) + scratch[:3]
+    held = (held_q,) + scratch[: ARRAYS - 1]
     main_staged, main_got, extra_staged, extra_got, staged = (
-        scratch[3 + 4 * i : 7 + 4 * i] for i in range(5)
+        scratch[ARRAYS * (i + 1) - 1 : ARRAYS * (i + 2) - 1] for i in range(5)
     )
-    sems, halo_sems = scratch[23:]
-    outs = (q_out, rows_out, k_out, v_out)
-    pieces = (None, conv_piece(conv_ref), head_piece(k_ref), head_piece(v_ref))
+    group = scratch[6 * ARRAYS - 1 : 6 * ARRAYS + 2]
+    mixture, sems, halo_sems, mix_sems = scratch[6 * ARRAYS + 2 :]
+    pieces = [None, head_piece(k_ref), head_piece(v_ref)] + [conv_piece(conv_ref, i) for i in range(len(PARTS))]
     spread = [None] + [
-        Spread(pieces[i], held[i], sems.at[0, i], sems.at[1, i]) for i in range(1, 4)
+        Spread(pieces[i], held[i], sems.at[0, i], sems.at[1, i]) for i in range(1, ARRAYS)
     ]
     main = [
         Along(MAIN_GROUPS, main_staged[i], main_got[i], sems.at[2, i], sems.at[3, i])
-        for i in range(4)
+        for i in range(ARRAYS)
     ]
     extra = [
         Along(EXTRA_GROUPS, extra_staged[i], extra_got[i], sems.at[4, i], sems.at[5, i])
-        for i in range(4)
+        for i in range(ARRAYS)
     ]
 
     def start_main(i):
@@ -508,32 +519,31 @@
         to = (row + k) % PLANE_DP
         return remote(
             staged[i].at[pl.ds(to * 16, 16)],
-            outs[i].at[:, row],
+            group[i].at[:, row],
             sems.at[6, i],
             sems.at[7, i],
             (z * PLANE_DP + to, ctx),
         )
 
-    channels = pl.ds(pl.multiple_of(row * WIDE, LANES), WIDE)
-
-    def part(to_row, to_ctx):
-        return staged[1].at[pl.ds(to_row * 16 + to_ctx * TILES_DEV, TILES_DEV)]
-
-    def conv_copy(k):
+    def part(i, to_row, to_ctx):
+        return staged[i].at[pl.ds(to_row * 16 + to_ctx * TILES_DEV, TILES_DEV)]
+
+    def rows_part(i):
+        return rows_out.at[:, ctx, :, conv_lanes(row, i - 3)]
+
+    def conv_copy(i, k):
         to_row, to_ctx, device = plane_peer(z, row, ctx, k)
-        return remote(
-            part(to_row, to_ctx), rows_out.at[:, ctx, :, channels], sems.at[6, 1], sems.at[7, 1], device
-        )
-
-    def halo(side, act):
+        return remote(part(i, to_row, to_ctx), rows_part(i), sems.at[6, i], sems.at[7, 3], device)
+
+    def halo(i, side, act):
         step, tile = (1, 1) if side == 0 else (-1, 0)
 
         def one(k):
             to_row = k // (N_CTX - 1)
             column = k % (N_CTX - 1) + (0 if side == 0 else 1)
             target = column + step
-            src = staged[1].at[to_row * 16 + column * TILES_DEV + tile]
-            dst = halo_out.at[side, :, channels]
+            src = staged[i].at[to_row * 16 + column * TILES_DEV + tile]
+            dst = halo_out.at[side, :, conv_lanes(row, i - 3)]
             is_own = (to_row == row) & (target == ctx)
 
             @pl.when(is_own)
@@ -558,45 +568,138 @@
     def start_final(i):
         extra[i].arrived()
         stage_final(table, held[i], main_got[i], extra_got[i], staged[i])
-        if i == 1:
-            repeat(1, PLANE, lambda k: conv_copy(k).start())
-            pltpu.make_async_copy(
-                part(row, ctx), rows_out.at[:, ctx, :, channels], sems.at[7, 1]
-            ).start()
-            halo(0, "start")
-            halo(1, "start")
+        if i >= 3:
+            repeat(1, PLANE, lambda k: conv_copy(i, k).start())
+            pltpu.make_async_copy(part(i, row, ctx), rows_part(i), sems.at[7, 3]).start()
+            halo(i, 0, "start")
+            halo(i, 1, "start")
         else:
             repeat(1, PLANE_DP, lambda k: head_copy(i, k).start())
             pltpu.make_async_copy(
-                staged[i].at[pl.ds(row * 16, 16)], outs[i].at[:, row], sems.at[7, i]
+                staged[i].at[pl.ds(row * 16, 16)], group[i].at[:, row], sems.at[7, i]
             ).start()
+
+    ends = [lengths[0, 0]]
+    for i in range(1, 3):
+        ends.append(ends[-1] + lengths[0, i])
+
+    def segment(unit):
+        seg = jnp.zeros(unit.shape, jnp.int32)
+        for end in ends:
+            seg = seg + (unit >= end).astype(jnp.int32)
+        return seg
+
+    mixed_at = heads_out.at[:, pl.ds(pl.multiple_of(ctx * LANES, LANES), LANES)]
+
+    def mix_copy(block):
+        return remote(mixture.at[block], mixed_at, mix_sems.at[0], mix_sems.at[1], (dp, block))
+
+    lane = lax.broadcasted_iota(jnp.int32, (QBLOCK, LANES), 1)
+    query = lax.broadcasted_iota(jnp.int32, (2 * QBLOCK, 1), 0) % QBLOCK
+    key = lax.broadcasted_iota(jnp.int32, (1, KEYS), 1)
+
+    def attend_block(block, first_key, steps):
+        queries = group[0][pl.ds(block * TILES_DEV, TILES_DEV)].reshape(QBLOCK, LANES) * 0.125
+        zero = jnp.zeros_like(queries)
+        both = jnp.concatenate(
+            [jnp.where(lane < HEAD_DIM, queries, zero), jnp.where(lane < HEAD_DIM, zero, queries)],
+            axis=0,
+        )
+        query_seg = segment(block * UNITS + query // SEG_UNIT)
+
+        def step(index, carry):
+            top, total, mixed = carry
+            at = first_key + index * KEYS
+            tiles = pl.ds(first_key // TILE + index * (KEYS // TILE), KEYS // TILE)
+            keys = group[1][tiles].reshape(KEYS, LANES)
+            values = group[2][tiles].reshape(KEYS, LANES)
+            scores = lax.dot_general(
+                both, keys, (((1,), (1,)), ((), ())), preferred_element_type=jnp.float32
+            )
+            key_seg = segment((at + key) // SEG_UNIT)
+            scores = jnp.where(query_seg == key_seg, scores, -2e30)
+            new_top = jnp.maximum(top, jnp.max(scores, axis=1, keepdims=True))
+            weights = jnp.exp(scores - new_top)
+            scale = jnp.exp(top - new_top)
+            total = total * scale + jnp.sum(weights, axis=1, keepdims=True)
+            mixed = mixed * scale + jnp.dot(
+                weights.astype(jnp.bfloat16), values, preferred_element_type=jnp.float32
+            )
+            return new_top, total, mixed
+
+        _, total, mixed = lax.fori_loop(
+            0,
+            steps,
+            step,
+            (
+                jnp.full((2 * QBLOCK, 1), -1e30, jnp.float32),
+                jnp.zeros((2 * QBLOCK, 1), jnp.float32),
+                jnp.zeros((2 * QBLOCK, LANES), jnp.float32),
+            ),
+        )
+        mixed = mixed / total
+        mixture[block] = jnp.where(lane < HEAD_DIM, mixed[:QBLOCK], mixed[QBLOCK:]).astype(jnp.bfloat16)
+
+        @pl.when(block == ctx)
+        def _():
+            pltpu.make_async_copy(mixture.at[block], mixed_at, mix_sems.at[1]).start()
+
+        @pl.when(block != ctx)
+        def _():
+            mix_copy(block).start()
+
+    def attend_blocks(first, last, first_key, steps):
+        repeat(first, last, lambda block: attend_block(block, first_key, steps))
 
     spread[1].start()
     start_main(0)
     spread[2].start()
     start_main(1)
     spread[3].start()
+    spread[4].start()
+    spread[5].start()
     start_extra(0)
     start_main(2)
     start_extra(1)
     start_final(0)
     start_main(3)
     start_extra(2)
+    start_main(4)
+    start_main(5)
     start_final(1)
+    start_final(2)
+    for i in range(3):
+        await_all(group[i], sems.at[7, i])
+    attend_blocks(0, 2, 0, 3)
     start_extra(3)
-    start_final(2)
+    attend_blocks(2, 4, 0, 4)
     start_final(3)
-    halo(0, "sent")
-    halo(1, "sent")
-    repeat(1, PLANE, lambda k: conv_copy(k).wait_send())
-    for i in range(4):
+    start_extra(4)
+    attend_blocks(4, 6, 0, 4)
+    start_final(4)
+    start_extra(5)
+    attend_blocks(6, 8, FRAMES - 3 * KEYS, 3)
+    start_final(5)
+    for i in range(ARRAYS):
         if i:
             spread[i].sent()
         main[i].sent()
         extra[i].sent()
-        if i != 1:
+        if i < 3:
             repeat(1, PLANE_DP, lambda k: head_copy(i, k).wait_send())
-        await_all(outs[i], sems.at[7, i])
+        else:
+            repeat(1, PLANE, lambda k: conv_copy(i, k).wait_send())
+            halo(i, 0, "sent")
+            halo(i, 1, "sent")
+
+    def mix_sent(block):
+        @pl.when(block != ctx)
+        def _():
+            mix_copy(block).wait_send()
+
+    repeat(0, N_CTX, mix_sent)
+    await_all(heads_out, mix_sems.at[1])
+    await_all(rows_out, sems.at[7, 3])
 
     @pl.when(ctx > 0)
     def _():
@@ -607,72 +710,58 @@
         await_all(halo_out.at[1], halo_sems.at[1])
 
 
-def exchange(table, held_q, conv, k, v):
+def exchange(table, lengths, held_q, k, v, conv):
     unit = (SEG_UNIT, LANES)
-    conv_unit = (16, WIDE)
     kind = held_q.dtype
 
     def buffers(count):
-        return [pltpu.VMEM((count,) + (conv_unit if i == 1 else unit), kind) for i in range(4)]
-
-    heads = jax.ShapeDtypeStruct((N_CTX * TILES_DEV, PLANE_DP) + unit, kind)
+        return [pltpu.VMEM((count,) + (unit if i < 3 else (16, PARTS[i - 3][1])), kind) for i in range(ARRAYS)]
+
+    smem = pl.BlockSpec(memory_space=pltpu.SMEM)
     return pl.pallas_call(
         exchange_kernel,
         out_shape=(
-            heads,
-            heads,
-            heads,
+            jax.ShapeDtypeStruct((COLUMN, N_CTX * LANES), kind),
             jax.ShapeDtypeStruct((TILES_DEV, N_CTX, 16, CHANNELS), kind),
             jax.ShapeDtypeStruct((2, 16, CHANNELS), kind),
         ),
-        in_specs=[pl.BlockSpec(memory_space=pltpu.SMEM), pl.BlockSpec(memory_space=pltpu.VMEM)]
+        in_specs=[smem, smem, pl.BlockSpec(memory_space=pltpu.VMEM)]
         + [pl.BlockSpec(memory_space=pl.ANY)] * 3,
-        out_specs=[pl.BlockSpec(memory_space=pl.ANY)] * 5,
+        out_specs=[pl.BlockSpec(memory_space=pl.ANY)] * 3,
         scratch_shapes=buffers(HELD)[1:]
         + buffers(MAIN)
         + buffers(MAIN)
         + buffers(EXTRA)
         + buffers(EXTRA)
         + buffers(HELD)
-        + [pltpu.SemaphoreType.DMA((8, 4)), pltpu.SemaphoreType.DMA((3,))],
+        + [pltpu.VMEM((N_CTX * TILES_DEV, PLANE_DP) + unit, kind)] * 3
+        + [
+            pltpu.VMEM((N_CTX, COLUMN, LANES), kind),
+            pltpu.SemaphoreType.DMA((8, ARRAYS)),
+            pltpu.SemaphoreType.DMA((3,)),
+            pltpu.SemaphoreType.DMA((2,)),
+        ],
         compiler_params=pltpu.CompilerParams(
-            collective_id=1, has_side_effects=True, vmem_limit_bytes=40 * 2**20
+            collective_id=1, has_side_effects=True, vmem_limit_bytes=48 * 2**20
         ),
         name="exchange",
-    )(table, held_q, conv, k, v)
+    )(table, lengths, held_q, k, v, conv)
 
 
 EDGE = 16
 
 
-def last_kernel(
+def convolve_kernel(
     len_ref,
-    mix_ref,
     rows_ref,
     halo_ref,
     taps_ref,
     scale_ref,
     shift_ref,
-    heads_out,
     conv_out,
     padded,
-    send,
-    recv,
 ):
-    z, row, ctx = place()
-    dp = z * PLANE_DP + row
-    repeat(1, N_CTX, lambda k: signal((dp, (ctx + k) % N_CTX)))
-    pl.semaphore_wait(pltpu.get_barrier_semaphore(), N_CTX - 1)
-    mixed = heads_out.at[:, pl.ds(pl.multiple_of(ctx * LANES, LANES), LANES)]
-
-    def copy(k):
-        to = (ctx + k) % N_CTX
-        return remote(mix_ref.at[to], mixed, send, recv, (dp, to))
-
-    repeat(1, N_CTX, lambda k: copy(k).start())
-    own = pltpu.make_async_copy(mix_ref.at[ctx], mixed, recv)
-    own.start()
-
+    ctx = lax.axis_index("ctx")
     padded[pl.ds(0, EDGE), :] = halo_ref[0]
     padded[pl.ds(EDGE, COLUMN), :] = rows_ref[...]
     padded[pl.ds(EDGE + COLUMN, EDGE), :] = halo_ref[1]
@@ -719,31 +808,19 @@
         repeat(0, UNITS, unit)
 
     repeat(0, CHANNELS // LANES, channels)
-    repeat(1, N_CTX, lambda k: copy(k).wait_send())
-    await_all(heads_out, recv)
-
-
-def last(lengths, mix, rows, halo, taps, scale, shift):
+
+
+def convolve_column(lengths, rows, halo, taps, scale, shift):
     vmem = pl.BlockSpec(memory_space=pltpu.VMEM)
-    anywhere = pl.BlockSpec(memory_space=pl.ANY)
     return pl.pallas_call(
-        last_kernel,
-        out_shape=(
-            jax.ShapeDtypeStruct((COLUMN, N_CTX * LANES), mix.dtype),
-            jax.ShapeDtypeStruct((COLUMN, CHANNELS), mix.dtype),
-        ),
-        in_specs=[pl.BlockSpec(memory_space=pltpu.SMEM), anywhere] + [vmem] * 5,
-        out_specs=[anywhere, vmem],
-        scratch_shapes=[
-            pltpu.VMEM((COLUMN + 2 * EDGE, CHANNELS), mix.dtype),
-            pltpu.SemaphoreType.DMA,
-            pltpu.SemaphoreType.DMA,
-        ],
-        compiler_params=pltpu.CompilerParams(
-            collective_id=2, has_side_effects=True, vmem_limit_bytes=32 * 2**20
-        ),
-        name="convolve_and_return",
-    )(lengths, mix, rows, halo, taps, scale, shift)
+        convolve_kernel,
+        out_shape=jax.ShapeDtypeStruct((COLUMN, CHANNELS), rows.dtype),
+        in_specs=[pl.BlockSpec(memory_space=pltpu.SMEM)] + [vmem] * 5,
+        out_specs=vmem,
+        scratch_shapes=[pltpu.VMEM((COLUMN + 2 * EDGE, CHANNELS), rows.dtype)],
+        compiler_params=pltpu.CompilerParams(vmem_limit_bytes=32 * 2**20),
+        name="convolve",
+    )(lengths, rows, halo, taps, scale, shift)
 
 
 STEP = 2
@@ -1137,18 +1214,16 @@
     shape = (TILES_DEV, PLANE_DP, SEG_UNIT, HEADS * HEAD_DIM)
     held_q, lists = first(query.reshape(shape), places)
     table = route(lists.reshape(HELD, LANES))
-    q, k, v, rows, halo = exchange(
+    attention_out, rows, halo = exchange(
         table,
+        lengths,
         held_q,
-        conv.reshape(TILES_DEV, N_CTX, 16, CHANNELS),
         key.reshape(shape),
         value.reshape(shape),
+        conv.reshape(TILES_DEV, N_CTX, 16, CHANNELS),
     )
-    heads = (FRAMES, LANES)
-    mix = attend(lengths, q.reshape(heads), k.reshape(heads), v.reshape(heads))
-    attention_out, conv_out = last(
+    conv_out = convolve_column(
         lengths,
-        mix,
         rows.reshape(COLUMN, CHANNELS),
         halo,
         conv_taps,

time: 236 us -> 225 us (0.953); the launches traced: 231 us -> 225 us
  Pallas kernels: 221 us -> 216 us
    pallas_call x3 -> x2, Pallas kernels: 181 us -> 177 us  [the longest x1 168 us: exchange(): pl.pallas_call(exchange_kernel, out_shape=(jax.ShapeDtypeStruct((COLUMN,...]
    unnamed x27 -> x24, local copies, waits for them, and re-layouts: 5.11 us -> 4.14 us
where the time goes in v5:
time: 225 us
  Pallas kernels  216 us (96%)
  local copies, waits for them, and re-layouts  6.17 us (3%)
    pallas_call x1, Pallas kernels, exchange(): pl.pallas_call(exchange_kernel, out_shape=(jax.ShapeDtypeStruct((COLUMN,...  168 us
    pallas_call x1, Pallas kernels, first(): pl.pallas_call(first_kernel, out_shape=(jax.ShapeDtypeStruct((HELD, SEG_U...  19.7 us
    pallas_call x1, Pallas kernels, route(): pl.pallas_call(route_kernel, out_shape=jax.ShapeDtypeStruct((TABLE,), jnp...  19.4 us
    pallas_call x1, Pallas kernels, convolve_column(): pl.pallas_call(convolve_kernel, out_shape=jax.ShapeDtypeStruct((COLUMN, C...  9.11 us

profile of v5, /device:TPU:1, one launch (start us, length us, event | category | flops | bytes accessed | tf_op | source)
XLA Modules:
  0.0 225.0 jit_solution(3754227494494161682)
XLA Ops:
  0.6 0.0 copy-start.10
  0.6 0.0 copy-start.8
  0.7 0.0 copy-start.7
  0.7 0.0 copy-start.9
  0.7 0.5 broadcast.173
  1.2 1.3 reduce.65
  2.5 0.1 reshape_squeeze.3
  2.6 0.1 copy.22
  2.7 0.6 pad.4.list_ref
  3.3 19.7 %spread_queries.1 = (bf16[64,32,128]{2,1,0:T(8,128)(2,1)}, s32[8,8,128]{2,1,0:T(8,128)}) custom-call(bf16[2,4,32,1024]{3,2,1,0:T(8,128)(2,1)} %bitcast.52, s32[8,128]{1,0:T(8,128)} %pad.4.list_ref), custom_call_target="tpu_custom_call" | custom-call | tf_op jit(solution)/shard_map/spread_queries/pallas_call | solution.py:212
  23.0 19.4 %route.1.table = s32[256]{0:T(256)} custom-call(s32[64,128]{1,0:T(8,128)} %bitcast.55), custom_call_target="tpu_custom_call" | custom-call | tf_op jit(solution)/shard_map/route/pallas_call | solution.py:455
  42.4 1.3 slice.309
  44.3 0.0 copy-start
  44.3 1.0 copy-done
  45.3 0.7 copy-done.2
  46.0 0.0 copy-start.11
  46.0 167.7 %exchange.1 = (bf16[256,1024]{1,0:T(8,128)(2,1)}, bf16[2,8,16,1536]{3,2,1,0:T(8,128)(2,1)S(1)}, bf16[2,16,1536]{2,1,0:T(8,128)(2,1)S(1)}) custom-call(s32[256]{0:T(256)S(1)} %copy-done.2, s32[1,4]{1,0:T(1,128)} %len_ref.1, bf16[64,32,128]{2,1,0:T(8,128)(2,1)S(1)} %copy-done, bf16[2,4,32,1024]{3,2,1,0:T(8,128)(2,1)} %bitcast.50, ...), custom_call_target="tpu_custom_call" | custom-call | tf_op jit(solution)/shard_map/exchange/pallas_call | solution.py:721
  213.7 0.0 copy-done.8
  213.7 0.0 copy-done.9
  213.8 0.0 copy-done.10
  213.8 9.1 %convolve.1 = bf16[256,1536]{1,0:T(8,128)(2,1)} custom-call(s32[1,4]{1,0:T(1,128)S(1)} %copy-done.10, bf16[256,1536]{1,0:T(8,128)(2,1)S(1)} %bitcast.36, bf16[2,16,1536]{2,1,0:T(8,128)(2,1)S(1)} %get-tuple-element.46.halo_ref, f32[31,1536]{1,0:T(8,128)S(1)} %copy-done.7, f32[1,1536]{1,0:T(1,128)S(1)} %reshape.188.scale_ref, f32[1,1536]{1,0:T(1,128)S(1)} %reshape.189.shift_ref), custom_call_target="tpu_custom_call" | custom-call | tf_op jit(solution)/shard_map/convolve/pallas_call | solution.py:815
  222.9 0.0 copy-done.4
  222.9 0.2 conditional.1
  223.2 1.9 copy.30
  (12 shorter events, 0.0 us)
Async XLA Ops:
  0.6 213.1 %copy-start.10 = (s32[1,4]{1,0:T(1,128)S(1)}, s32[1,4]{1,0:T(1,128)}, u32[]{:S(2)}) copy-start(s32[1,4]{1,0:T(1,128)} %len_ref.1) | copy-start | bytes 52
  0.6 213.1 %copy-start.8 = (f32[1536]{0:T(1024)S(1)}, f32[1536]{0:T(1024)}, u32[]{:S(2)}) copy-start(f32[1536]{0:T(1024)} %param.18) | copy-start | bytes 18436
  0.7 213.1 %copy-start.7 = (f32[31,1536]{1,0:T(8,128)S(1)}, f32[31,1536]{1,0:T(8,128)}, u32[]{:S(2)}) copy-start(f32[31,1536]{1,0:T(8,128)} %taps_ref.1) | copy-start | bytes 571396
  0.7 213.1 %copy-start.9 = (f32[1536]{0:T(1024)S(1)}, f32[1536]{0:T(1024)}, u32[]{:S(2)}) copy-start(f32[1536]{0:T(1024)} %param.19) | copy-start | bytes 18436
  44.3 1.0 copy-start
  45.3 0.7 copy-start.2
  46.0 176.9 %copy-start.3 = (bf16[1,256,1536]{2,1,0:T(8,128)(2,1)S(1)}, bf16[1,256,1536]{2,1,0:T(8,128)(2,1)}, u32[]{:S(2)}) copy-start(bf16[1,256,1536]{2,1,0:T(8,128)(2,1)} %param.14) | copy-start | bytes 2359300
  46.0 176.9 %copy-start.4 = (bf16[1,256,1024]{2,1,0:T(8,128)(2,1)S(1)}, bf16[1,256,1024]{2,1,0:T(8,128)(2,1)}, u32[]{:S(2)}) copy-start(bf16[1,256,1024]{2,1,0:T(8,128)(2,1)} %param.12) | copy-start | bytes 1572868
  46.0 176.9 %copy-start.5 = (bf16[1,256,1024]{2,1,0:T(8,128)(2,1)S(1)}, bf16[1,256,1024]{2,1,0:T(8,128)(2,1)}, u32[]{:S(2)}) copy-start(bf16[1,256,1024]{2,1,0:T(8,128)(2,1)} %param.13) | copy-start | bytes 1572868
  46.0 176.9 %copy-start.6 = (bf16[1,256,1024]{2,1,0:T(8,128)(2,1)S(1)}, bf16[1,256,1024]{2,1,0:T(8,128)(2,1)}, u32[]{:S(2)}) copy-start(bf16[1,256,1024]{2,1,0:T(8,128)(2,1)} %param.11) | copy-start | bytes 1572868
  46.0 176.9 %copy-start.11 = (s32[1,128]{1,0:T(1,128)S(1)}, s32[1,128]{1,0:T(1,128)}, u32[]{:S(2)}) copy-start(s32[1,128]{1,0:T(1,128)} %param.15) | copy-start | bytes 1540

commit v6 on v5

--- a/solution.py
+++ b/solution.py
@@ -239,31 +239,31 @@
     return jnp.where((fields & bit) != 0, 1, 0) + jnp.where((fields & (bit << 1)) != 0, 2, 0)
 
 
-def relay_fields(y):
-    fields = 0
-    for m in range(N_Z):
-        shift = (y - m) % N_Z
-        order = 2 * (shift - 1) if shift <= N_Z // 2 else 2 * (N_Z - shift) - 1
-        if shift and order < RELAYS:
-            fields |= RELAY_SLOTS << (2 * m)
-    return fields - (1 << 32) if fields >= 1 << 31 else fields
-
-
-LOW, HIGH, OVER = N_Z, N_Z + 1, N_Z + 2
+STEPS = 12
+MOST_LANE, OVER_LANE = N_Z, N_Z + 1
+A_ROW, B_ROW, MISSED_ROW = 0, 1, 2
 
 
 def route_kernel(
     lists_ref,
     table,
     count_v,
+    extra_v,
     excess_v,
     tile_v,
     slot_v,
+    code_v,
+    state_v,
+    relay_v,
     count,
     excess,
     tile,
     slot,
+    code,
+    state,
+    relay,
     direct,
+    free_s,
     relay_free,
     sems,
 ):
@@ -279,29 +279,23 @@
         return jnp.sum(values, axis=0, keepdims=True, dtype=jnp.int32)
 
     for i in range(N_Z):
-        count_v[pl.ds(i, 1), :] = total(jnp.where(source == i, 1, 0))
+        count_v[pl.ds(i, 1), :] = total(jnp.where(source == ((lanes - i) & 15), 1, 0))
     held = count_v[...]
-    z = lax.broadcasted_iota(jnp.int32, held.shape, 0)
-    y = lax.broadcasted_iota(jnp.int32, held.shape, 1)
-    shift = (y - z) & 15
+    shift = lax.broadcasted_iota(jnp.int32, held.shape, 0)
+    lane = lax.broadcasted_iota(jnp.int32, held.shape, 1)
     stays = shift == 0
     most = jnp.where(stays, RANKS, main_slots(shift))
-    real = y < N_Z
-    left = jnp.where(stays, 3, jnp.clip(most - held, 0, 3)) << (2 * (y & 7))
-    low = jnp.sum(jnp.where(y < 8, left, 0), axis=1, keepdims=True)
-    high = jnp.sum(jnp.where((y >= 8) & real, left, 0), axis=1, keepdims=True)
-    over = jnp.max(jnp.where(real & (held > RANKS), 1, 0), axis=1, keepdims=True)
-    extra = jnp.where(real, jnp.maximum(jnp.minimum(held, RANKS) - most, 0), 0)
-    extra = jnp.where(y == LOW, low, jnp.where(y == HIGH, high, jnp.where(y == OVER, over, extra)))
-    excess_v[...] = extra
-    copies = [
-        pltpu.make_async_copy(a, b, sems.at[i])
-        for i, (a, b) in enumerate(
-            ((count_v, count), (excess_v, excess), (tile_v, tile), (slot_v, slot))
-        )
-    ]
-    copies[0].start()
-    copies[1].start()
+    left = jnp.where(stays, 3, jnp.clip(most - held, 0, 3)) << (2 * (lane & 15))
+    extra = jnp.maximum(jnp.minimum(held, RANKS) - most, 0)
+    extra_v[...] = extra
+    largest = jnp.minimum(jnp.max(extra, axis=1, keepdims=True), STEPS)
+    over = jnp.max(jnp.where((held > RANKS) | (extra > STEPS), 1, 0), axis=1, keepdims=True)
+    kept = jnp.minimum(extra, STEPS)
+    excess_v[...] = jnp.where(lane == MOST_LANE, largest, jnp.where(lane == OVER_LANE, over, kept))
+    ahead = pltpu.make_async_copy(excess_v, excess, sems.at[0])
+    ahead.start()
+    count_copy = pltpu.make_async_copy(count_v, count, sems.at[1])
+    count_copy.start()
 
     def add_rank(i, rank):
         other = lists_ref[pl.ds(i, 1), :] >> 3
@@ -316,34 +310,154 @@
     for i in range(RANKS):
         tile_v[pl.ds(i, 1), :] = total(jnp.where(mine == i, local, 0))
         slot_v[pl.ds(i, 1), :] = total(jnp.where(taken == i, position, 0))
-    copies[2].start()
-    copies[3].start()
+    copies = [
+        pltpu.make_async_copy(tile_v, tile, sems.at[2]),
+        pltpu.make_async_copy(slot_v, slot, sems.at[3]),
+    ]
+    for copy in copies:
+        copy.start()
+
+    y = lax.broadcasted_iota(jnp.int32, (1, LANES), 1) & 15
+    free = jnp.zeros((1, LANES), jnp.int32)
+    relays = jnp.zeros((1, LANES), jnp.int32)
+    for i in range(N_Z):
+        row = left[i : i + 1, :]
+        free = free | (pltpu.roll(row, LANES - i, 1) if i else row)
+        away = (y - i) & 15
+        opened = (away != 0) & (order_of(away) < RELAYS)
+        relays = relays | (jnp.where(opened, RELAY_SLOTS, 0) << (2 * i))
+    code_v[...] = jnp.zeros(code_v.shape, jnp.int32)
+    ahead.wait()
+
+    def displacement(i, carry):
+        free, relays, missed = carry
+        free = pltpu.roll(free, 1, 1)
+        z = (y - i) & 15
+        own = 1 << (2 * z)
+        from_z = jnp.int32(-1) << (2 * z)
+        wanted = extra_v[pl.ds(i, 1), :]
+
+        def one(e, carry):
+            free, relays, missed = carry
+            active = wanted > e
+            open_ = filled(free) & filled(relays)
+            late = open_ & from_z
+            chosen = jnp.where(late != 0, late, open_)
+            bit = jnp.where(active, chosen & -chosen, 0)
+            entry_ = (
+                (1 << 12)
+                | field_index(bit)
+                | (field_value(free, bit) << 4)
+                | (field_value(relays, bit) << 8)
+            )
+            code_v[pl.ds(i * STEPS + e, 1), :] = jnp.where(bit != 0, entry_, 0)
+            missed = missed | jnp.where(active & (open_ == 0), 1 << i, 0)
+            return free - jnp.where(bit == own, 0, bit), relays - bit, missed
+
+        return lax.fori_loop(0, excess[i, MOST_LANE], one, (free, relays, missed))
+
+    free, relays, missed = lax.fori_loop(
+        1, N_Z, displacement, (free, relays, jnp.zeros((1, LANES), jnp.int32))
+    )
+    state_v[pl.ds(A_ROW, 1), :] = pltpu.roll(free, 1, 1)
+    state_v[pl.ds(B_ROW, 1), :] = relays
+    state_v[pl.ds(MISSED_ROW, 1), :] = missed
+    last_copies = [
+        pltpu.make_async_copy(code_v, code, sems.at[4]),
+        pltpu.make_async_copy(state_v, state, sems.at[5]),
+    ]
+    for copy in last_copies:
+        copy.start()
+    codes = code_v[...]
+    places = lax.broadcasted_iota(jnp.int32, codes.shape, 0)
+    from_shift = (places * 171) >> 11
+    places = (from_shift << 4) | (places - STEPS * from_shift)
+    through_me = jnp.where((codes != 0) & ((codes & 15) == me), codes >> 8 & 3, 0)
+    for i in range(RELAY_SLOTS):
+        relay_v[pl.ds(i, 1), :] = total(
+            jnp.where(through_me == i + 1, (1 << 12) | (places << 4) | ((codes >> 4) & 3), 0)
+        )
+    relay_copy = pltpu.make_async_copy(relay_v, relay, sems.at[6])
+    relay_copy.start()
     for i in range(AT_BAD):
         table[i] = 0
+    count_copy.wait()
+    for copy in copies + last_copies:
+        copy.wait()
+    relay_copy.wait()
+
+    def slots_of(shift):
+        return jnp.where(shift == 0, RANKS, main_slots(shift))
+
+    def open_row(shift):
+        for y in range(N_Z):
+            direct[shift * N_Z + y] = jnp.minimum(count[shift, y], slots_of(shift))
+
+    repeat(0, N_Z, open_row)
+
+    def open_plane(i):
+        free_s[i] = state[A_ROW, i]
+        relay_free[i] = state[B_ROW, i]
+
     for i in range(N_Z):
-        relay_free[i] = jnp.int32(relay_fields(i))
-    for copy in copies:
-        copy.wait()
-
-    def open_row(z):
-        def open_pair(y):
-            shift = (y - z) & 15
-            most = jnp.where(shift == 0, RANKS, main_slots(shift))
-            direct[z * N_Z + y] = jnp.minimum(count[z, y], most)
-
-        for y in range(N_Z):
-            open_pair(y)
-
-    repeat(0, N_Z, open_row)
+        open_plane(i)
+
+    def own_main(z, m, field):
+        return main_offset((m - z) & 15) + count[(m - z) & 15, m] + field - 1
+
+    def leave(shift):
+        y = (me + shift) & 15
+
+        def one(e):
+            entry_ = code[shift * STEPS + e, y]
+            m = entry_ & 15
+
+            @pl.when((entry_ != 0) & (m != me))
+            def _():
+                table[AT_MAIN + own_main(me, m, (entry_ >> 4) & 3)] = tile[main_slots(shift) + e, y]
+
+        repeat(0, excess[shift, y], one)
+
+    def reach(shift):
+        z = (me - shift) & 15
+
+        def one(e):
+            entry_ = code[shift * STEPS + e, me]
+
+            @pl.when(entry_ != 0)
+            def _():
+                extra_at = relay_offset((me - (entry_ & 15)) & 15) + ((entry_ >> 8) & 3) - 1
+                table[AT_FINAL + slot[main_slots(shift) + e, z]] = HELD + MAIN + extra_at
+
+        repeat(0, excess[shift, me], one)
+
+    repeat(1, N_Z, leave)
+    repeat(1, N_Z, reach)
+
+    def pass_on(y):
+        for i in range(RELAY_SLOTS):
+            entry_ = relay[i, y]
+
+            @pl.when(entry_ != 0)
+            def _():
+                shift = (entry_ >> 8) & 15
+                z = (y - shift) & 15
+                rank = main_slots(shift) + ((entry_ >> 4) & 15)
+                table[AT_EXTRA + relay_offset((y - me) & 15) + i] = jnp.where(
+                    z == me, tile[rank, y], HELD + own_main(z, me, entry_ & 3)
+                )
+
+    repeat(0, N_Z, pass_on)
     my_bit = jnp.int32(1) << (2 * me)
 
-    def record(z, y, bit, rank, free, relay, main):
+    def record(z, y, bit, rank, free, relay_, main):
         @pl.when((z == me) | (bit == my_bit) | (y == me))
         def _():
             m = field_index(bit)
-            own = jnp.where(main >= 0, main, count[z, m] + field_value(free, bit) - 1)
-            main_at = main_offset((m - z) & 15) + own
-            extra_at = relay_offset((y - m) & 15) + field_value(relay, bit) - 1
+            main_at = jnp.where(
+                main >= 0, main_offset((m - z) & 15) + main, own_main(z, m, field_value(free, bit))
+            )
+            extra_at = relay_offset((y - m) & 15) + field_value(relay_, bit) - 1
 
             @pl.when((z == me) & (m != z))
             def _():
@@ -357,68 +471,73 @@
             def _():
                 table[AT_FINAL + slot[rank, z]] = HELD + MAIN + extra_at
 
-    def place_row(z, bad):
+    def mend(shift, e, y):
+        z = (y - shift) & 15
         own = jnp.int32(1) << (2 * z)
-
-        def take(free, bit):
-            return free - jnp.where(bit == own, 0, bit)
-
-        def place_pair(i, carry):
-            y = (i + z) & 15
-            most = main_slots(i)
-
-            def place_one(e, carry):
-                free, bad = carry
-                relay = relay_free[y]
-                open_ = filled(free) & filled(relay)
-
-                def simple():
-                    late = open_ & (jnp.int32(-1) << (2 * ((y + 8) & 15)))
-                    chosen = jnp.where(late != 0, late, open_)
-                    bit = chosen & -chosen
-                    record(z, y, bit, most + e, free, relay, jnp.int32(-1))
-                    relay_free[y] = relay - bit
-                    return take(free, bit), bad
-
-                def swap():
-                    def look(m, carry):
-                        free, done = carry
-                        bit = jnp.int32(1) << (2 * m)
-                        relay_m = relay_free[m]
-                        other = filled(free) & filled(relay_m)
-                        straight = direct[z * N_Z + m]
-                        fits = (
-                            (done == 0)
-                            & (m != z)
-                            & (m != y)
-                            & ((filled(relay) & bit) != 0)
-                            & (straight > 0)
-                            & (other != 0)
-                        )
-
-                        def do():
-                            instead = other & -other
-                            direct[z * N_Z + m] = straight - 1
-                            record(z, m, instead, straight - 1, free, relay_m, jnp.int32(-1))
-                            record(z, y, bit, most + e, free, relay, straight - 1)
-                            relay_free[m] = relay_m - instead
-                            relay_free[y] = relay - bit
-                            return take(free, instead), jnp.int32(1)
-
-                        return lax.cond(fits, do, lambda: (free, done))
-
-                    free_, done = lax.fori_loop(0, N_Z, look, (free, jnp.int32(0)))
-                    return free_, bad | (1 - done)
-
-                return lax.cond(open_ != 0, simple, swap)
-
-            return lax.fori_loop(0, excess[z, y], place_one, carry)
-
-        free = excess[z, LOW] | (excess[z, HIGH] << 16)
-        free, bad = lax.fori_loop(1, N_Z, place_pair, (free, bad | excess[z, OVER]))
-        return bad
-
-    table[AT_BAD] = lax.fori_loop(0, N_Z, place_row, jnp.int32(0))
+        rank = main_slots(shift) + e
+        mine_free, mine_relay = free_s[z], relay_free[y]
+        open_ = filled(mine_free) & filled(mine_relay)
+
+        def take(bit):
+            free_s[z] = free_s[z] - jnp.where(bit == own, 0, bit)
+
+        def simple():
+            bit = open_ & -open_
+            record(z, y, bit, rank, mine_free, mine_relay, jnp.int32(-1))
+            take(bit)
+            relay_free[y] = mine_relay - bit
+            return jnp.int32(0)
+
+        def swap():
+            def look(m, done):
+                bit = jnp.int32(1) << (2 * m)
+                relay_m = relay_free[m]
+                other = filled(mine_free) & filled(relay_m)
+                at = ((m - z) & 15) * N_Z + m
+                straight = direct[at]
+                fits = (
+                    (done == 0)
+                    & (m != z)
+                    & (m != y)
+                    & ((filled(mine_relay) & bit) != 0)
+                    & (straight > 0)
+                    & (other != 0)
+                )
+
+                def do():
+                    instead = other & -other
+                    direct[at] = straight - 1
+                    record(z, m, instead, straight - 1, mine_free, relay_m, jnp.int32(-1))
+                    record(z, y, bit, rank, mine_free, mine_relay, straight - 1)
+                    relay_free[m] = relay_m - instead
+                    relay_free[y] = mine_relay - bit
+                    take(instead)
+                    return jnp.int32(1)
+
+                return lax.cond(fits, do, lambda: done)
+
+            return 1 - lax.fori_loop(0, N_Z, look, jnp.int32(0))
+
+        return lax.cond(open_ != 0, simple, swap)
+
+    def mend_target(y, bad):
+        gaps = state[MISSED_ROW, y]
+
+        def mend_pair(shift, bad):
+            def mend_one(e, bad):
+                return lax.cond(
+                    code[shift * STEPS + e, y] == 0, lambda: bad | mend(shift, e, y), lambda: bad
+                )
+
+            count_ = jnp.where(((gaps >> shift) & 1) != 0, excess[shift, y], 0)
+            return lax.fori_loop(0, count_, mend_one, bad)
+
+        return lax.fori_loop(1, jnp.where(gaps != 0, N_Z, 1), mend_pair, bad)
+
+    bad = lax.fori_loop(0, N_Z, mend_target, jnp.int32(0))
+    for i in range(N_Z):
+        bad = bad | excess[i, OVER_LANE]
+    table[AT_BAD] = bad
 
     def straight(other):
         shift_out = (other - me) & 15
@@ -435,31 +554,35 @@
             def arrive(r):
                 table[AT_FINAL + slot[r, other]] = first_in + r
 
-            repeat(0, direct[me * N_Z + other], out)
-            repeat(0, direct[other * N_Z + me], arrive)
+            repeat(0, direct[shift_out * N_Z + other], out)
+            repeat(0, direct[shift_in * N_Z + me], arrive)
 
         @pl.when(shift_out == 0)
         def _():
             def keep(r):
                 table[AT_FINAL + slot[r, me]] = tile[r, me]
 
-            repeat(0, direct[me * N_Z + me], keep)
+            repeat(0, direct[me], keep)
 
     repeat(0, N_Z, straight)
 
 
 def route(lists):
-    smem = pltpu.SMEM
-    square = smem((N_Z, LANES), jnp.int32)
-    square_v = pltpu.VMEM((N_Z, LANES), jnp.int32)
+    vmem, smem = pltpu.VMEM, pltpu.SMEM
+    square = (N_Z, LANES)
+    steps = (N_Z * STEPS, LANES)
+    small = (8, LANES)
+    kind = jnp.int32
     return pl.pallas_call(
         route_kernel,
-        out_shape=jax.ShapeDtypeStruct((TABLE,), jnp.int32),
-        in_specs=[pl.BlockSpec(memory_space=pltpu.VMEM)],
+        out_shape=jax.ShapeDtypeStruct((TABLE,), kind),
+        in_specs=[pl.BlockSpec(memory_space=vmem)],
         out_specs=pl.BlockSpec(memory_space=smem),
-        scratch_shapes=[square_v] * 4
-        + [square] * 4
-        + [smem((PAIRS,), jnp.int32), smem((N_Z,), jnp.int32), pltpu.SemaphoreType.DMA((4,))],
+        scratch_shapes=[vmem(square, kind)] * 5
+        + [vmem(steps, kind), vmem(small, kind), vmem(small, kind)]
+        + [smem(square, kind)] * 4
+        + [smem(steps, kind), smem(small, kind), smem(small, kind)]
+        + [smem((PAIRS,), kind), smem((N_Z,), kind), smem((N_Z,), kind), pltpu.SemaphoreType.DMA((7,))],
         name="route",
     )(lists)
 
@@ -1210,7 +1333,7 @@
 def on_device(*inputs):
     query, key, value, conv, slot_tile, lengths, conv_taps, norm_scale, norm_shift = inputs
     places = jnp.transpose(slot_tile[0].reshape(N_Z, 8))
-    places = jnp.pad(places, ((0, 0), (0, LANES - N_Z)), constant_values=1 << 16)
+    places = jnp.tile(places, (1, LANES // N_Z))
     shape = (TILES_DEV, PLANE_DP, SEG_UNIT, HEADS * HEAD_DIM)
     held_q, lists = first(query.reshape(shape), places)
     table = route(lists.reshape(HELD, LANES))

time: 225 us -> 217 us (0.964)
  Pallas kernels: 216 us -> 207 us
    pallas_call x1, Pallas kernels: 19.4 us -> 9.94 us  [route(): pl.pallas_call(route_kernel, out_shape=jax.ShapeDtypeStruct((TABLE,), kin...]
where the time goes in v6:
time: 217 us; the launch traced here: 216 us
  Pallas kernels  207 us (95%)
  local copies, waits for them, and re-layouts  6.25 us (3%)
    pallas_call x1, Pallas kernels, exchange(): pl.pallas_call(exchange_kernel, out_shape=(jax.ShapeDtypeStruct((COLUMN,...  168 us
    pallas_call x1, Pallas kernels, first(): pl.pallas_call(first_kernel, out_shape=(jax.ShapeDtypeStruct((HELD, SEG_U...  19.7 us
    pallas_call x1, Pallas kernels, route(): pl.pallas_call(route_kernel, out_shape=jax.ShapeDtypeStruct((TABLE,), kin...  9.94 us
    pallas_call x1, Pallas kernels, convolve_column(): pl.pallas_call(convolve_kernel, out_shape=jax.ShapeDtypeStruct((COLUMN, C...  9.11 us

profile of v6, /device:TPU:1, one launch (start us, length us, event | category | flops | bytes accessed | tf_op | source)
XLA Modules:
  0.0 215.8 jit_solution(5815588561514057462)
XLA Ops:
  0.6 0.0 copy-start.10
  0.6 0.0 copy-start.8
  0.7 0.0 copy-start.7
  0.7 0.0 copy-start.9
  0.7 0.5 broadcast.174
  1.2 1.3 reduce.65
  2.5 0.1 reshape_squeeze.3
  2.6 0.1 copy.22
  2.7 0.7 tile.10.list_ref
  3.3 19.7 %spread_queries.1 = (bf16[64,32,128]{2,1,0:T(8,128)(2,1)}, s32[8,8,128]{2,1,0:T(8,128)}) custom-call(bf16[2,4,32,1024]{3,2,1,0:T(8,128)(2,1)} %bitcast.52, s32[8,128]{1,0:T(8,128)} %tile.10.list_ref), custom_call_target="tpu_custom_call" | custom-call | tf_op jit(solution)/shard_map/spread_queries/pallas_call | solution.py:212
  23.1 9.9 %route.1.table = s32[256]{0:T(256)} custom-call(s32[64,128]{1,0:T(8,128)} %bitcast.55), custom_call_target="tpu_custom_call" | custom-call | tf_op jit(solution)/shard_map/route/pallas_call | solution.py:576
  33.0 1.3 slice.309
  34.9 0.0 copy-start
  34.9 1.0 copy-done
  36.0 0.7 copy-done.2
  36.7 0.0 copy-start.11
  36.7 167.7 %exchange.1 = (bf16[256,1024]{1,0:T(8,128)(2,1)}, bf16[2,8,16,1536]{3,2,1,0:T(8,128)(2,1)S(1)}, bf16[2,16,1536]{2,1,0:T(8,128)(2,1)S(1)}) custom-call(s32[256]{0:T(256)S(1)} %copy-done.2, s32[1,4]{1,0:T(1,128)} %len_ref.1, bf16[64,32,128]{2,1,0:T(8,128)(2,1)S(1)} %copy-done, bf16[2,4,32,1024]{3,2,1,0:T(8,128)(2,1)} %bitcast.50, ...), custom_call_target="tpu_custom_call" | custom-call | tf_op jit(solution)/shard_map/exchange/pallas_call | solution.py:844
  204.4 0.0 copy-done.8
  204.4 0.0 copy-done.9
  204.5 0.0 copy-done.10
  204.5 0.0 copy-done.7
  204.5 9.1 %convolve.1 = bf16[256,1536]{1,0:T(8,128)(2,1)} custom-call(s32[1,4]{1,0:T(1,128)S(1)} %copy-done.10, bf16[256,1536]{1,0:T(8,128)(2,1)S(1)} %bitcast.36, bf16[2,16,1536]{2,1,0:T(8,128)(2,1)S(1)} %get-tuple-element.46.halo_ref, f32[31,1536]{1,0:T(8,128)S(1)} %copy-done.7, f32[1,1536]{1,0:T(1,128)S(1)} %reshape.192.scale_ref, f32[1,1536]{1,0:T(1,128)S(1)} %reshape.193.shift_ref), custom_call_target="tpu_custom_call" | custom-call | tf_op jit(solution)/shard_map/convolve/pallas_call | solution.py:938
  213.6 0.2 conditional.1
  213.9 1.9 copy.30
  (13 shorter events, 0.0 us)
Async XLA Ops:
  0.6 203.8 %copy-start.10 = (s32[1,4]{1,0:T(1,128)S(1)}, s32[1,4]{1,0:T(1,128)}, u32[]{:S(2)}) copy-start(s32[1,4]{1,0:T(1,128)} %len_ref.1) | copy-start | bytes 52
  0.6 203.8 %copy-start.8 = (f32[1536]{0:T(1024)S(1)}, f32[1536]{0:T(1024)}, u32[]{:S(2)}) copy-start(f32[1536]{0:T(1024)} %param.18) | copy-start | bytes 18436
  0.7 203.8 %copy-start.7 = (f32[31,1536]{1,0:T(8,128)S(1)}, f32[31,1536]{1,0:T(8,128)}, u32[]{:S(2)}) copy-start(f32[31,1536]{1,0:T(8,128)} %taps_ref.1) | copy-start | bytes 571396
  0.7 203.8 %copy-start.9 = (f32[1536]{0:T(1024)S(1)}, f32[1536]{0:T(1024)}, u32[]{:S(2)}) copy-start(f32[1536]{0:T(1024)} %param.19) | copy-start | bytes 18436
  34.9 1.0 copy-start
  36.0 0.7 copy-start.2
  36.7 177.0 %copy-start.3 = (bf16[1,256,1536]{2,1,0:T(8,128)(2,1)S(1)}, bf16[1,256,1536]{2,1,0:T(8,128)(2,1)}, u32[]{:S(2)}) copy-start(bf16[1,256,1536]{2,1,0:T(8,128)(2,1)} %param.14) | copy-start | bytes 2359300
  36.7 177.0 %copy-start.4 = (bf16[1,256,1024]{2,1,0:T(8,128)(2,1)S(1)}, bf16[1,256,1024]{2,1,0:T(8,128)(2,1)}, u32[]{:S(2)}) copy-start(bf16[1,256,1024]{2,1,0:T(8,128)(2,1)} %param.12) | copy-start | bytes 1572868
  36.7 177.0 %copy-start.5 = (bf16[1,256,1024]{2,1,0:T(8,128)(2,1)S(1)}, bf16[1,256,1024]{2,1,0:T(8,128)(2,1)}, u32[]{:S(2)}) copy-start(bf16[1,256,1024]{2,1,0:T(8,128)(2,1)} %param.13) | copy-start | bytes 1572868
  36.7 177.0 %copy-start.6 = (bf16[1,256,1024]{2,1,0:T(8,128)(2,1)S(1)}, bf16[1,256,1024]{2,1,0:T(8,128)(2,1)}, u32[]{:S(2)}) copy-start(bf16[1,256,1024]{2,1,0:T(8,128)(2,1)} %param.11) | copy-start | bytes 1572868
  36.7 177.0 %copy-start.11 = (s32[1,128]{1,0:T(1,128)S(1)}, s32[1,128]{1,0:T(1,128)}, u32[]{:S(2)}) copy-start(s32[1,128]{1,0:T(1,128)} %param.15) | copy-start | bytes 1540
